TPU v7x, 32 devices: a whole 2x2x4 slice. The times are simulated.
32 devices in a mesh: clip: 2 (over x), blk: 16 (over z, y, core).
Axes of the slice: x: 2, y: 2, z: 4, core: 2. Of those that a mesh axis runs over, the one named last changes fastest.
Arguments:
- queries: bfloat16 [8192, 2560], P(('clip', 'blk')), parts along dimension 0, may hold values from -24 to 24
- keys: bfloat16 [8192, 2560], P(('clip', 'blk')), parts along dimension 0, may hold values from -24 to 24
- values: bfloat16 [8192, 2560], P(('clip', 'blk')), parts along dimension 0, may hold values from -6 to 6
- kept_blocks: int32 [64, 8], P(('clip', 'blk')), parts along dimension 0, may hold values from 0 to 31, as said below
Outputs:
- attended: bfloat16 [8192, 2560], P(('clip', 'blk')), parts along dimension 0
There are 2 independent parts, one for each index of `clip`. A program takes and returns all parts, laid end to end along the dimension named above; each array names one. Nothing has to cross between parts.
Inputs may be any that keep to these rules, and one draw needn't show every extreme that they name: `kept_blocks`: row b lists 8 distinct key blocks in increasing order; b itself is one of them, and for every listed block j the difference j // 2 - b // 2 is 0 or plus or minus a power of two of at most 8.
All inputs are finite; a program needn't handle non-finite values.
Results may differ from a plain program's by a relative error of at most 0.0065.
Values may be sent and summed in bfloat16 or wider, within the bound.
No kernel may reach another device: no remote copies, remote signals or barrier semaphores. Data moves between devices by JAX's collectives and lax.ppermute only.
A program may use at most 128 MiB of HBM per device.

v0:
```python
import math

import jax
import jax.numpy as jnp
from jax import lax
from jax.sharding import PartitionSpec as P

DH = 128
BLOCK = 128
REACH = 8


very_negative = -1e30


def passed_along(value, axis, steps):
    count = lax.axis_size(axis)
    leading, last = (max(0, -steps), min(count, count - steps))
    return lax.ppermute(value, axis, [(source, source + steps) for source in range(leading, last)])


def padded(block, sides, width):
    for axis, dim in sides:
        count = lax.axis_size(axis)
        forward = [(i, i + 1) for i in range(count - 1)]
        backward = [(target, source) for source, target in forward]
        low = lax.ppermute(
            lax.slice_in_dim(block, block.shape[dim] - width, None, axis=dim), axis, forward
        )
        high = lax.ppermute(lax.slice_in_dim(block, 0, width, axis=dim), axis, backward)
        block = jnp.concatenate([low, block, high], axis=dim)
    return block


def tile_mask(kept_blocks, source_device, local_blocks):
    first_block = source_device * local_blocks
    block_ids = first_block + jnp.arange(local_blocks, dtype=jnp.int32)
    return jnp.any(kept_blocks[:, :, None] == block_ids[None, None, :], axis=1)


def absorb_block(running, query_rows, key_rows, value_rows, allowed_rows):
    running_top, denominator, numerator = running
    scores = jnp.einsum("qhd,khd->hqk", query_rows, key_rows, preferred_element_type=jnp.float32)
    scores = scores * (1.0 / math.sqrt(query_rows.shape[-1]))
    masked = jnp.where(allowed_rows[None], scores, very_negative)
    new_top = jnp.maximum(running_top, jnp.max(masked, axis=-1))
    weight = jnp.where(allowed_rows[None], jnp.exp(scores - new_top[..., None]), 0.0)
    rescale = jnp.exp(running_top - new_top)
    denominator = denominator * rescale + jnp.sum(weight, axis=-1)
    rounded = weight.astype(jnp.bfloat16)
    numerator = numerator * jnp.transpose(rescale)[:, :, None] + jnp.einsum(
        "hqk,khd->qhd", rounded, value_rows, preferred_element_type=jnp.float32
    )
    return (new_top, denominator, numerator)


def absorb_tile(states, key_tile, source_device, kept_blocks, query_blocks):
    local_blocks, block_len, heads, head_dim = query_blocks.shape
    key_rows = key_tile[0].reshape(local_blocks * block_len, heads, head_dim)
    value_rows = key_tile[1].reshape(local_blocks * block_len, heads, head_dim)
    allowed = tile_mask(kept_blocks, source_device, local_blocks)
    updated = []
    for query_slot in range(local_blocks):
        running = states[query_slot]
        token_allowed = jnp.repeat(allowed[query_slot], block_len)[None, :]
        running = absorb_block(
            running, query_blocks[query_slot], key_rows, value_rows, token_allowed
        )
        updated.append(running)
    return updated


def fetch_distant(stacked, offset_by):
    return passed_along(stacked, "blk", offset_by)


def per_device(queries, keys, values, kept_blocks):
    cycle_size = lax.axis_size("blk")
    position = lax.axis_index("blk")
    local_rows = queries.shape[0]
    local_blocks = local_rows // BLOCK
    heads = queries.shape[1] // DH
    query_blocks = queries.reshape(local_blocks, BLOCK, heads, DH)
    states = []
    for query_slot in range(local_blocks):
        states.append(
            (
                jnp.full((heads, BLOCK), very_negative, jnp.float32),
                jnp.zeros((heads, BLOCK), jnp.float32),
                jnp.zeros((BLOCK, heads, DH), jnp.float32),
            )
        )
    stacked = jnp.stack((keys, values))
    states = absorb_tile(states, stacked, position, kept_blocks, query_blocks)
    neighbours = padded(stacked, (("blk", 1),), local_rows)
    states = absorb_tile(
        states, neighbours[:, :local_rows], position - 1, kept_blocks, query_blocks
    )
    states = absorb_tile(
        states, neighbours[:, 2 * local_rows :], position + 1, kept_blocks, query_blocks
    )
    farthest = min(REACH, cycle_size - 1)
    distance = 2
    while distance <= farthest:
        for direction in (1, -1):
            key_tile = fetch_distant(stacked, -direction * distance)
            states = absorb_tile(
                states, key_tile, position + direction * distance, kept_blocks, query_blocks
            )
        distance = distance * 2
    outputs = []
    for query_slot in range(local_blocks):
        running_top, denominator, numerator = states[query_slot]
        outputs.append(numerator / jnp.transpose(denominator)[:, :, None])
    attended = jnp.concatenate(outputs, axis=0).reshape(local_rows, heads * DH)
    return attended.astype(jnp.bfloat16)


def solution(mesh):
    placed = (
        P(("clip", "blk"), None),
        P(("clip", "blk"), None),
        P(("clip", "blk"), None),
        P(("clip", "blk"), None),
    )
    return jax.shard_map(
        per_device, mesh=mesh, in_specs=placed, out_specs=P(("clip", "blk"), None), check_vma=False
    )
```

profile of v0, /device:TPU:19, one launch (start us, length us, event | category | flops | bytes accessed | tf_op | source)
XLA Modules:
  0.0 357.2 jit_solution(14420054263135990229)
XLA Ops:
  0.0 1.6 copy.107
  1.6 2.1 copy.104
  3.7 1.7 pad_maximum_fusion
  5.4 3.0 collective-permute-start.2
  8.5 3.1 collective-permute-start
  11.6 1.3 collective-permute-start.7
  12.9 7.9 %collective-permute-start.6 = (bf16[2,256,2560]{1,2,0:T(8,128)(2,1)}, bf16[2,256,2560]{1,2,0:T(8,128)(2,1)}, u32[]{:S(2)}, u32[]{:S(2)}) collective-permute-start(bf16[2,256,2560]{1,2,0:T(8,128)(2,1)} %pad_maximum_fusion), channel_id=1, source_target_pairs={{8,0},{9,1},{10,2},{11,3},{12,4},{13,5},{14,6},{15,7},{24,16},{25,... | collective-permute-start | bytes 7864328 | tf_op jit(solution)/shard_map/ppermute | solution.py:19
  20.8 4.6 %collective-permute-start.5 = (bf16[2,256,2560]{1,2,0:T(8,128)(2,1)}, bf16[2,256,2560]{1,2,0:T(8,128)(2,1)}, u32[]{:S(2)}, u32[]{:S(2)}) collective-permute-start(bf16[2,256,2560]{1,2,0:T(8,128)(2,1)} %pad_maximum_fusion), channel_id=1, source_target_pairs={{0,4},{1,5},{2,6},{3,7},{4,8},{5,9},{6,10},{7,11},{8,12},{9,13},{1... | collective-permute-start | bytes 7864328 | tf_op jit(solution)/shard_map/ppermute | solution.py:19
  26.9 2.2 fusion.192
  29.2 1.4 copy.251
  31.3 2.2 select_reduce_fusion.17
  33.5 2.1 select_reduce_fusion.8
  35.6 47.9 %collective-permute-done.2 = bf16[2,256,2560]{1,2,0:T(8,128)(2,1)} collective-permute-done((bf16[2,256,2560]{1,2,0:T(8,128)(2,1)}, bf16[2,256,2560]{1,2,0:T(8,128)(2,1)}, u32[]{:S(2)}, u32[]{:S(2)}) %collective-permute-start.2) | collective-permute-done | bytes 2621472 | tf_op jit(solution)/shard_map/ppermute | solution.py:19
  83.4 1.9 collective-permute-start.3
  85.3 1.9 fusion.189
  87.2 13.5 %collective-permute-done = bf16[2,256,2560]{1,2,0:T(8,128)(2,1)} collective-permute-done((bf16[2,256,2560]{1,2,0:T(8,128)(2,1)}, bf16[2,256,2560]{1,2,0:T(8,128)(2,1)}, u32[]{:S(2)}, u32[]{:S(2)}) %collective-permute-start) | collective-permute-done | bytes 2621472 | tf_op jit(solution)/shard_map/ppermute | solution.py:27
  100.7 25.0 %collective-permute-start.1 = (bf16[2,256,2560]{1,2,0:T(8,128)(2,1)}, bf16[2,256,2560]{1,2,0:T(8,128)(2,1)S(1)}, u32[]{:S(2)}, u32[]{:S(2)}) collective-permute-start(bf16[2,256,2560]{1,2,0:T(8,128)(2,1)} %pad_maximum_fusion), channel_id=1, source_target_pairs={{1,0},{2,1},{3,2},{4,3},{5,4},{6,5},{7,6},{8,7},{9,8},{10,9},{11,1... | collective-permute-start | bytes 7864328 | tf_op jit(solution)/shard_map/ppermute | solution.py:30
  125.8 3.0 fusion.191
  131.7 135.9 %collective-permute-done.3 = bf16[2,256,2560]{1,2,0:T(8,128)(2,1)S(1)} collective-permute-done((bf16[2,256,2560]{1,2,0:T(8,128)(2,1)}, bf16[2,256,2560]{1,2,0:T(8,128)(2,1)S(1)}, u32[]{:S(2)}, u32[]{:S(2)}) %collective-permute-start.3) | collective-permute-done | bytes 2621472 | tf_op jit(solution)/shard_map/ppermute | solution.py:19
  267.6 2.1 collective-permute-start.4
  272.4 2.9 fusion.184
  278.1 1.9 fusion.185
  280.0 2.2 select_reduce_fusion.9
  282.2 2.2 select_reduce_fusion
  285.9 2.9 fusion.186
  290.3 14.5 %collective-permute-done.4 = bf16[2,256,2560]{1,2,0:T(8,128)(2,1)S(1)} collective-permute-done((bf16[2,256,2560]{1,2,0:T(8,128)(2,1)}, bf16[2,256,2560]{1,2,0:T(8,128)(2,1)S(1)}, u32[]{:S(2)}, u32[]{:S(2)}) %collective-permute-start.4) | collective-permute-done | bytes 2621472 | tf_op jit(solution)/shard_map/ppermute | solution.py:19
  321.4 4.0 %fusion.39 = f32[128,20,128]{2,0,1:T(8,128)} fusion(bf16[256,20,128]{0,2,1:T(8,128)(2,1)S(1)} %bitcast.656, f32[20,128,256]{2,1,0:T(8,128)} %get-tuple-element.127, f32[20,128]{1,0:T(8,128)S(1)} %get-tuple-element.71, pred[256]{0:T(512)(128)(4,1)S(1)} %get-tuple-element.137, f32[128,20]{0,1:T(8,128)S(1)} %get-tuple-element.68, ...), kind=kOutput, calls=%fused_computation.126 | convolution fusion | flops 171048960 | bytes 5273856 | tf_op jit(solution)/shard_map/hqk,khd->qhd/dot_general | solution.py:51
  325.5 4.6 %fusion.21 = f32[128,20,128]{2,0,1:T(8,128)} fusion(bf16[256,20,128]{0,2,1:T(8,128)(2,1)} %bitcast.655, f32[20,128,256]{2,1,0:T(8,128)} %get-tuple-element.109, f32[20,128]{1,0:T(8,128)S(1)} %get-tuple-element.73, pred[256]{0:T(512)(128)(4,1)S(1)} %get-tuple-element.136, f32[128,20]{0,1:T(8,128)S(1)} %get-tuple-element.69, f32[128,20]{0,1:T(8,128)S(1)} %get-tuple-element.72), kind=kOutput, calls=%fused_computation.99 | convolution fusion | flops 171048960 | bytes 5273856 | tf_op jit(solution)/shard_map/hqk,khd->qhd/dot_general | solution.py:51
  330.1 3.8 %fusion.37 = f32[128,20,128]{2,0,1:T(8,128)} fusion(f32[128,20,128]{2,0,1:T(8,128)} %fusion.39, bf16[256,20,128]{0,2,1:T(8,128)(2,1)S(1)} %bitcast.630, f32[20,256,128]{2,1,0:T(8,128)S(1)} %get-tuple-element.125, f32[20,128]{1,0:T(8,128)S(1)} %get-tuple-element.29, pred[256]{0:T(512)(128)(4,1)S(1)} %broadcast_bitcast_fusion.16, ...), kind=kOutput, calls=%fused_computation.123 | convolution fusion | flops 171048960 | bytes 6574336 | tf_op jit(solution)/shard_map/hqk,khd->qhd/dot_general | solution.py:51
  333.9 2.4 fusion.19
  336.3 2.3 fusion.35
  355.5 1.6 copy.180
  (123 shorter events, 46.7 us)
Async XLA Ops:
  1.6 27.6 %copy-start.11 = (bf16[256,2560]{0,1:T(8,128)(2,1)}, bf16[256,2560]{0,1:T(8,128)(2,1)S(1)}, u32[]{:S(2)}) copy-start(bf16[256,2560]{0,1:T(8,128)(2,1)S(1)} %copy.107) | copy-start | bytes 3932164
  3.7 21.9 %copy-start.14 = (s32[2,8]{1,0:T(2,128)S(1)}, s32[2,8]{1,0:T(2,128)}, u32[]{:S(2)}) copy-start(s32[2,8]{1,0:T(2,128)} %param.7) | copy-start | bytes 196
  5.4 78.0 %collective-permute-start.2 = (bf16[2,256,2560]{1,2,0:T(8,128)(2,1)}, bf16[2,256,2560]{1,2,0:T(8,128)(2,1)}, u32[]{:S(2)}, u32[]{:S(2)}) collective-permute-start(bf16[2,256,2560]{1,2,0:T(8,128)(2,1)} %pad_maximum_fusion), channel_id=1, source_target_pairs={{2,0},{3,1},{4,2},{5,3},{6,4},{7,5},{8,6},{9,7},{10,8},{11,9},{12,... | collective-permute-start | bytes 7864328 | tf_op jit(solution)/shard_map/ppermute | solution.py:19
  8.5 92.3 %collective-permute-start = (bf16[2,256,2560]{1,2,0:T(8,128)(2,1)}, bf16[2,256,2560]{1,2,0:T(8,128)(2,1)}, u32[]{:S(2)}, u32[]{:S(2)}) collective-permute-start(bf16[2,256,2560]{1,2,0:T(8,128)(2,1)} %pad_maximum_fusion), channel_id=1, source_target_pairs={{0,1},{1,2},{2,3},{3,4},{4,5},{5,6},{6,7},{7,8},{8,9},{9,10},{10,1... | collective-permute-start | bytes 7864328 | tf_op jit(solution)/shard_map/ppermute | solution.py:27
  11.6 260.8 %collective-permute-start.7 = (bf16[2,256,2560]{1,2,0:T(8,128)(2,1)}, bf16[2,256,2560]{1,2,0:T(8,128)(2,1)}, u32[]{:S(2)}, u32[]{:S(2)}) collective-permute-start(bf16[2,256,2560]{1,2,0:T(8,128)(2,1)} %pad_maximum_fusion), channel_id=1, source_target_pairs={{0,8},{1,9},{2,10},{3,11},{4,12},{5,13},{6,14},{7,15},{16,24},{17,... | collective-permute-start | bytes 7864328 | tf_op jit(solution)/shard_map/ppermute | solution.py:19
  12.9 265.2 %collective-permute-start.6 = (bf16[2,256,2560]{1,2,0:T(8,128)(2,1)}, bf16[2,256,2560]{1,2,0:T(8,128)(2,1)}, u32[]{:S(2)}, u32[]{:S(2)}) collective-permute-start(bf16[2,256,2560]{1,2,0:T(8,128)(2,1)} %pad_maximum_fusion), channel_id=1, source_target_pairs={{8,0},{9,1},{10,2},{11,3},{12,4},{13,5},{14,6},{15,7},{24,16},{25,... | collective-permute-start | bytes 7864328 | tf_op jit(solution)/shard_map/ppermute | solution.py:19
  20.8 265.1 %collective-permute-start.5 = (bf16[2,256,2560]{1,2,0:T(8,128)(2,1)}, bf16[2,256,2560]{1,2,0:T(8,128)(2,1)}, u32[]{:S(2)}, u32[]{:S(2)}) collective-permute-start(bf16[2,256,2560]{1,2,0:T(8,128)(2,1)} %pad_maximum_fusion), channel_id=1, source_target_pairs={{0,4},{1,5},{2,6},{3,7},{4,8},{5,9},{6,10},{7,11},{8,12},{9,13},{1... | collective-permute-start | bytes 7864328 | tf_op jit(solution)/shard_map/ppermute | solution.py:19
  83.4 184.2 %collective-permute-start.3 = (bf16[2,256,2560]{1,2,0:T(8,128)(2,1)}, bf16[2,256,2560]{1,2,0:T(8,128)(2,1)S(1)}, u32[]{:S(2)}, u32[]{:S(2)}) collective-permute-start(bf16[2,256,2560]{1,2,0:T(8,128)(2,1)} %pad_maximum_fusion), channel_id=1, source_target_pairs={{0,2},{1,3},{2,4},{3,5},{4,6},{5,7},{6,8},{7,9},{8,10},{9,11},{10,... | collective-permute-start | bytes 7864328 | tf_op jit(solution)/shard_map/ppermute | solution.py:19
  100.7 174.6 %collective-permute-start.1 = (bf16[2,256,2560]{1,2,0:T(8,128)(2,1)}, bf16[2,256,2560]{1,2,0:T(8,128)(2,1)S(1)}, u32[]{:S(2)}, u32[]{:S(2)}) collective-permute-start(bf16[2,256,2560]{1,2,0:T(8,128)(2,1)} %pad_maximum_fusion), channel_id=1, source_target_pairs={{1,0},{2,1},{3,2},{4,3},{5,4},{6,5},{7,6},{8,7},{9,8},{10,9},{11,1... | collective-permute-start | bytes 7864328 | tf_op jit(solution)/shard_map/ppermute | solution.py:30
  267.6 37.1 %collective-permute-start.4 = (bf16[2,256,2560]{1,2,0:T(8,128)(2,1)}, bf16[2,256,2560]{1,2,0:T(8,128)(2,1)S(1)}, u32[]{:S(2)}, u32[]{:S(2)}) collective-permute-start(bf16[2,256,2560]{1,2,0:T(8,128)(2,1)} %pad_maximum_fusion), channel_id=1, source_target_pairs={{4,0},{5,1},{6,2},{7,3},{8,4},{9,5},{10,6},{11,7},{12,8},{13,9},{1... | collective-permute-start | bytes 7864328 | tf_op jit(solution)/shard_map/ppermute | solution.py:19
  306.7 1.7 copy-start.10
  312.5 1.7 copy-start.7
  313.1 2.1 copy-start.9
  319.0 1.7 copy-start.5
  319.6 1.8 copy-start.12
  325.5 4.6 %copy-start.1 = (bf16[1,256,2560]{1,2,0:T(8,128)(2,1)S(1)}, bf16[1,256,2560]{1,2,0:T(8,128)(2,1)}, u32[]{:S(2)}) copy-start(bf16[1,256,2560]{1,2,0:T(8,128)(2,1)} %get-tuple-element.64) | copy-start | bytes 3932164
  333.9 2.4 copy-start.3
  340.6 1.3 copy-start
  343.0 1.3 copy-start.4
  345.3 1.3 copy-start.2
  349.8 1.7 copy-start.8
  349.8 2.1 copy-start.13
  351.9 1.7 copy-start.6
where the time goes:
time: 364 us; the launch traced here: 357 us
  waiting for transfers between devices  212 us (58%)
  matrix products  49.5 us (14%)
  starting transfers between devices  49 us (13%)
  local copies, waits for them, and re-layouts  32.5 us (9%)
  other arithmetic  13.8 us (4%)
    ppermute x6, waiting for transfers between devices, passed_along(): lax.ppermute(value, axis, [(source, source + steps) for source in range(l...  198 us
    dot_general x18, matrix products, absorb_block(): jnp.einsum('hqk,khd->qhd', rounded, value_rows, preferred_element_type=jn...  30.5 us
    ppermute x1, starting transfers between devices, padded(): lax.ppermute(lax.slice_in_dim(block, 0, width, axis=dim), axis, backward)  25 us
    ppermute x6, starting transfers between devices, passed_along(): lax.ppermute(value, axis, [(source, source + steps) for source in range(l...  20.8 us
    dot_general x18, matrix products, absorb_block(): jnp.einsum('qhd,khd->hqk', query_rows, key_rows, preferred_element_type=j...  18.9 us
    slice x8, local copies, waits for them, and re-layouts, absorb_tile(): value_rows = key_tile[1].reshape(local_blocks * block_len, heads, head_dim)  16.3 us
    ppermute x1, waiting for transfers between devices, padded(): lax.ppermute(lax.slice_in_dim(block, block.shape[dim] - width, None, axis...  13.5 us
    reduce_sum x18, other arithmetic, absorb_block(): denominator = denominator * rescale + jnp.sum(weight, axis=-1)  11.3 us
  transfers between devices with their start and end apart: 8, of which 4 were waited for; matrix products, arithmetic and copies ran while one was open for 11% of the time, Pallas kernels for 0%

commit v1 on v0

v1 whole, which is shorter than its diff:
```python
import functools
import math

import jax
import jax.numpy as jnp
from jax import lax
from jax.experimental import pallas as pl
from jax.experimental.pallas import tpu as pltpu
from jax.sharding import PartitionSpec as P

DH = 128
BLOCK = 128
HEAD_SPLIT = (5, 5, 5, 5)
TILES = 9


def head_chunks(heads):
    chunks, first = [], 0
    for count in HEAD_SPLIT:
        count = min(count, heads - first)
        if count > 0:
            chunks.append((first, count))
            first += count
    if first < heads:
        chunks.append((first, heads - first))
    return chunks


def shifted(value, steps):
    count = lax.axis_size("blk")
    pairs = [(i, i + steps) for i in range(count) if 0 <= i + steps < count]
    return lax.ppermute(value, "blk", pairs)


def swapped(value, bit):
    count = lax.axis_size("blk")
    return lax.ppermute(value, "blk", [(i, i ^ bit) for i in range(count)])


def attend_kernel(first, count, local_blocks, keep, place, kept, *refs):
    q_hbm, k_hbm, v_hbm = refs[:3]
    remote = refs[3 : 3 + TILES - 1]
    out_hbm = refs[3 + TILES]
    queries, tiles, result, sems, out_sem = refs[4 + TILES :]
    columns = pl.ds(first * DH, count * DH)
    copies = [
        pltpu.make_async_copy(q_hbm.at[:, columns], queries, sems.at[0]),
        pltpu.make_async_copy(k_hbm.at[:, columns], tiles.at[0, 0], sems.at[1]),
        pltpu.make_async_copy(v_hbm.at[:, columns], tiles.at[0, 1], sems.at[2]),
    ]
    for index, ref in enumerate(remote):
        copies.append(pltpu.make_async_copy(ref, tiles.at[index + 1], sems.at[3 + index]))
    for copy in copies:
        copy.start()
    for copy in copies:
        copy.wait()
    position = place[0]
    core, side = position % 2, (position // 2) % 2
    scale = math.log2(math.e) / math.sqrt(DH)
    for block in range(local_blocks):
        slots, halves = [], []
        for entry in range(keep):
            listed = kept[block, entry]
            offset = listed // local_blocks - position
            ahead = (offset > 0).astype(jnp.int32)
            near = jnp.abs(offset)
            step = (
                (near >= 1).astype(jnp.int32)
                + (near >= 2).astype(jnp.int32)
                + (near >= 4).astype(jnp.int32)
                + (near >= 8).astype(jnp.int32)
            )
            flip = jnp.where(step == 1, core, jnp.where(step == 2, side, 0))
            first_of_pair = (ahead + flip) % 2
            slots.append(jnp.where(step == 0, 0, 2 * step - first_of_pair))
            halves.append(pl.multiple_of((listed % local_blocks) * BLOCK, BLOCK))
        for head in range(count):
            lanes = pl.ds(head * DH, DH)
            query = queries[pl.ds(block * BLOCK, BLOCK), lanes]
            keys = jnp.concatenate(
                [tiles[s, 0, pl.ds(h, BLOCK), lanes] for s, h in zip(slots, halves)], axis=0
            )
            values = jnp.concatenate(
                [tiles[s, 1, pl.ds(h, BLOCK), lanes] for s, h in zip(slots, halves)], axis=0
            )
            scores = lax.dot_general(
                query, keys, (((1,), (1,)), ((), ())), preferred_element_type=jnp.float32
            )
            top = jnp.max(scores, axis=1, keepdims=True)
            weight = jnp.exp2((scores - top) * scale)
            total = jnp.sum(weight, axis=1, keepdims=True)
            numerator = jnp.dot(
                weight.astype(jnp.bfloat16), values, preferred_element_type=jnp.float32
            )
            result[pl.ds(block * BLOCK, BLOCK), lanes] = (numerator / total).astype(jnp.bfloat16)
    copy = pltpu.make_async_copy(result, out_hbm.at[:, columns], out_sem)
    copy.start()
    copy.wait()


def attend(first, count, place, kept, queries, keys, values, remote, attended):
    rows = queries.shape[0]
    local_blocks, keep = kept.shape
    width = count * DH
    anywhere = pl.BlockSpec(memory_space=pl.ANY)
    scalars = pl.BlockSpec(memory_space=pltpu.SMEM)
    pairs = local_blocks * keep * count
    return pl.pallas_call(
        functools.partial(attend_kernel, first, count, local_blocks, keep),
        out_shape=jax.ShapeDtypeStruct(attended.shape, attended.dtype),
        in_specs=[scalars, scalars] + [anywhere] * (3 + len(remote) + 1),
        out_specs=anywhere,
        scratch_shapes=[
            pltpu.VMEM((rows, width), jnp.bfloat16),
            pltpu.VMEM((TILES, 2, rows, width), jnp.bfloat16),
            pltpu.VMEM((rows, width), jnp.bfloat16),
            pltpu.SemaphoreType.DMA((2 + TILES,)),
            pltpu.SemaphoreType.DMA,
        ],
        input_output_aliases={5 + len(remote): 0},
        compiler_params=pltpu.CompilerParams(vmem_limit_bytes=40 * 1024 * 1024),
        cost_estimate=pl.CostEstimate(
            flops=4 * pairs * BLOCK * BLOCK * DH,
            bytes_accessed=(2 * TILES + 2) * rows * width * 2,
            transcendentals=pairs * BLOCK * BLOCK,
        ),
        name=f"attend_{first}",
    )(place, kept, queries, keys, values, *remote, attended)


def per_device(queries, keys, values, kept_blocks):
    position = lax.axis_index("blk")
    place = position.astype(jnp.int32).reshape(1)
    core, side = position % 2, (position // 2) % 2
    heads = queries.shape[1] // DH
    chunks = head_chunks(heads)
    own = []
    for first, count in chunks:
        lanes = slice(first * DH, (first + count) * DH)
        own.append(jnp.stack((keys[:, lanes], values[:, lanes])))
    attended = jnp.zeros(queries.shape, jnp.bfloat16)
    for (first, count), tile in zip(chunks, own):
        from_below, from_above = shifted(tile, 4), shifted(tile, -4)
        near_side = swapped(tile, 2)
        near_core = swapped(tile, 1)
        far_below, far_above = shifted(from_below, 4), shifted(from_above, -4)
        far_side = swapped(jnp.where(side == 0, from_above, from_below), 2)
        far_core = swapped(jnp.where(core == side, near_side, far_side), 1)
        remote = (
            near_core, far_core, near_side, far_side, from_above, from_below, far_above, far_below
        )
        attended = attend(
            first, count, place, kept_blocks, queries, keys, values, remote, attended
        )
    return attended


def solution(mesh):
    placed = P(("clip", "blk"), None)
    return jax.shard_map(
        per_device, mesh=mesh, in_specs=(placed,) * 4, out_specs=placed, check_vma=False
    )
```

time: 364 us -> 165 us (0.45)
  the two profiles are of different devices: /device:TPU:19 before, /device:TPU:0 now
where the time goes in v1:
time: 165 us; the launch traced here: 164 us
  waiting for transfers between devices  60.1 us (36%)
  starting transfers between devices  59.7 us (36%)
  Pallas kernels  28.1 us (17%)
  other arithmetic  11 us (7%)
  local copies, waits for them, and re-layouts  4.79 us (3%)
    ppermute x16, starting transfers between devices, shifted(): return lax.ppermute(value, 'blk', pairs)  46.7 us
    ppermute x16, waiting for transfers between devices, swapped(): return lax.ppermute(value, 'blk', [(i, i ^ bit) for i in range(count)])  37.1 us
    pallas_call x4, Pallas kernels, attend(): pl.pallas_call(functools.partial(attend_kernel, first, count, local_block...  28.1 us
    ppermute x16, waiting for transfers between devices, shifted(): return lax.ppermute(value, 'blk', pairs)  23.1 us
    ppermute x16, starting transfers between devices, swapped(): return lax.ppermute(value, 'blk', [(i, i ^ bit) for i in range(count)])  12.9 us
    another operation x4, other arithmetic, per_device(): own.append(jnp.stack((keys[:, lanes], values[:, lanes])))  3.91 us
    select_n x4, other arithmetic, per_device(): far_core = swapped(jnp.where(core == side, near_side, far_side), 1)  3.67 us
    select_n x4, other arithmetic, per_device(): far_side = swapped(jnp.where(side == 0, from_above, from_below), 2)  3.37 us
  transfers between devices with their start and end apart: 32, of which 9 were waited for; matrix products, arithmetic and copies ran while one was open for 7% of the time, Pallas kernels for 13%

profile of v1, /device:TPU:0, one launch (start us, length us, event | category | flops | bytes accessed | tf_op | source)
XLA Modules:
  0.0 164.2 jit_solution(10829428606785439801)
XLA Ops:
  0.0 2.8 %slice_bitcast_fusion = (bf16[1,256,640]{2,1,0:T(8,128)(2,1)S(1)}, bf16[1,256,640]{2,1,0:T(8,128)(2,1)S(1)}, bf16[1,256,640]{2,1,0:T(8,128)(2,1)S(1)}, bf16[1,25...) fusion(bf16[256,2560]{1,0:T(8,128)(2,1)} %refs_2_.7, ...), kind=kLoop, calls=%fused_computation.12 | loop fusion | bytes 5242880 | tf_op jit(solution)/shard_map/stack | solution.py:140
  2.9 1.3 collective-permute-start.26
  4.2 5.6 %collective-permute-start.27 = (bf16[2,256,640]{2,1,0:T(8,128)(2,1)S(1)}, bf16[2,256,640]{2,1,0:T(8,128)(2,1)S(1)}, u32[]{:S(2)}, u32[]{:S(2)}) collective-permute-start(bf16[2,256,640]{2,1,0:T(8,128)(2,1)S(1)} %pad_maximum_fusion.3), channel_id=1, source_target_pairs={{0,4},{1,5},{2,6},{3,7},{4,8},{5,9},{6,10},{7,11},{8,12},{9,13},{1... | collective-permute-start | bytes 1966088 | tf_op jit(solution)/shard_map/ppermute | solution.py:32
  9.8 2.0 %collective-permute-start.25 = (bf16[2,256,640]{2,1,0:T(8,128)(2,1)S(1)}, bf16[2,256,640]{2,1,0:T(8,128)(2,1)S(1)}, u32[]{:S(2)}, u32[]{:S(2)}) collective-permute-start(bf16[2,256,640]{2,1,0:T(8,128)(2,1)S(1)} %pad_maximum_fusion.3), channel_id=1, source_target_pairs={{0,2},{1,3},{2,0},{3,1},{4,6},{5,7},{6,4},{7,5},{8,10},{9,11},{10,... | collective-permute-start | bytes 1966088 | tf_op jit(solution)/shard_map/ppermute | solution.py:37
  14.0 9.3 %collective-permute-done.26.refs_7_ = bf16[2,256,640]{2,1,0:T(8,128)(2,1)S(1)} collective-permute-done((bf16[2,256,640]{2,1,0:T(8,128)(2,1)S(1)}, bf16[2,256,640]{2,1,0:T(8,128)(2,1)S(1)}, u32[]{:S(2)}, u32[]{:S(2)}) %collective-permute-start.26) | collective-permute-done | bytes 655392 | tf_op jit(solution)/shard_map/ppermute | solution.py:32
  23.3 4.0 %collective-permute-start.19 = (bf16[2,256,640]{2,1,0:T(8,128)(2,1)}, bf16[2,256,640]{2,1,0:T(8,128)(2,1)S(1)}, u32[]{:S(2)}, u32[]{:S(2)}) collective-permute-start(bf16[2,256,640]{2,1,0:T(8,128)(2,1)} %pad_maximum_fusion.2), channel_id=1, source_target_pairs={{0,4},{1,5},{2,6},{3,7},{4,8},{5,9},{6,10},{7,11},{8,12},{9,13},{1... | collective-permute-start | bytes 1966088 | tf_op jit(solution)/shard_map/ppermute | solution.py:32
  27.3 1.6 collective-permute-start.17
  32.0 5.2 %collective-permute-done.18.refs_7_ = bf16[2,256,640]{2,1,0:T(8,128)(2,1)S(1)} collective-permute-done((bf16[2,256,640]{2,1,0:T(8,128)(2,1)}, bf16[2,256,640]{2,1,0:T(8,128)(2,1)S(1)}, u32[]{:S(2)}, u32[]{:S(2)}) %collective-permute-start.18) | collective-permute-done | bytes 655392 | tf_op jit(solution)/shard_map/ppermute | solution.py:32
  37.2 4.7 %collective-permute-start.11 = (bf16[2,256,640]{2,1,0:T(8,128)(2,1)}, bf16[2,256,640]{2,1,0:T(8,128)(2,1)}, u32[]{:S(2)}, u32[]{:S(2)}) collective-permute-start(bf16[2,256,640]{2,1,0:T(8,128)(2,1)} %pad_maximum_fusion.1), channel_id=1, source_target_pairs={{0,4},{1,5},{2,6},{3,7},{4,8},{5,9},{6,10},{7,11},{8,12},{9,13},{1... | collective-permute-start | bytes 1966088 | tf_op jit(solution)/shard_map/ppermute | solution.py:32
  41.8 1.9 %collective-permute-start.9 = (bf16[2,256,640]{2,1,0:T(8,128)(2,1)}, bf16[2,256,640]{2,1,0:T(8,128)(2,1)}, u32[]{:S(2)}, u32[]{:S(2)}) collective-permute-start(bf16[2,256,640]{2,1,0:T(8,128)(2,1)} %pad_maximum_fusion.1), channel_id=1, source_target_pairs={{0,2},{1,3},{2,0},{3,1},{4,6},{5,7},{6,4},{7,5},{8,10},{9,11},{10,... | collective-permute-start | bytes 1966088 | tf_op jit(solution)/shard_map/ppermute | solution.py:37
  43.7 2.0 %pad_maximum_fusion = bf16[2,256,640]{2,1,0:T(8,128)(2,1)} fusion(bf16[1,256,640]{2,1,0:T(8,128)(2,1)} %get-tuple-element.12, bf16[1,256,640]{2,1,0:T(8,128)(2,1)} %get-tuple-element.13), kind=kLoop, calls=%fused_computation | loop fusion | flops 327680 | bytes 1310720 | tf_op jit(solution)/shard_map/stack | solution.py:140
  48.0 2.7 %collective-permute-done.10.refs_7_ = bf16[2,256,640]{2,1,0:T(8,128)(2,1)} collective-permute-done((bf16[2,256,640]{2,1,0:T(8,128)(2,1)}, bf16[2,256,640]{2,1,0:T(8,128)(2,1)}, u32[]{:S(2)}, u32[]{:S(2)}) %collective-permute-start.10) | collective-permute-done | bytes 655392 | tf_op jit(solution)/shard_map/ppermute | solution.py:32
  50.7 5.0 %collective-permute-start.3 = (bf16[2,256,640]{2,1,0:T(8,128)(2,1)}, bf16[2,256,640]{2,1,0:T(8,128)(2,1)}, u32[]{:S(2)}, u32[]{:S(2)}) collective-permute-start(bf16[2,256,640]{2,1,0:T(8,128)(2,1)} %pad_maximum_fusion), channel_id=1, source_target_pairs={{0,4},{1,5},{2,6},{3,7},{4,8},{5,9},{6,10},{7,11},{8,12},{9,13},{1... | collective-permute-start | bytes 1966088 | tf_op jit(solution)/shard_map/ppermute | solution.py:32
  55.7 2.1 %collective-permute-start.1 = (bf16[2,256,640]{2,1,0:T(8,128)(2,1)}, bf16[2,256,640]{2,1,0:T(8,128)(2,1)}, u32[]{:S(2)}, u32[]{:S(2)}) collective-permute-start(bf16[2,256,640]{2,1,0:T(8,128)(2,1)} %pad_maximum_fusion), channel_id=1, source_target_pairs={{0,2},{1,3},{2,0},{3,1},{4,6},{5,7},{6,4},{7,5},{8,10},{9,11},{10,... | collective-permute-start | bytes 1966088 | tf_op jit(solution)/shard_map/ppermute | solution.py:37
  59.7 5.8 %collective-permute-done.2.refs_7_ = bf16[2,256,640]{2,1,0:T(8,128)(2,1)} collective-permute-done((bf16[2,256,640]{2,1,0:T(8,128)(2,1)}, bf16[2,256,640]{2,1,0:T(8,128)(2,1)}, u32[]{:S(2)}, u32[]{:S(2)}) %collective-permute-start.2) | collective-permute-done | bytes 655392 | tf_op jit(solution)/shard_map/ppermute | solution.py:32
  65.4 2.1 %collective-permute-start.20 = (bf16[2,256,640]{2,1,0:T(8,128)(2,1)S(1)}, bf16[2,256,640]{2,1,0:T(8,128)(2,1)S(1)}, u32[]{:S(2)}, u32[]{:S(2)}) collective-permute-start(bf16[2,256,640]{2,1,0:T(8,128)(2,1)S(1)} %broadcast_select_fusion.1), channel_id=1, source_target_pairs={{0,2},{1,3},{2,0},{3,1},{4,6},{5,7},{6,4},{7,5},{8,10},{9,11},{10,... | collective-permute-start | bytes 1966088 | tf_op jit(solution)/shard_map/ppermute | solution.py:37
  69.3 4.5 %collective-permute-done.1.refs_5_ = bf16[2,256,640]{2,1,0:T(8,128)(2,1)} collective-permute-done((bf16[2,256,640]{2,1,0:T(8,128)(2,1)}, bf16[2,256,640]{2,1,0:T(8,128)(2,1)}, u32[]{:S(2)}, u32[]{:S(2)}) %collective-permute-start.1) | collective-permute-done | bytes 655392 | tf_op jit(solution)/shard_map/ppermute | solution.py:37
  73.8 3.2 %collective-permute-start.31 = (bf16[2,256,640]{2,1,0:T(8,128)(2,1)S(1)}, bf16[2,256,640]{2,1,0:T(8,128)(2,1)S(1)}, u32[]{:S(2)}, u32[]{:S(2)}) collective-permute-start(bf16[2,256,640]{2,1,0:T(8,128)(2,1)S(1)} %collective-permute-done.27.refs_8_), channel_id=1, source_target_pairs={{0,4},{1,5},{2,6},{3,7},{4,8},{5,9},{6,10},{7,11},{8,12},{9,13},{1... | collective-permute-start | bytes 1966088 | tf_op jit(solution)/shard_map/ppermute | solution.py:32
  77.1 10.8 %collective-permute-done.28.refs_6_ = bf16[2,256,640]{2,1,0:T(8,128)(2,1)} collective-permute-done((bf16[2,256,640]{2,1,0:T(8,128)(2,1)}, bf16[2,256,640]{2,1,0:T(8,128)(2,1)}, u32[]{:S(2)}, u32[]{:S(2)}) %collective-permute-start.28) | collective-permute-done | bytes 655392 | tf_op jit(solution)/shard_map/ppermute | solution.py:37
  89.2 4.6 %collective-permute-start.23 = (bf16[2,256,640]{2,1,0:T(8,128)(2,1)S(1)}, bf16[2,256,640]{2,1,0:T(8,128)(2,1)S(1)}, u32[]{:S(2)}, u32[]{:S(2)}) collective-permute-start(bf16[2,256,640]{2,1,0:T(8,128)(2,1)S(1)} %collective-permute-done.19.refs_8_), channel_id=1, source_target_pairs={{0,4},{1,5},{2,6},{3,7},{4,8},{5,9},{6,10},{7,11},{8,12},{9,13},{1... | collective-permute-start | bytes 1966088 | tf_op jit(solution)/shard_map/ppermute | solution.py:32
  95.0 6.8 %collective-permute-done.20.refs_6_ = bf16[2,256,640]{2,1,0:T(8,128)(2,1)S(1)} collective-permute-done((bf16[2,256,640]{2,1,0:T(8,128)(2,1)S(1)}, bf16[2,256,640]{2,1,0:T(8,128)(2,1)S(1)}, u32[]{:S(2)}, u32[]{:S(2)}) %collective-permute-start.20) | collective-permute-done | bytes 655392 | tf_op jit(solution)/shard_map/ppermute | solution.py:37
  101.8 2.0 %collective-permute-start.4 = (bf16[2,256,640]{2,1,0:T(8,128)(2,1)S(1)}, bf16[2,256,640]{2,1,0:T(8,128)(2,1)S(1)}, u32[]{:S(2)}, u32[]{:S(2)}) collective-permute-start(bf16[2,256,640]{2,1,0:T(8,128)(2,1)S(1)} %broadcast_select_fusion.3), channel_id=1, source_target_pairs={{0,2},{1,3},{2,0},{3,1},{4,6},{5,7},{6,4},{7,5},{8,10},{9,11},{10,... | collective-permute-start | bytes 1966088 | tf_op jit(solution)/shard_map/ppermute | solution.py:37
  105.0 1.3 collective-permute-start.14
  106.3 4.6 %collective-permute-start.15 = (bf16[2,256,640]{2,1,0:T(8,128)(2,1)}, bf16[2,256,640]{2,1,0:T(8,128)(2,1)S(1)}, u32[]{:S(2)}, u32[]{:S(2)}) collective-permute-start(bf16[2,256,640]{2,1,0:T(8,128)(2,1)} %collective-permute-done.11.refs_8_), channel_id=1, source_target_pairs={{0,4},{1,5},{2,6},{3,7},{4,8},{5,9},{6,10},{7,11},{8,12},{9,13},{1... | collective-permute-start | bytes 1966088 | tf_op jit(solution)/shard_map/ppermute | solution.py:32
  111.0 4.9 %collective-permute-done.12.refs_6_ = bf16[2,256,640]{2,1,0:T(8,128)(2,1)S(1)} collective-permute-done((bf16[2,256,640]{2,1,0:T(8,128)(2,1)S(1)}, bf16[2,256,640]{2,1,0:T(8,128)(2,1)S(1)}, u32[]{:S(2)}, u32[]{:S(2)}) %collective-permute-start.12) | collective-permute-done | bytes 655392 | tf_op jit(solution)/shard_map/ppermute | solution.py:37
  117.2 10.1 %collective-permute-done.4.refs_6_ = bf16[2,256,640]{2,1,0:T(8,128)(2,1)S(1)} collective-permute-done((bf16[2,256,640]{2,1,0:T(8,128)(2,1)S(1)}, bf16[2,256,640]{2,1,0:T(8,128)(2,1)S(1)}, u32[]{:S(2)}, u32[]{:S(2)}) %collective-permute-start.4) | collective-permute-done | bytes 655392 | tf_op jit(solution)/shard_map/ppermute | solution.py:37
  128.5 1.3 collective-permute-start.6
  129.8 4.8 %collective-permute-start.7 = (bf16[2,256,640]{2,1,0:T(8,128)(2,1)}, bf16[2,256,640]{2,1,0:T(8,128)(2,1)S(1)}, u32[]{:S(2)}, u32[]{:S(2)}) collective-permute-start(bf16[2,256,640]{2,1,0:T(8,128)(2,1)} %collective-permute-done.3.refs_8_), channel_id=1, source_target_pairs={{0,4},{1,5},{2,6},{3,7},{4,8},{5,9},{6,10},{7,11},{8,12},{9,13},{1... | collective-permute-start | bytes 1966088 | tf_op jit(solution)/shard_map/ppermute | solution.py:32
  135.8 7.4 %attend_0.1.refs_11_ = bf16[256,2560]{1,0:T(8,128)(2,1)} custom-call(s32[1]{0:T(128)} %bitcast.place, s32[2,8]{1,0:T(2,128)S(1)} %copy-done.5, bf16[256,2560]{1,0:T(8,128)(2,1)S(1)} %copy-done.2, bf16[256,2560]{1,0:T(8,128)(2,1)S(1)} %copy-done, bf16[256,2560]{1,0:T(8,128)(2,1)S(1)} %copy-done.1, ...), custom_call_target="tpu_custom_call", output_to_operand_aliasing={{}: (13, {})} | custom-call | flops 671088640 | bytes 6553600 | tf_op jit(solution)/shard_map/attend_0/pallas_call | solution.py:108
  143.2 6.6 %attend_5.1.refs_11_ = bf16[256,2560]{1,0:T(8,128)(2,1)} custom-call(s32[1]{0:T(128)} %bitcast.place, s32[2,8]{1,0:T(2,128)S(1)} %copy-done.5, bf16[256,2560]{1,0:T(8,128)(2,1)S(1)} %copy-done.2, bf16[256,2560]{1,0:T(8,128)(2,1)S(1)} %copy-done, bf16[256,2560]{1,0:T(8,128)(2,1)S(1)} %copy-done.1, ...), custom_call_target="tpu_custom_call", output_to_operand_aliasing={{}: (13, {})} | custom-call | flops 671088640 | bytes 6553600 | tf_op jit(solution)/shard_map/attend_5/pallas_call | solution.py:108
  149.8 7.0 %attend_10.1.refs_11_ = bf16[256,2560]{1,0:T(8,128)(2,1)} custom-call(s32[1]{0:T(128)} %bitcast.place, s32[2,8]{1,0:T(2,128)S(1)} %copy-done.5, bf16[256,2560]{1,0:T(8,128)(2,1)S(1)} %copy-done.2, bf16[256,2560]{1,0:T(8,128)(2,1)S(1)} %copy-done, bf16[256,2560]{1,0:T(8,128)(2,1)S(1)} %copy-done.1, ...), custom_call_target="tpu_custom_call", output_to_operand_aliasing={{}: (13, {})} | custom-call | flops 671088640 | bytes 6553600 | tf_op jit(solution)/shard_map/attend_10/pallas_call | solution.py:108
  156.9 7.2 %attend_15.1 = bf16[256,2560]{1,0:T(8,128)(2,1)} custom-call(s32[1]{0:T(128)} %bitcast.place, s32[2,8]{1,0:T(2,128)S(1)} %copy-done.5, bf16[256,2560]{1,0:T(8,128)(2,1)S(1)} %copy-done.2, bf16[256,2560]{1,0:T(8,128)(2,1)S(1)} %copy-done, bf16[256,2560]{1,0:T(8,128)(2,1)S(1)} %copy-done.1, ...), custom_call_target="tpu_custom_call", output_to_operand_aliasing={{}: (13, {})} | custom-call | flops 671088640 | bytes 6553600 | tf_op jit(solution)/shard_map/attend_15/pallas_call | solution.py:108
  (62 shorter events, 18.6 us)
Async XLA Ops:
  2.9 20.5 %collective-permute-start.26 = (bf16[2,256,640]{2,1,0:T(8,128)(2,1)S(1)}, bf16[2,256,640]{2,1,0:T(8,128)(2,1)S(1)}, u32[]{:S(2)}, u32[]{:S(2)}) collective-permute-start(bf16[2,256,640]{2,1,0:T(8,128)(2,1)S(1)} %pad_maximum_fusion.3), channel_id=1, source_target_pairs={{4,0},{5,1},{6,2},{7,3},{8,4},{9,5},{10,6},{11,7},{12,8},{13,9},{1... | collective-permute-start | bytes 1966088 | tf_op jit(solution)/shard_map/ppermute | solution.py:32
  4.2 23.2 %collective-permute-start.27 = (bf16[2,256,640]{2,1,0:T(8,128)(2,1)S(1)}, bf16[2,256,640]{2,1,0:T(8,128)(2,1)S(1)}, u32[]{:S(2)}, u32[]{:S(2)}) collective-permute-start(bf16[2,256,640]{2,1,0:T(8,128)(2,1)S(1)} %pad_maximum_fusion.3), channel_id=1, source_target_pairs={{0,4},{1,5},{2,6},{3,7},{4,8},{5,9},{6,10},{7,11},{8,12},{9,13},{1... | collective-permute-start | bytes 1966088 | tf_op jit(solution)/shard_map/ppermute | solution.py:32
  9.8 19.2 %collective-permute-start.25 = (bf16[2,256,640]{2,1,0:T(8,128)(2,1)S(1)}, bf16[2,256,640]{2,1,0:T(8,128)(2,1)S(1)}, u32[]{:S(2)}, u32[]{:S(2)}) collective-permute-start(bf16[2,256,640]{2,1,0:T(8,128)(2,1)S(1)} %pad_maximum_fusion.3), channel_id=1, source_target_pairs={{0,2},{1,3},{2,0},{3,1},{4,6},{5,7},{6,4},{7,5},{8,10},{9,11},{10,... | collective-permute-start | bytes 1966088 | tf_op jit(solution)/shard_map/ppermute | solution.py:37
  11.8 18.1 %collective-permute-start.24 = (bf16[2,256,640]{2,1,0:T(8,128)(2,1)S(1)}, bf16[2,256,640]{2,1,0:T(8,128)(2,1)S(1)}, u32[]{:S(2)}, u32[]{:S(2)}) collective-permute-start(bf16[2,256,640]{2,1,0:T(8,128)(2,1)S(1)} %pad_maximum_fusion.3), channel_id=1, source_target_pairs={{0,1},{1,0},{2,3},{3,2},{4,5},{5,4},{6,7},{7,6},{8,9},{9,8},{10,11... | collective-permute-start | bytes 1966088 | tf_op jit(solution)/shard_map/ppermute | solution.py:37
  12.7 24.5 %collective-permute-start.18 = (bf16[2,256,640]{2,1,0:T(8,128)(2,1)}, bf16[2,256,640]{2,1,0:T(8,128)(2,1)S(1)}, u32[]{:S(2)}, u32[]{:S(2)}) collective-permute-start(bf16[2,256,640]{2,1,0:T(8,128)(2,1)} %pad_maximum_fusion.2), channel_id=1, source_target_pairs={{4,0},{5,1},{6,2},{7,3},{8,4},{9,5},{10,6},{11,7},{12,8},{13,9},{1... | collective-permute-start | bytes 1966088 | tf_op jit(solution)/shard_map/ppermute | solution.py:32
  23.3 18.5 %collective-permute-start.19 = (bf16[2,256,640]{2,1,0:T(8,128)(2,1)}, bf16[2,256,640]{2,1,0:T(8,128)(2,1)S(1)}, u32[]{:S(2)}, u32[]{:S(2)}) collective-permute-start(bf16[2,256,640]{2,1,0:T(8,128)(2,1)} %pad_maximum_fusion.2), channel_id=1, source_target_pairs={{0,4},{1,5},{2,6},{3,7},{4,8},{5,9},{6,10},{7,11},{8,12},{9,13},{1... | collective-permute-start | bytes 1966088 | tf_op jit(solution)/shard_map/ppermute | solution.py:32
  27.3 16.4 %collective-permute-start.17 = (bf16[2,256,640]{2,1,0:T(8,128)(2,1)}, bf16[2,256,640]{2,1,0:T(8,128)(2,1)}, u32[]{:S(2)}, u32[]{:S(2)}) collective-permute-start(bf16[2,256,640]{2,1,0:T(8,128)(2,1)} %pad_maximum_fusion.2), channel_id=1, source_target_pairs={{0,2},{1,3},{2,0},{3,1},{4,6},{5,7},{6,4},{7,5},{8,10},{9,11},{10,... | collective-permute-start | bytes 1966088 | tf_op jit(solution)/shard_map/ppermute | solution.py:37
  28.9 16.8 %collective-permute-start.16 = (bf16[2,256,640]{2,1,0:T(8,128)(2,1)}, bf16[2,256,640]{2,1,0:T(8,128)(2,1)}, u32[]{:S(2)}, u32[]{:S(2)}) collective-permute-start(bf16[2,256,640]{2,1,0:T(8,128)(2,1)} %pad_maximum_fusion.2), channel_id=1, source_target_pairs={{0,1},{1,0},{2,3},{3,2},{4,5},{5,4},{6,7},{7,6},{8,9},{9,8},{10,11... | collective-permute-start | bytes 1966088 | tf_op jit(solution)/shard_map/ppermute | solution.py:37
  30.7 20.0 %collective-permute-start.10 = (bf16[2,256,640]{2,1,0:T(8,128)(2,1)}, bf16[2,256,640]{2,1,0:T(8,128)(2,1)}, u32[]{:S(2)}, u32[]{:S(2)}) collective-permute-start(bf16[2,256,640]{2,1,0:T(8,128)(2,1)} %pad_maximum_fusion.1), channel_id=1, source_target_pairs={{4,0},{5,1},{6,2},{7,3},{8,4},{9,5},{10,6},{11,7},{12,8},{13,9},{1... | collective-permute-start | bytes 1966088 | tf_op jit(solution)/shard_map/ppermute | solution.py:32
  37.2 18.6 %collective-permute-start.11 = (bf16[2,256,640]{2,1,0:T(8,128)(2,1)}, bf16[2,256,640]{2,1,0:T(8,128)(2,1)}, u32[]{:S(2)}, u32[]{:S(2)}) collective-permute-start(bf16[2,256,640]{2,1,0:T(8,128)(2,1)} %pad_maximum_fusion.1), channel_id=1, source_target_pairs={{0,4},{1,5},{2,6},{3,7},{4,8},{5,9},{6,10},{7,11},{8,12},{9,13},{1... | collective-permute-start | bytes 1966088 | tf_op jit(solution)/shard_map/ppermute | solution.py:32
  41.8 16.0 %collective-permute-start.9 = (bf16[2,256,640]{2,1,0:T(8,128)(2,1)}, bf16[2,256,640]{2,1,0:T(8,128)(2,1)}, u32[]{:S(2)}, u32[]{:S(2)}) collective-permute-start(bf16[2,256,640]{2,1,0:T(8,128)(2,1)} %pad_maximum_fusion.1), channel_id=1, source_target_pairs={{0,2},{1,3},{2,0},{3,1},{4,6},{5,7},{6,4},{7,5},{8,10},{9,11},{10,... | collective-permute-start | bytes 1966088 | tf_op jit(solution)/shard_map/ppermute | solution.py:37
  43.7 14.6 %collective-permute-start.8 = (bf16[2,256,640]{2,1,0:T(8,128)(2,1)}, bf16[2,256,640]{2,1,0:T(8,128)(2,1)}, u32[]{:S(2)}, u32[]{:S(2)}) collective-permute-start(bf16[2,256,640]{2,1,0:T(8,128)(2,1)} %pad_maximum_fusion.1), channel_id=1, source_target_pairs={{0,1},{1,0},{2,3},{3,2},{4,5},{5,4},{6,7},{7,6},{8,9},{9,8},{10,11... | collective-permute-start | bytes 1966088 | tf_op jit(solution)/shard_map/ppermute | solution.py:37
  45.7 19.7 %collective-permute-start.2 = (bf16[2,256,640]{2,1,0:T(8,128)(2,1)}, bf16[2,256,640]{2,1,0:T(8,128)(2,1)}, u32[]{:S(2)}, u32[]{:S(2)}) collective-permute-start(bf16[2,256,640]{2,1,0:T(8,128)(2,1)} %pad_maximum_fusion), channel_id=1, source_target_pairs={{4,0},{5,1},{6,2},{7,3},{8,4},{9,5},{10,6},{11,7},{12,8},{13,9},{1... | collective-permute-start | bytes 1966088 | tf_op jit(solution)/shard_map/ppermute | solution.py:32
  50.7 18.0 %collective-permute-start.3 = (bf16[2,256,640]{2,1,0:T(8,128)(2,1)}, bf16[2,256,640]{2,1,0:T(8,128)(2,1)}, u32[]{:S(2)}, u32[]{:S(2)}) collective-permute-start(bf16[2,256,640]{2,1,0:T(8,128)(2,1)} %pad_maximum_fusion), channel_id=1, source_target_pairs={{0,4},{1,5},{2,6},{3,7},{4,8},{5,9},{6,10},{7,11},{8,12},{9,13},{1... | collective-permute-start | bytes 1966088 | tf_op jit(solution)/shard_map/ppermute | solution.py:32
  55.7 18.1 %collective-permute-start.1 = (bf16[2,256,640]{2,1,0:T(8,128)(2,1)}, bf16[2,256,640]{2,1,0:T(8,128)(2,1)}, u32[]{:S(2)}, u32[]{:S(2)}) collective-permute-start(bf16[2,256,640]{2,1,0:T(8,128)(2,1)} %pad_maximum_fusion), channel_id=1, source_target_pairs={{0,2},{1,3},{2,0},{3,1},{4,6},{5,7},{6,4},{7,5},{8,10},{9,11},{10,... | collective-permute-start | bytes 1966088 | tf_op jit(solution)/shard_map/ppermute | solution.py:37
  57.9 30.0 %collective-permute-start.28 = (bf16[2,256,640]{2,1,0:T(8,128)(2,1)}, bf16[2,256,640]{2,1,0:T(8,128)(2,1)}, u32[]{:S(2)}, u32[]{:S(2)}) collective-permute-start(bf16[2,256,640]{2,1,0:T(8,128)(2,1)} %broadcast_select_fusion), channel_id=1, source_target_pairs={{0,2},{1,3},{2,0},{3,1},{4,6},{5,7},{6,4},{7,5},{8,10},{9,11},{10,... | collective-permute-start | bytes 1966088 | tf_op jit(solution)/shard_map/ppermute | solution.py:37
  58.3 30.9 %collective-permute-start.30 = (bf16[2,256,640]{2,1,0:T(8,128)(2,1)S(1)}, bf16[2,256,640]{2,1,0:T(8,128)(2,1)}, u32[]{:S(2)}, u32[]{:S(2)}) collective-permute-start(bf16[2,256,640]{2,1,0:T(8,128)(2,1)S(1)} %collective-permute-done.26.refs_7_), channel_id=1, source_target_pairs={{4,0},{5,1},{6,2},{7,3},{8,4},{9,5},{10,6},{11,7},{12,8},{13,9},{1... | collective-permute-start | bytes 1966088 | tf_op jit(solution)/shard_map/ppermute | solution.py:32
  65.4 36.4 %collective-permute-start.20 = (bf16[2,256,640]{2,1,0:T(8,128)(2,1)S(1)}, bf16[2,256,640]{2,1,0:T(8,128)(2,1)S(1)}, u32[]{:S(2)}, u32[]{:S(2)}) collective-permute-start(bf16[2,256,640]{2,1,0:T(8,128)(2,1)S(1)} %broadcast_select_fusion.1), channel_id=1, source_target_pairs={{0,2},{1,3},{2,0},{3,1},{4,6},{5,7},{6,4},{7,5},{8,10},{9,11},{10,... | collective-permute-start | bytes 1966088 | tf_op jit(solution)/shard_map/ppermute | solution.py:37
  68.8 47.1 %collective-permute-start.12 = (bf16[2,256,640]{2,1,0:T(8,128)(2,1)S(1)}, bf16[2,256,640]{2,1,0:T(8,128)(2,1)S(1)}, u32[]{:S(2)}, u32[]{:S(2)}) collective-permute-start(bf16[2,256,640]{2,1,0:T(8,128)(2,1)S(1)} %broadcast_select_fusion.2), channel_id=1, source_target_pairs={{0,2},{1,3},{2,0},{3,1},{4,6},{5,7},{6,4},{7,5},{8,10},{9,11},{10,... | collective-permute-start | bytes 1966088 | tf_op jit(solution)/shard_map/ppermute | solution.py:37
  73.8 31.2 %collective-permute-start.31 = (bf16[2,256,640]{2,1,0:T(8,128)(2,1)S(1)}, bf16[2,256,640]{2,1,0:T(8,128)(2,1)S(1)}, u32[]{:S(2)}, u32[]{:S(2)}) collective-permute-start(bf16[2,256,640]{2,1,0:T(8,128)(2,1)S(1)} %collective-permute-done.27.refs_8_), channel_id=1, source_target_pairs={{0,4},{1,5},{2,6},{3,7},{4,8},{5,9},{6,10},{7,11},{8,12},{9,13},{1... | collective-permute-start | bytes 1966088 | tf_op jit(solution)/shard_map/ppermute | solution.py:32
  87.9 18.4 %collective-permute-start.22 = (bf16[2,256,640]{2,1,0:T(8,128)(2,1)S(1)}, bf16[2,256,640]{2,1,0:T(8,128)(2,1)S(1)}, u32[]{:S(2)}, u32[]{:S(2)}) collective-permute-start(bf16[2,256,640]{2,1,0:T(8,128)(2,1)S(1)} %collective-permute-done.18.refs_7_), channel_id=1, source_target_pairs={{4,0},{5,1},{6,2},{7,3},{8,4},{9,5},{10,6},{11,7},{12,8},{13,9},{1... | collective-permute-start | bytes 1966088 | tf_op jit(solution)/shard_map/ppermute | solution.py:32
  89.2 21.7 %collective-permute-start.23 = (bf16[2,256,640]{2,1,0:T(8,128)(2,1)S(1)}, bf16[2,256,640]{2,1,0:T(8,128)(2,1)S(1)}, u32[]{:S(2)}, u32[]{:S(2)}) collective-permute-start(bf16[2,256,640]{2,1,0:T(8,128)(2,1)S(1)} %collective-permute-done.19.refs_8_), channel_id=1, source_target_pairs={{0,4},{1,5},{2,6},{3,7},{4,8},{5,9},{6,10},{7,11},{8,12},{9,13},{1... | collective-permute-start | bytes 1966088 | tf_op jit(solution)/shard_map/ppermute | solution.py:32
  101.8 25.4 %collective-permute-start.4 = (bf16[2,256,640]{2,1,0:T(8,128)(2,1)S(1)}, bf16[2,256,640]{2,1,0:T(8,128)(2,1)S(1)}, u32[]{:S(2)}, u32[]{:S(2)}) collective-permute-start(bf16[2,256,640]{2,1,0:T(8,128)(2,1)S(1)} %broadcast_select_fusion.3), channel_id=1, source_target_pairs={{0,2},{1,3},{2,0},{3,1},{4,6},{5,7},{6,4},{7,5},{8,10},{9,11},{10,... | collective-permute-start | bytes 1966088 | tf_op jit(solution)/shard_map/ppermute | solution.py:37
  105.0 23.4 %collective-permute-start.14 = (bf16[2,256,640]{2,1,0:T(8,128)(2,1)}, bf16[2,256,640]{2,1,0:T(8,128)(2,1)S(1)}, u32[]{:S(2)}, u32[]{:S(2)}) collective-permute-start(bf16[2,256,640]{2,1,0:T(8,128)(2,1)} %collective-permute-done.10.refs_7_), channel_id=1, source_target_pairs={{4,0},{5,1},{6,2},{7,3},{8,4},{9,5},{10,6},{11,7},{12,8},{13,9},{1... | collective-permute-start | bytes 1966088 | tf_op jit(solution)/shard_map/ppermute | solution.py:32
  106.3 22.2 %collective-permute-start.15 = (bf16[2,256,640]{2,1,0:T(8,128)(2,1)}, bf16[2,256,640]{2,1,0:T(8,128)(2,1)S(1)}, u32[]{:S(2)}, u32[]{:S(2)}) collective-permute-start(bf16[2,256,640]{2,1,0:T(8,128)(2,1)} %collective-permute-done.11.refs_8_), channel_id=1, source_target_pairs={{0,4},{1,5},{2,6},{3,7},{4,8},{5,9},{6,10},{7,11},{8,12},{9,13},{1... | collective-permute-start | bytes 1966088 | tf_op jit(solution)/shard_map/ppermute | solution.py:32
  110.9 18.9 %collective-permute-start.29 = (bf16[2,256,640]{2,1,0:T(8,128)(2,1)S(1)}, bf16[2,256,640]{2,1,0:T(8,128)(2,1)S(1)}, u32[]{:S(2)}, u32[]{:S(2)}) collective-permute-start(bf16[2,256,640]{2,1,0:T(8,128)(2,1)S(1)} %broadcast_select_fusion.4), channel_id=1, source_target_pairs={{0,1},{1,0},{2,3},{3,2},{4,5},{5,4},{6,7},{7,6},{8,9},{9,8},{10,11... | collective-permute-start | bytes 1966088 | tf_op jit(solution)/shard_map/ppermute | solution.py:37
  115.9 18.7 %collective-permute-start.21 = (bf16[2,256,640]{2,1,0:T(8,128)(2,1)S(1)}, bf16[2,256,640]{2,1,0:T(8,128)(2,1)S(1)}, u32[]{:S(2)}, u32[]{:S(2)}) collective-permute-start(bf16[2,256,640]{2,1,0:T(8,128)(2,1)S(1)} %broadcast_select_fusion.5), channel_id=1, source_target_pairs={{0,1},{1,0},{2,3},{3,2},{4,5},{5,4},{6,7},{7,6},{8,9},{9,8},{10,11... | collective-permute-start | bytes 1966088 | tf_op jit(solution)/shard_map/ppermute | solution.py:37
  127.2 22.6 %collective-permute-start.13 = (bf16[2,256,640]{2,1,0:T(8,128)(2,1)S(1)}, bf16[2,256,640]{2,1,0:T(8,128)(2,1)S(1)}, u32[]{:S(2)}, u32[]{:S(2)}) collective-permute-start(bf16[2,256,640]{2,1,0:T(8,128)(2,1)S(1)} %broadcast_select_fusion.6), channel_id=1, source_target_pairs={{0,1},{1,0},{2,3},{3,2},{4,5},{5,4},{6,7},{7,6},{8,9},{9,8},{10,11... | collective-permute-start | bytes 1966088 | tf_op jit(solution)/shard_map/ppermute | solution.py:37
  128.4 28.4 %collective-permute-start = (bf16[2,256,640]{2,1,0:T(8,128)(2,1)}, bf16[2,256,640]{2,1,0:T(8,128)(2,1)S(1)}, u32[]{:S(2)}, u32[]{:S(2)}) collective-permute-start(bf16[2,256,640]{2,1,0:T(8,128)(2,1)} %pad_maximum_fusion), channel_id=1, source_target_pairs={{0,1},{1,0},{2,3},{3,2},{4,5},{5,4},{6,7},{7,6},{8,9},{9,8},{10,11... | collective-permute-start | bytes 1966088 | tf_op jit(solution)/shard_map/ppermute | solution.py:37
  128.5 28.3 %collective-permute-start.6 = (bf16[2,256,640]{2,1,0:T(8,128)(2,1)}, bf16[2,256,640]{2,1,0:T(8,128)(2,1)S(1)}, u32[]{:S(2)}, u32[]{:S(2)}) collective-permute-start(bf16[2,256,640]{2,1,0:T(8,128)(2,1)} %collective-permute-done.2.refs_7_), channel_id=1, source_target_pairs={{4,0},{5,1},{6,2},{7,3},{8,4},{9,5},{10,6},{11,7},{12,8},{13,9},{1... | collective-permute-start | bytes 1966088 | tf_op jit(solution)/shard_map/ppermute | solution.py:32
  129.8 27.0 %collective-permute-start.7 = (bf16[2,256,640]{2,1,0:T(8,128)(2,1)}, bf16[2,256,640]{2,1,0:T(8,128)(2,1)S(1)}, u32[]{:S(2)}, u32[]{:S(2)}) collective-permute-start(bf16[2,256,640]{2,1,0:T(8,128)(2,1)} %collective-permute-done.3.refs_8_), channel_id=1, source_target_pairs={{0,4},{1,5},{2,6},{3,7},{4,8},{5,9},{6,10},{7,11},{8,12},{9,13},{1... | collective-permute-start | bytes 1966088 | tf_op jit(solution)/shard_map/ppermute | solution.py:32
  134.6 22.3 %collective-permute-start.5 = (bf16[2,256,640]{2,1,0:T(8,128)(2,1)S(1)}, bf16[2,256,640]{2,1,0:T(8,128)(2,1)S(1)}, u32[]{:S(2)}, u32[]{:S(2)}) collective-permute-start(bf16[2,256,640]{2,1,0:T(8,128)(2,1)S(1)} %broadcast_select_fusion.7), channel_id=1, source_target_pairs={{0,1},{1,0},{2,3},{3,2},{4,5},{5,4},{6,7},{7,6},{8,9},{9,8},{10,11... | collective-permute-start | bytes 1966088 | tf_op jit(solution)/shard_map/ppermute | solution.py:37
  (6 other events, 95.6 us)

commit v2 on v1

v2 whole, which is shorter than its diff:
```python
import functools
import math

import jax
import jax.numpy as jnp
from jax import lax
from jax.experimental import pallas as pl
from jax.experimental.pallas import tpu as pltpu
from jax.sharding import PartitionSpec as P

DH = 128
BLOCK = 128
VALUE_SPLIT = (20,)
VMEM = 18 * 1024 * 1024


def permuted(value, target):
    count = lax.axis_size("blk")
    pairs = [(i, target(i)) for i in range(count)]
    return lax.ppermute(value, "blk", [(i, t) for i, t in pairs if t is not None and 0 <= t < count])


def swapped(value, bit):
    return permuted(value, lambda i: i ^ bit)


def swapped_odd(value):
    return permuted(value, lambda i: i + 4 if i & 4 else i - 4)


def far_even(value):
    count = lax.axis_size("blk")
    return permuted(value, lambda i: i ^ 4 if 0 <= (i + 4 if i & 4 else i - 4) < count else None)


def far_side(value):
    count = lax.axis_size("blk")
    return permuted(value, lambda i: i ^ 2 if 0 <= (i - 4 if i & 2 else i + 4) < count else None)


def after(value, *earlier):
    return lax.optimization_barrier((value, *earlier))[0]


def slots_of(place, kept, block, local_blocks, keep):
    position = place[0]
    bits = [position % 2, (position // 2) % 2, (position // 4) % 2]
    found = []
    for entry in range(keep):
        listed = kept[block, entry]
        offset = listed // local_blocks - position
        ahead = (offset > 0).astype(jnp.int32)
        near = jnp.abs(offset)
        step = sum((near >= reach).astype(jnp.int32) for reach in (1, 2, 4, 8))
        flip = jnp.where(step == 1, bits[0], jnp.where(step == 2, bits[1], bits[2]))
        slot = jnp.where(step == 0, 0, 2 * step - (ahead + flip) % 2)
        found.append((slot, pl.multiple_of((listed % local_blocks) * BLOCK, BLOCK)))
    return found


def score_kernel(local_blocks, keep, place, kept, queries, *refs):
    tiles, (weights, totals), staged = refs[:9], refs[9:11], refs[11]
    scale = math.log2(math.e) / math.sqrt(DH)
    found = [slots_of(place, kept, block, local_blocks, keep) for block in range(local_blocks)]

    def one_head(head, carry):
        lanes = pl.ds(pl.multiple_of(head * DH, DH), DH)
        for index, tile in enumerate(tiles):
            staged[index] = tile[:, lanes]
        for block in range(local_blocks):
            rows = pl.ds(block * BLOCK, BLOCK)
            keys = jnp.concatenate(
                [staged[slot, pl.ds(row, BLOCK), :] for slot, row in found[block]], axis=0
            )
            scores = lax.dot_general(
                queries[rows, lanes],
                keys,
                (((1,), (1,)), ((), ())),
                preferred_element_type=jnp.float32,
            )
            top = jnp.max(scores, axis=1, keepdims=True)
            weight = jnp.exp2((scores - top) * scale)
            total = jnp.sum(weight, axis=1, keepdims=True)
            weights[head, rows, :] = weight.astype(jnp.bfloat16)
            totals[head, rows, :] = jnp.broadcast_to(total, (BLOCK, DH))
        return carry

    lax.fori_loop(0, queries.shape[1] // DH, one_head, 0, unroll=2)


def value_kernel(first, count, local_blocks, keep, place, kept, weights, totals, *refs):
    tiles, attended, staged = refs[:9], refs[9], refs[10]
    found = [slots_of(place, kept, block, local_blocks, keep) for block in range(local_blocks)]

    def one_head(head, carry):
        part = pl.ds(pl.multiple_of(head * DH, DH), DH)
        whole = pl.ds(pl.multiple_of((first + head) * DH, DH), DH)
        for index, tile in enumerate(tiles):
            staged[index] = tile[:, part if tile.shape[1] == count * DH else whole]
        for block in range(local_blocks):
            rows = pl.ds(block * BLOCK, BLOCK)
            values = jnp.concatenate(
                [staged[slot, pl.ds(row, BLOCK), :] for slot, row in found[block]], axis=0
            )
            numerator = jnp.dot(
                weights[first + head, rows, :], values, preferred_element_type=jnp.float32
            )
            attended[rows, part] = (numerator / totals[first + head, rows, :]).astype(jnp.bfloat16)
        return carry

    lax.fori_loop(0, count, one_head, 0, unroll=2)


def in_vmem(arrays):
    return [pltpu.with_memory_space_constraint(array, pltpu.VMEM) for array in arrays]


def weigh(place, kept, queries, tiles):
    rows, columns = queries.shape
    heads = columns // DH
    local_blocks, keep = kept.shape
    scalars = pl.BlockSpec(memory_space=pltpu.SMEM)
    held = pl.BlockSpec(memory_space=pltpu.VMEM)
    pairs = local_blocks * keep * heads
    return pl.pallas_call(
        functools.partial(score_kernel, local_blocks, keep),
        out_shape=(
            pltpu.VMEM((heads, rows, keep * BLOCK), jnp.bfloat16),
            pltpu.VMEM((heads, rows, DH), jnp.float32),
        ),
        in_specs=[scalars, scalars] + [held] * (1 + len(tiles)),
        out_specs=(held, held),
        scratch_shapes=[pltpu.VMEM((len(tiles), rows, DH), jnp.bfloat16)],
        compiler_params=pltpu.CompilerParams(vmem_limit_bytes=VMEM),
        cost_estimate=pl.CostEstimate(
            flops=2 * pairs * BLOCK * BLOCK * DH,
            bytes_accessed=(len(tiles) + 1) * rows * columns * 2 + heads * rows * keep * BLOCK * 2,
            transcendentals=pairs * BLOCK * BLOCK,
        ),
        name="weigh",
    )(place, kept, *in_vmem((queries, *tiles)))


def combine(first, count, place, kept, weights, totals, tiles):
    heads, rows, _ = weights.shape
    local_blocks, keep = kept.shape
    scalars = pl.BlockSpec(memory_space=pltpu.SMEM)
    held = pl.BlockSpec(memory_space=pltpu.VMEM)
    return pl.pallas_call(
        functools.partial(value_kernel, first, count, local_blocks, keep),
        out_shape=jax.ShapeDtypeStruct((rows, count * DH), jnp.bfloat16),
        in_specs=[scalars, scalars] + [held] * (2 + len(tiles)),
        out_specs=held,
        scratch_shapes=[pltpu.VMEM((len(tiles), rows, DH), jnp.bfloat16)],
        compiler_params=pltpu.CompilerParams(vmem_limit_bytes=VMEM),
        cost_estimate=pl.CostEstimate(
            flops=2 * local_blocks * keep * count * BLOCK * BLOCK * DH,
            bytes_accessed=len(tiles) * rows * count * DH * 2 + count * rows * keep * BLOCK * 2,
            transcendentals=0,
        ),
        name=f"combine_{first}",
    )(place, kept, *in_vmem((weights, totals, *tiles)))


def per_device(queries, keys, values, kept_blocks):
    position = lax.axis_index("blk").astype(jnp.int32)
    place = position.reshape(1)
    core_bit, side_bit, level_bit = (position % 2, (position // 2) % 2, (position // 4) % 2)
    same_side, same_core = side_bit == level_bit, core_bit == side_bit
    heads = queries.shape[1] // DH

    k_side, k_odd, k_even = swapped(keys, 2), swapped_odd(keys), swapped(keys, 4)
    v_side, v_odd, v_even = swapped(after(values, k_side), 2), swapped_odd(values), swapped(values, 4)
    k_mix = jnp.where(same_side, k_even, k_odd)
    k_odd_far, k_even_far = swapped_odd(k_even), far_even(k_odd)
    k_side_far = far_side(after(k_mix, v_side))
    v_mix = jnp.where(same_side, after(v_even, v_side), after(v_odd, v_side))
    k_core = swapped(after(keys, v_odd, v_even, v_mix), 1)
    v_core = swapped(after(values, v_odd, v_even, v_mix), 1)
    v_odd_far = swapped_odd(after(v_even, v_side))
    v_even_far = far_even(after(v_odd, v_side))
    v_side_far = far_side(after(v_mix, k_side_far))
    k_core_far = swapped(after(jnp.where(same_core, k_side, k_side_far), k_core, v_core, k_odd_far, k_even_far), 1)

    tiles = (keys, k_core, k_core_far, k_side, k_side_far, k_even, k_odd, k_even_far, k_odd_far)
    weights, totals = weigh(place, kept_blocks, queries, tiles)

    v_side_done = after(v_side_far, totals)
    v_core_far = swapped(jnp.where(same_core, v_side, v_side_done), 1)
    tiles = (
        values, v_core, v_core_far, v_side, v_side_done, v_even, v_odd, v_even_far, v_odd_far
    )
    return combine(0, heads, place, kept_blocks, weights, totals, tiles)


def solution(mesh):
    placed = P(("clip", "blk"), None)
    return jax.shard_map(
        per_device, mesh=mesh, in_specs=(placed,) * 4, out_specs=placed, check_vma=False
    )
```

time: 165 us -> 142 us (0.86)
  starting transfers between devices: 59.7 us -> 27.7 us
  waiting for transfers between devices: 60.1 us -> 84.8 us
  other arithmetic: 11 us -> 5.41 us
  Pallas kernels: 28.1 us -> 22.9 us
  local copies, waits for them, and re-layouts: 4.79 us -> 0.01 us
    ppermute x32 -> x16, starting transfers between devices: 59.7 us -> 27.7 us  [permuted(): lax.ppermute(value, 'blk', [(i, t) for i, t in pairs if t is not None and...]
    ppermute x32 -> x16, waiting for transfers between devices: 60.1 us -> 84.8 us  [permuted(): lax.ppermute(value, 'blk', [(i, t) for i, t in pairs if t is not None and...]
    pallas_call x4 -> x2, Pallas kernels: 28.1 us -> 22.9 us  [the longest x1 13.1 us: weigh(): pl.pallas_call(functools.partial(score_kernel, local_blocks, keep), out_s...]
    another operation x4 -> x0, other arithmetic: 3.91 us -> none  [per_device(): own.append(jnp.stack((keys[:, lanes], values[:, lanes])))]
    another operation x1 -> x0, local copies, waits for them, and re-layouts: 2.78 us -> none  [per_device(): own.append(jnp.stack((keys[:, lanes], values[:, lanes])))]
    select_n x8 -> x4, other arithmetic: 7.04 us -> 5.41 us  [the longest x1 2.51 us: per_device(): k_mix = jnp.where(same_side, k_even, k_odd)]
  transfers between devices with their start and end apart: 32 -> 16, of which waited for: 9 -> 5; matrix products, arithmetic and copies ran while one was open for 7% -> 4% of each run, Pallas kernels for 13% -> 9%
where the time goes in v2:
time: 142 us; the launch traced here: 141 us
  waiting for transfers between devices  84.8 us (60%)
  starting transfers between devices  27.7 us (20%)
  Pallas kernels  22.9 us (16%)
  other arithmetic  5.41 us (4%)
    ppermute x16, waiting for transfers between devices, permuted(): lax.ppermute(value, 'blk', [(i, t) for i, t in pairs if t is not None and...  84.8 us
    ppermute x16, starting transfers between devices, permuted(): lax.ppermute(value, 'blk', [(i, t) for i, t in pairs if t is not None and...  27.7 us
    pallas_call x1, Pallas kernels, weigh(): pl.pallas_call(functools.partial(score_kernel, local_blocks, keep), out_s...  13.1 us
    pallas_call x1, Pallas kernels, combine(): pl.pallas_call(functools.partial(value_kernel, first, count, local_blocks...  9.78 us
  transfers between devices with their start and end apart: 16, of which 5 were waited for; matrix products, arithmetic and copies ran while one was open for 4% of the time, Pallas kernels for 9%

profile of v2, /device:TPU:0, one launch (start us, length us, event | category | flops | bytes accessed | tf_op | source)
XLA Modules:
  0.0 140.9 jit_solution(15232507486242216984)
XLA Ops:
  0.0 3.0 %collective-permute-start.2 = (bf16[256,2560]{1,0:T(8,128)(2,1)}, bf16[256,2560]{1,0:T(8,128)(2,1)}, u32[]{:S(2)}, u32[]{:S(2)}) collective-permute-start(bf16[256,2560]{1,0:T(8,128)(2,1)} %refs_0_.2), channel_id=1, source_target_pairs={{0,2},{1,3},{2,0},{3,1},{4,6},{5,7},{6,4},{7,5},{8,10},{9,11},{10,... | collective-permute-start | bytes 3932168 | tf_op jit(solution)/shard_map/ppermute | solution.py:20
  3.0 1.7 %collective-permute-start.6 = (bf16[256,2560]{1,0:T(8,128)(2,1)}, bf16[256,2560]{1,0:T(8,128)(2,1)}, u32[]{:S(2)}, u32[]{:S(2)}) collective-permute-start(bf16[256,2560]{1,0:T(8,128)(2,1)} %refs_0_.2), channel_id=1, source_target_pairs={{4,8},{5,9},{6,10},{7,11},{8,4},{9,5},{10,6},{11,7},{20,24},{21,25... | collective-permute-start | bytes 3932168 | tf_op jit(solution)/shard_map/ppermute | solution.py:20
  4.7 3.4 %collective-permute-start.5 = (bf16[256,2560]{1,0:T(8,128)(2,1)}, bf16[256,2560]{1,0:T(8,128)(2,1)}, u32[]{:S(2)}, u32[]{:S(2)}) collective-permute-start(bf16[256,2560]{1,0:T(8,128)(2,1)} %refs_0_.2), channel_id=1, source_target_pairs={{0,4},{1,5},{2,6},{3,7},{4,0},{5,1},{6,2},{7,3},{8,12},{9,13},{10,... | collective-permute-start | bytes 3932168 | tf_op jit(solution)/shard_map/ppermute | solution.py:20
  8.1 24.0 %collective-permute-done.2.refs_3_ = bf16[256,2560]{1,0:T(8,128)(2,1)} collective-permute-done((bf16[256,2560]{1,0:T(8,128)(2,1)}, bf16[256,2560]{1,0:T(8,128)(2,1)}, u32[]{:S(2)}, u32[]{:S(2)}) %collective-permute-start.2) | collective-permute-done | bytes 1310752 | tf_op jit(solution)/shard_map/ppermute | solution.py:20
  32.1 1.7 %collective-permute-start.3 = (bf16[256,2560]{1,0:T(8,128)(2,1)}, bf16[256,2560]{1,0:T(8,128)(2,1)S(1)}, u32[]{:S(2)}, u32[]{:S(2)}) collective-permute-start(bf16[256,2560]{1,0:T(8,128)(2,1)} %refs_0_.3), channel_id=1, source_target_pairs={{0,2},{1,3},{2,0},{3,1},{4,6},{5,7},{6,4},{7,5},{8,10},{9,11},{10,... | collective-permute-start | bytes 3932168 | tf_op jit(solution)/shard_map/ppermute | solution.py:20
  33.8 1.6 %collective-permute-start.1 = (bf16[256,2560]{1,0:T(8,128)(2,1)}, bf16[256,2560]{1,0:T(8,128)(2,1)S(1)}, u32[]{:S(2)}, u32[]{:S(2)}) collective-permute-start(bf16[256,2560]{1,0:T(8,128)(2,1)} %refs_0_.3), channel_id=1, source_target_pairs={{0,4},{1,5},{2,6},{3,7},{4,0},{5,1},{6,2},{7,3},{8,12},{9,13},{10,... | collective-permute-start | bytes 3932168 | tf_op jit(solution)/shard_map/ppermute | solution.py:20
  35.4 1.7 %collective-permute-start = (bf16[256,2560]{1,0:T(8,128)(2,1)}, bf16[256,2560]{1,0:T(8,128)(2,1)}, u32[]{:S(2)}, u32[]{:S(2)}) collective-permute-start(bf16[256,2560]{1,0:T(8,128)(2,1)} %refs_0_.3), channel_id=1, source_target_pairs={{4,8},{5,9},{6,10},{7,11},{8,4},{9,5},{10,6},{11,7},{20,24},{21,25... | collective-permute-start | bytes 3932168 | tf_op jit(solution)/shard_map/ppermute | solution.py:20
  37.1 0.0 collective-permute-done.6.refs_6_
  37.1 1.3 collective-permute-start.10
  38.4 0.0 collective-permute-done.5.refs_5_
  38.4 1.7 %collective-permute-start.9 = (bf16[256,2560]{1,0:T(8,128)(2,1)}, bf16[256,2560]{1,0:T(8,128)(2,1)}, u32[]{:S(2)}, u32[]{:S(2)}) collective-permute-start(bf16[256,2560]{1,0:T(8,128)(2,1)} %collective-permute-done.5.refs_5_), channel_id=1, source_target_pairs={{4,8},{5,9},{6,10},{7,11},{8,4},{9,5},{10,6},{11,7},{20,24},{21,25... | collective-permute-start | bytes 3932168 | tf_op jit(solution)/shard_map/ppermute | solution.py:20
  40.2 2.5 %broadcast_select_fusion.2 = bf16[256,2560]{1,0:T(8,128)(2,1)} fusion(bf16[256,2560]{1,0:T(8,128)(2,1)} %collective-permute-done.5.refs_5_, bf16[256,2560]{1,0:T(8,128)(2,1)} %collective-permute-done.6.refs_6_, pred[]{:T(512)S(6)} %eq.10), kind=kLoop, calls=%fused_computation.2 | loop fusion | flops 655360 | bytes 3932161 | tf_op jit(solution)/shard_map/jit(_where)/select_n | solution.py:174
  42.7 19.6 %collective-permute-done.3.refs_3_ = bf16[256,2560]{1,0:T(8,128)(2,1)S(1)} collective-permute-done((bf16[256,2560]{1,0:T(8,128)(2,1)}, bf16[256,2560]{1,0:T(8,128)(2,1)S(1)}, u32[]{:S(2)}, u32[]{:S(2)}) %collective-permute-start.3) | collective-permute-done | bytes 1310752 | tf_op jit(solution)/shard_map/ppermute | solution.py:20
  62.2 4.4 %collective-permute-start.7 = (bf16[256,2560]{1,0:T(8,128)(2,1)}, bf16[256,2560]{1,0:T(8,128)(2,1)}, u32[]{:S(2)}, u32[]{:S(2)}) collective-permute-start(bf16[256,2560]{1,0:T(8,128)(2,1)} %broadcast_select_fusion.2), channel_id=1, source_target_pairs={{0,2},{1,3},{4,6},{5,7},{6,4},{7,5},{8,10},{9,11},{10,8},{11,9},{1... | collective-permute-start | bytes 3932168 | tf_op jit(solution)/shard_map/ppermute | solution.py:20
  66.6 1.3 broadcast_select_fusion.3
  67.9 0.0 collective-permute-start.8
  67.9 0.5 collective-permute-start.4
  68.4 23.7 %collective-permute-done.7.refs_4_ = bf16[256,2560]{1,0:T(8,128)(2,1)} collective-permute-done((bf16[256,2560]{1,0:T(8,128)(2,1)}, bf16[256,2560]{1,0:T(8,128)(2,1)}, u32[]{:S(2)}, u32[]{:S(2)}) %collective-permute-start.7) | collective-permute-done | bytes 1310752 | tf_op jit(solution)/shard_map/ppermute | solution.py:20
  92.1 1.5 %broadcast_select_fusion.1 = bf16[256,2560]{1,0:T(8,128)(2,1)S(1)} fusion(bf16[256,2560]{1,0:T(8,128)(2,1)} %collective-permute-done.2.refs_3_, bf16[256,2560]{1,0:T(8,128)(2,1)} %collective-permute-done.7.refs_4_, pred[]{:T(512)S(6)} %eq.11), kind=kLoop, calls=%fused_computation.1 | loop fusion | flops 655360 | bytes 3932161 | tf_op jit(solution)/shard_map/jit(_where)/select_n | solution.py:183
  93.6 0.0 collective-permute-done.9.refs_8_
  93.6 0.0 collective-permute-done.8.refs_1_
  93.6 0.1 collective-permute-start.11
  93.7 4.5 %collective-permute-start.12 = (bf16[256,2560]{1,0:T(8,128)(2,1)S(1)}, bf16[256,2560]{1,0:T(8,128)(2,1)S(1)}, u32[]{:S(2)}, u32[]{:S(2)}) collective-permute-start(bf16[256,2560]{1,0:T(8,128)(2,1)S(1)} %copy-done.2), channel_id=1, source_target_pairs={{0,2},{1,3},{4,6},{5,7},{6,4},{7,5},{8,10},{9,11},{10,8},{11,9},{1... | collective-permute-start | bytes 3932168 | tf_op jit(solution)/shard_map/ppermute | solution.py:20
  98.2 1.3 collective-permute-start.14
  99.5 0.7 collective-permute-start.15
  100.2 13.1 %weigh.1 = (bf16[20,256,1024]{2,1,0:T(8,128)(2,1)S(1)}, f32[20,256,128]{2,1,0:T(8,128)S(1)}) custom-call(s32[1]{0:T(128)} %bitcast.place, s32[2,8]{1,0:T(2,128)S(1)} %copy-done.1, bf16[256,2560]{1,0:T(8,128)(2,1)S(1)} %copy-done, bf16[256,2560]{1,0:T(8,128)(2,1)} %refs_0_.2, bf16[256,2560]{1,0:T(8,128)(2,1)} %collective-permute-done.4.refs_1_, ...), custom_call_target="tpu_custom_call" | custom-call | flops 1342177280 | bytes 23592960 | tf_op jit(solution)/shard_map/weigh/pallas_call | solution.py:125
  113.3 13.4 %collective-permute-done.12.refs_4_ = bf16[256,2560]{1,0:T(8,128)(2,1)S(1)} collective-permute-done((bf16[256,2560]{1,0:T(8,128)(2,1)S(1)}, bf16[256,2560]{1,0:T(8,128)(2,1)S(1)}, u32[]{:S(2)}, u32[]{:S(2)}) %collective-permute-start.12) | collective-permute-done | bytes 1310752 | tf_op jit(solution)/shard_map/ppermute | solution.py:20
  126.7 0.2 broadcast_select_fusion
  126.9 0.1 collective-permute-start.13
  127.0 4.2 %collective-permute-done.14.refs_7_ = bf16[256,2560]{1,0:T(8,128)(2,1)S(1)} collective-permute-done((bf16[256,2560]{1,0:T(8,128)(2,1)}, bf16[256,2560]{1,0:T(8,128)(2,1)S(1)}, u32[]{:S(2)}, u32[]{:S(2)}) %collective-permute-start.14) | collective-permute-done | bytes 1310752 | tf_op jit(solution)/shard_map/ppermute | solution.py:20
  131.1 0.0 collective-permute-done.15.refs_8_
  131.2 9.8 %combine_0.1 = bf16[256,2560]{1,0:T(8,128)(2,1)} custom-call(s32[1]{0:T(128)} %bitcast.place, s32[2,8]{1,0:T(2,128)S(1)} %copy-done.1, bf16[20,256,1024]{2,1,0:T(8,128)(2,1)S(1)} %get-tuple-element.23.weights, f32[20,256,128]{2,1,0:T(8,128)S(1)} %get-tuple-element.24.totals, bf16[256,2560]{1,0:T(8,128)(2,1)} %refs_0_.3, ...), custom_call_target="tpu_custom_call" | custom-call | flops 1342177280 | bytes 22282240 | tf_op jit(solution)/shard_map/combine_0/pallas_call | solution.py:149
  (12 shorter events, 0.0 us)
Async XLA Ops:
  0.0 32.1 %collective-permute-start.2 = (bf16[256,2560]{1,0:T(8,128)(2,1)}, bf16[256,2560]{1,0:T(8,128)(2,1)}, u32[]{:S(2)}, u32[]{:S(2)}) collective-permute-start(bf16[256,2560]{1,0:T(8,128)(2,1)} %refs_0_.2), channel_id=1, source_target_pairs={{0,2},{1,3},{2,0},{3,1},{4,6},{5,7},{6,4},{7,5},{8,10},{9,11},{10,... | collective-permute-start | bytes 3932168 | tf_op jit(solution)/shard_map/ppermute | solution.py:20
  3.0 34.2 %collective-permute-start.6 = (bf16[256,2560]{1,0:T(8,128)(2,1)}, bf16[256,2560]{1,0:T(8,128)(2,1)}, u32[]{:S(2)}, u32[]{:S(2)}) collective-permute-start(bf16[256,2560]{1,0:T(8,128)(2,1)} %refs_0_.2), channel_id=1, source_target_pairs={{4,8},{5,9},{6,10},{7,11},{8,4},{9,5},{10,6},{11,7},{20,24},{21,25... | collective-permute-start | bytes 3932168 | tf_op jit(solution)/shard_map/ppermute | solution.py:20
  4.7 33.7 %collective-permute-start.5 = (bf16[256,2560]{1,0:T(8,128)(2,1)}, bf16[256,2560]{1,0:T(8,128)(2,1)}, u32[]{:S(2)}, u32[]{:S(2)}) collective-permute-start(bf16[256,2560]{1,0:T(8,128)(2,1)} %refs_0_.2), channel_id=1, source_target_pairs={{0,4},{1,5},{2,6},{3,7},{4,0},{5,1},{6,2},{7,3},{8,12},{9,13},{10,... | collective-permute-start | bytes 3932168 | tf_op jit(solution)/shard_map/ppermute | solution.py:20
  32.1 30.2 %collective-permute-start.3 = (bf16[256,2560]{1,0:T(8,128)(2,1)}, bf16[256,2560]{1,0:T(8,128)(2,1)S(1)}, u32[]{:S(2)}, u32[]{:S(2)}) collective-permute-start(bf16[256,2560]{1,0:T(8,128)(2,1)} %refs_0_.3), channel_id=1, source_target_pairs={{0,2},{1,3},{2,0},{3,1},{4,6},{5,7},{6,4},{7,5},{8,10},{9,11},{10,... | collective-permute-start | bytes 3932168 | tf_op jit(solution)/shard_map/ppermute | solution.py:20
  33.8 32.8 %collective-permute-start.1 = (bf16[256,2560]{1,0:T(8,128)(2,1)}, bf16[256,2560]{1,0:T(8,128)(2,1)S(1)}, u32[]{:S(2)}, u32[]{:S(2)}) collective-permute-start(bf16[256,2560]{1,0:T(8,128)(2,1)} %refs_0_.3), channel_id=1, source_target_pairs={{0,4},{1,5},{2,6},{3,7},{4,0},{5,1},{6,2},{7,3},{8,12},{9,13},{10,... | collective-permute-start | bytes 3932168 | tf_op jit(solution)/shard_map/ppermute | solution.py:20
  35.4 31.3 %collective-permute-start = (bf16[256,2560]{1,0:T(8,128)(2,1)}, bf16[256,2560]{1,0:T(8,128)(2,1)}, u32[]{:S(2)}, u32[]{:S(2)}) collective-permute-start(bf16[256,2560]{1,0:T(8,128)(2,1)} %refs_0_.3), channel_id=1, source_target_pairs={{4,8},{5,9},{6,10},{7,11},{8,4},{9,5},{10,6},{11,7},{20,24},{21,25... | collective-permute-start | bytes 3932168 | tf_op jit(solution)/shard_map/ppermute | solution.py:20
  37.1 56.4 %collective-permute-start.10 = (bf16[256,2560]{1,0:T(8,128)(2,1)}, bf16[256,2560]{1,0:T(8,128)(2,1)}, u32[]{:S(2)}, u32[]{:S(2)}) collective-permute-start(bf16[256,2560]{1,0:T(8,128)(2,1)} %collective-permute-done.6.refs_6_), channel_id=1, source_target_pairs={{4,0},{5,1},{6,2},{7,3},{8,12},{9,13},{10,14},{11,15},{20,16},{21,... | collective-permute-start | bytes 3932168 | tf_op jit(solution)/shard_map/ppermute | solution.py:20
  38.4 55.1 %collective-permute-start.9 = (bf16[256,2560]{1,0:T(8,128)(2,1)}, bf16[256,2560]{1,0:T(8,128)(2,1)}, u32[]{:S(2)}, u32[]{:S(2)}) collective-permute-start(bf16[256,2560]{1,0:T(8,128)(2,1)} %collective-permute-done.5.refs_5_), channel_id=1, source_target_pairs={{4,8},{5,9},{6,10},{7,11},{8,4},{9,5},{10,6},{11,7},{20,24},{21,25... | collective-permute-start | bytes 3932168 | tf_op jit(solution)/shard_map/ppermute | solution.py:20
  62.2 29.9 %collective-permute-start.7 = (bf16[256,2560]{1,0:T(8,128)(2,1)}, bf16[256,2560]{1,0:T(8,128)(2,1)}, u32[]{:S(2)}, u32[]{:S(2)}) collective-permute-start(bf16[256,2560]{1,0:T(8,128)(2,1)} %broadcast_select_fusion.2), channel_id=1, source_target_pairs={{0,2},{1,3},{4,6},{5,7},{6,4},{7,5},{8,10},{9,11},{10,8},{11,9},{1... | collective-permute-start | bytes 3932168 | tf_op jit(solution)/shard_map/ppermute | solution.py:20
  67.9 25.7 %collective-permute-start.8 = (bf16[256,2560]{1,0:T(8,128)(2,1)}, bf16[256,2560]{1,0:T(8,128)(2,1)}, u32[]{:S(2)}, u32[]{:S(2)}) collective-permute-start(bf16[256,2560]{1,0:T(8,128)(2,1)} %refs_0_.3), channel_id=1, source_target_pairs={{0,1},{1,0},{2,3},{3,2},{4,5},{5,4},{6,7},{7,6},{8,9},{9,8},{10,11... | collective-permute-start | bytes 3932168 | tf_op jit(solution)/shard_map/ppermute | solution.py:20
  67.9 25.7 %collective-permute-start.4 = (bf16[256,2560]{1,0:T(8,128)(2,1)}, bf16[256,2560]{1,0:T(8,128)(2,1)}, u32[]{:S(2)}, u32[]{:S(2)}) collective-permute-start(bf16[256,2560]{1,0:T(8,128)(2,1)} %refs_0_.2), channel_id=1, source_target_pairs={{0,1},{1,0},{2,3},{3,2},{4,5},{5,4},{6,7},{7,6},{8,9},{9,8},{10,11... | collective-permute-start | bytes 3932168 | tf_op jit(solution)/shard_map/ppermute | solution.py:20
  68.4 25.3 %copy-start.2 = (bf16[256,2560]{1,0:T(8,128)(2,1)S(1)}, bf16[256,2560]{1,0:T(8,128)(2,1)}, u32[]{:S(2)}) copy-start(bf16[256,2560]{1,0:T(8,128)(2,1)} %broadcast_select_fusion.3) | copy-start | bytes 3932164
  68.4 31.8 %copy-start = (bf16[256,2560]{1,0:T(8,128)(2,1)S(1)}, bf16[256,2560]{1,0:T(8,128)(2,1)}, u32[]{:S(2)}) copy-start(bf16[256,2560]{1,0:T(8,128)(2,1)} %queries.1) | copy-start | bytes 3932164
  68.4 31.8 %copy-start.1 = (s32[2,8]{1,0:T(2,128)S(1)}, s32[2,8]{1,0:T(2,128)}, u32[]{:S(2)}) copy-start(s32[2,8]{1,0:T(2,128)} %kept.3) | copy-start | bytes 196
  93.6 6.6 %collective-permute-start.11 = (bf16[256,2560]{1,0:T(8,128)(2,1)S(1)}, bf16[256,2560]{1,0:T(8,128)(2,1)S(1)}, u32[]{:S(2)}, u32[]{:S(2)}) collective-permute-start(bf16[256,2560]{1,0:T(8,128)(2,1)S(1)} %broadcast_select_fusion.1), channel_id=1, source_target_pairs={{0,1},{1,0},{2,3},{3,2},{4,5},{5,4},{6,7},{7,6},{8,9},{9,8},{10,11... | collective-permute-start | bytes 3932168 | tf_op jit(solution)/shard_map/ppermute | solution.py:20
  93.7 33.1 %collective-permute-start.12 = (bf16[256,2560]{1,0:T(8,128)(2,1)S(1)}, bf16[256,2560]{1,0:T(8,128)(2,1)S(1)}, u32[]{:S(2)}, u32[]{:S(2)}) collective-permute-start(bf16[256,2560]{1,0:T(8,128)(2,1)S(1)} %copy-done.2), channel_id=1, source_target_pairs={{0,2},{1,3},{4,6},{5,7},{6,4},{7,5},{8,10},{9,11},{10,8},{11,9},{1... | collective-permute-start | bytes 3932168 | tf_op jit(solution)/shard_map/ppermute | solution.py:20
  98.2 33.0 %collective-permute-start.14 = (bf16[256,2560]{1,0:T(8,128)(2,1)}, bf16[256,2560]{1,0:T(8,128)(2,1)S(1)}, u32[]{:S(2)}, u32[]{:S(2)}) collective-permute-start(bf16[256,2560]{1,0:T(8,128)(2,1)} %collective-permute-done.refs_6_), channel_id=1, source_target_pairs={{4,0},{5,1},{6,2},{7,3},{8,12},{9,13},{10,14},{11,15},{20,16},{21,... | collective-permute-start | bytes 3932168 | tf_op jit(solution)/shard_map/ppermute | solution.py:20
  99.5 31.7 %collective-permute-start.15 = (bf16[256,2560]{1,0:T(8,128)(2,1)S(1)}, bf16[256,2560]{1,0:T(8,128)(2,1)S(1)}, u32[]{:S(2)}, u32[]{:S(2)}) collective-permute-start(bf16[256,2560]{1,0:T(8,128)(2,1)S(1)} %collective-permute-done.1.refs_5_), channel_id=1, source_target_pairs={{4,8},{5,9},{6,10},{7,11},{8,4},{9,5},{10,6},{11,7},{20,24},{21,25... | collective-permute-start | bytes 3932168 | tf_op jit(solution)/shard_map/ppermute | solution.py:20
  126.9 4.2 %collective-permute-start.13 = (bf16[256,2560]{1,0:T(8,128)(2,1)S(1)}, bf16[256,2560]{1,0:T(8,128)(2,1)S(1)}, u32[]{:S(2)}, u32[]{:S(2)}) collective-permute-start(bf16[256,2560]{1,0:T(8,128)(2,1)S(1)} %broadcast_select_fusion), channel_id=1, source_target_pairs={{0,1},{1,0},{2,3},{3,2},{4,5},{5,4},{6,7},{7,6},{8,9},{9,8},{10,11... | collective-permute-start | bytes 3932168 | tf_op jit(solution)/shard_map/ppermute | solution.py:20

commit v3 on v2

v3 whole, which is shorter than its diff:
```python
import functools
import math

import jax
import jax.numpy as jnp
from jax import lax
from jax.experimental import pallas as pl
from jax.experimental.pallas import tpu as pltpu
from jax.sharding import PartitionSpec as P

DH = 128
BLOCK = 128
NEAR, FAR = (0, 1, 3, 5, 6), (2, 4, 7, 8)
TILES = 9
GROUPS = 4
UNROLL = 5


def permuted(value, target):
    count = lax.axis_size("blk")
    pairs = [(i, target(i)) for i in range(count)]
    return lax.ppermute(value, "blk", [(i, t) for i, t in pairs if t is not None and 0 <= t < count])


def swapped(value, bit):
    return permuted(value, lambda i: i ^ bit)


def swapped_odd(value):
    return permuted(value, lambda i: i + 4 if i & 4 else i - 4)


def far_even(value):
    count = lax.axis_size("blk")
    return permuted(value, lambda i: i ^ 4 if 0 <= (i + 4 if i & 4 else i - 4) < count else None)


def far_side(value):
    count = lax.axis_size("blk")
    return permuted(value, lambda i: i ^ 2 if 0 <= (i - 4 if i & 2 else i + 4) < count else None)


def after(value, *earlier):
    return lax.optimization_barrier((value, *earlier))[0]


def slots_of(place, kept, block, local_blocks, keep):
    position = place[0]
    bits = [position % 2, (position // 2) % 2, (position // 4) % 2]
    found = []
    for entry in range(keep):
        listed = kept[block, entry]
        offset = listed // local_blocks - position
        ahead = (offset > 0).astype(jnp.int32)
        near = jnp.abs(offset)
        step = sum((near >= reach).astype(jnp.int32) for reach in (1, 2, 4, 8))
        flip = jnp.where(step == 1, bits[0], jnp.where(step == 2, bits[1], bits[2]))
        slot = jnp.where(step == 0, 0, 2 * step - (ahead + flip) % 2)
        found.append((slot, pl.multiple_of((listed % local_blocks) * BLOCK, BLOCK)))
    return found


def score_kernel(local_blocks, keep, groups, place, kept, queries, *refs):
    tiles, near = refs[:TILES], refs[TILES : TILES + len(NEAR)]
    weights, totals, values, keys, key_sems, value_sems = refs[TILES + len(NEAR) :]
    copies = []
    for group, (first, count) in enumerate(groups):
        lanes = pl.ds(first * DH, count * DH)
        copies.append(
            [
                pltpu.make_async_copy(
                    tile.at[:, lanes], keys.at[index, :, lanes], key_sems.at[group, index]
                )
                for index, tile in enumerate(tiles)
            ]
        )
        for copy in copies[-1]:
            copy.start()
    value_copies = [
        pltpu.make_async_copy(tile, values.at[slot], value_sems.at[index])
        for index, (slot, tile) in enumerate(zip(NEAR, near))
    ]
    for copy in value_copies:
        copy.start()
    scale = math.log2(math.e) / math.sqrt(DH)
    found = [slots_of(place, kept, block, local_blocks, keep) for block in range(local_blocks)]

    def one_head(head, carry):
        lanes = pl.ds(pl.multiple_of(head * DH, DH), DH)
        for block in range(local_blocks):
            rows = pl.ds(block * BLOCK, BLOCK)
            gathered = jnp.concatenate(
                [keys[slot, pl.ds(row, BLOCK), lanes] for slot, row in found[block]], axis=0
            )
            scores = lax.dot_general(
                queries[rows, lanes],
                gathered,
                (((1,), (1,)), ((), ())),
                preferred_element_type=jnp.float32,
            )
            top = jnp.max(scores, axis=1, keepdims=True)
            weight = jnp.exp2((scores - top) * scale)
            total = jnp.sum(weight, axis=1, keepdims=True)
            weights[head, rows, :] = weight.astype(jnp.bfloat16)
            totals[head, rows, :] = jnp.broadcast_to(total, (BLOCK, DH))
        return carry

    for (first, count), arriving in zip(groups, copies):
        for copy in arriving:
            copy.wait()
        lax.fori_loop(first, first + count, one_head, 0, unroll=UNROLL)
    for copy in value_copies:
        copy.wait()


def value_kernel(local_blocks, keep, groups, place, kept, weights, totals, *refs):
    far, (attended, values, result, far_sems, out_sems) = refs[1:-5], refs[-5:]
    copies = []
    for group, (first, count) in enumerate(groups):
        lanes = pl.ds(first * DH, count * DH)
        arriving = []
        for index, (slot, tile) in enumerate(zip(FAR, far)):
            arriving.append(
                pltpu.make_async_copy(
                    tile.at[:, lanes], values.at[slot, :, lanes], far_sems.at[group, index]
                )
            )
        for copy in arriving:
            copy.start()
        copies.append(arriving)
    found = [slots_of(place, kept, block, local_blocks, keep) for block in range(local_blocks)]

    def one_head(head, carry):
        lanes = pl.ds(pl.multiple_of(head * DH, DH), DH)
        for block in range(local_blocks):
            rows = pl.ds(block * BLOCK, BLOCK)
            gathered = jnp.concatenate(
                [values[slot, pl.ds(row, BLOCK), lanes] for slot, row in found[block]], axis=0
            )
            numerator = jnp.dot(
                weights[head, rows, :], gathered, preferred_element_type=jnp.float32
            )
            result[rows, lanes] = (numerator / totals[head, rows, :]).astype(jnp.bfloat16)
        return carry

    leaving = []
    for group, (first, count) in enumerate(groups):
        for copy in copies[group]:
            copy.wait()
        lax.fori_loop(first, first + count, one_head, 0, unroll=UNROLL)
        lanes = pl.ds(first * DH, count * DH)
        leaving.append(
            pltpu.make_async_copy(
                result.at[:, lanes], attended.at[:, lanes], out_sems.at[group]
            )
        )
        leaving[-1].start()
    for copy in leaving:
        copy.wait()


def in_vmem(array):
    return pltpu.with_memory_space_constraint(array, pltpu.VMEM)


def weigh(place, kept, queries, tiles, near, groups):
    rows, columns = queries.shape
    heads = columns // DH
    local_blocks, keep = kept.shape
    scalars = pl.BlockSpec(memory_space=pltpu.SMEM)
    held = pl.BlockSpec(memory_space=pltpu.VMEM)
    anywhere = pl.BlockSpec(memory_space=pl.ANY)
    pairs = local_blocks * keep * heads
    return pl.pallas_call(
        functools.partial(score_kernel, local_blocks, keep, groups),
        out_shape=(
            pltpu.VMEM((heads, rows, keep * BLOCK), jnp.bfloat16),
            pltpu.VMEM((heads, rows, DH), jnp.float32),
            pltpu.VMEM((TILES, rows, columns), jnp.bfloat16),
        ),
        in_specs=[scalars, scalars, held] + [anywhere] * (len(tiles) + len(near)),
        out_specs=(held, held, held),
        scratch_shapes=[
            pltpu.VMEM((TILES, rows, columns), jnp.bfloat16),
            pltpu.SemaphoreType.DMA((len(groups), TILES)),
            pltpu.SemaphoreType.DMA((len(near),)),
        ],
        compiler_params=pltpu.CompilerParams(vmem_limit_bytes=16 * 1024 * 1024),
        cost_estimate=pl.CostEstimate(
            flops=2 * pairs * BLOCK * BLOCK * DH,
            bytes_accessed=(len(tiles) + 1) * rows * columns * 2 + heads * rows * keep * BLOCK * 2,
            transcendentals=pairs * BLOCK * BLOCK,
        ),
        name="weigh",
    )(place, kept, in_vmem(queries), *tiles, *near)


def combine(place, kept, weights, totals, values, far, groups):
    heads, rows, _ = weights.shape
    local_blocks, keep = kept.shape
    scalars = pl.BlockSpec(memory_space=pltpu.SMEM)
    held = pl.BlockSpec(memory_space=pltpu.VMEM)
    anywhere = pl.BlockSpec(memory_space=pl.ANY)
    return pl.pallas_call(
        functools.partial(value_kernel, local_blocks, keep, groups),
        out_shape=(
            jax.ShapeDtypeStruct((rows, heads * DH), jnp.bfloat16),
            pltpu.VMEM(values.shape, values.dtype),
        ),
        in_specs=[scalars, scalars] + [held] * 3 + [anywhere] * len(far),
        out_specs=(anywhere, held),
        input_output_aliases={4: 1},
        scratch_shapes=[
            pltpu.VMEM((rows, heads * DH), jnp.bfloat16),
            pltpu.SemaphoreType.DMA((len(groups), len(FAR))),
            pltpu.SemaphoreType.DMA((len(groups),)),
        ],
        compiler_params=pltpu.CompilerParams(vmem_limit_bytes=4 * 1024 * 1024),
        cost_estimate=pl.CostEstimate(
            flops=2 * local_blocks * keep * heads * BLOCK * BLOCK * DH,
            bytes_accessed=len(FAR) * rows * heads * DH * 2,
            transcendentals=0,
        ),
        name="combine",
    )(place, kept, in_vmem(weights), in_vmem(totals), in_vmem(values), *far)[0]


def per_device(queries, keys, values, kept_blocks):
    position = lax.axis_index("blk").astype(jnp.int32)
    place = position.reshape(1)
    core_bit, side_bit, level_bit = (position % 2, (position // 2) % 2, (position // 4) % 2)
    same_side, same_core = side_bit == level_bit, core_bit == side_bit
    heads = queries.shape[1] // DH

    count = heads // GROUPS
    groups = [(first, count) for first in range(0, heads, count)]

    k_side, k_odd, k_even = swapped(keys, 2), swapped_odd(keys), swapped(keys, 4)
    v_side, v_odd, v_even = swapped(after(values, k_side), 2), swapped_odd(values), swapped(values, 4)
    k_mix = jnp.where(same_side, k_even, k_odd)
    k_odd_far, k_even_far = swapped_odd(k_even), swapped(k_odd, 4)
    k_side_far = swapped(after(k_mix, v_side), 2)
    v_mix = jnp.where(same_side, after(v_even, v_side), after(v_odd, v_side))
    k_core = swapped(after(keys, v_odd, v_even, v_mix), 1)
    v_core = swapped(after(values, v_odd, v_even, v_mix), 1)
    v_odd_far = swapped_odd(after(v_even, v_side))
    v_even_far = swapped(after(v_odd, v_side), 4)
    v_side_far = swapped(after(v_mix, k_side_far), 2)
    k_core_far = swapped(
        after(jnp.where(same_core, k_side, k_side_far), k_core, v_core, k_odd_far, k_even_far), 1
    )

    tiles = (keys, k_core, k_core_far, k_side, k_side_far, k_even, k_odd, k_even_far, k_odd_far)
    near = (values, v_core, v_side, v_even, v_odd)
    weights, totals, staged = weigh(place, kept_blocks, queries, tiles, near, groups)

    v_side_done = after(v_side_far, totals)
    v_core_far = swapped(jnp.where(same_core, v_side, v_side_done), 1)
    far = (v_core_far, v_side_done, v_even_far, v_odd_far)
    return combine(place, kept_blocks, weights, totals, staged, far, groups)


def solution(mesh):
    placed = P(("clip", "blk"), None)
    return jax.shard_map(
        per_device, mesh=mesh, in_specs=(placed,) * 4, out_specs=placed, check_vma=False
    )
```

time: 142 us -> 136 us (0.958)
  Pallas kernels: 22.9 us -> 14 us
  starting transfers between devices: 27.7 us -> 25 us
  waiting for transfers between devices: 84.8 us -> 87.4 us
    pallas_call x2, Pallas kernels: 22.9 us -> 14 us  [the longest x1 8.41 us: weigh(): pl.pallas_call(functools.partial(score_kernel, local_blocks, keep, groups...]
    ppermute x16, starting transfers between devices: 27.7 us -> 25 us  [permuted(): lax.ppermute(value, 'blk', [(i, t) for i, t in pairs if t is not None and...]
    ppermute x16, waiting for transfers between devices: 84.8 us -> 87.4 us  [permuted(): lax.ppermute(value, 'blk', [(i, t) for i, t in pairs if t is not None and...]
  transfers between devices with their start and end apart: 16 -> 16, of which waited for: 5 -> 8; matrix products, arithmetic and copies ran while one was open for 4% -> 5% of each run, Pallas kernels for 9% -> 6%
where the time goes in v3:
time: 136 us; the launch traced here: 134 us
  waiting for transfers between devices  87.4 us (64%)
  starting transfers between devices  25 us (18%)
  Pallas kernels  14 us (10%)
  other arithmetic  6.61 us (5%)
    ppermute x16, waiting for transfers between devices, permuted(): lax.ppermute(value, 'blk', [(i, t) for i, t in pairs if t is not None and...  87.4 us
    ppermute x16, starting transfers between devices, permuted(): lax.ppermute(value, 'blk', [(i, t) for i, t in pairs if t is not None and...  25 us
    pallas_call x1, Pallas kernels, weigh(): pl.pallas_call(functools.partial(score_kernel, local_blocks, keep, groups...  8.41 us
    pallas_call x1, Pallas kernels, combine(): pl.pallas_call(functools.partial(value_kernel, local_blocks, keep, groups...  5.63 us
  transfers between devices with their start and end apart: 16, of which 8 were waited for; matrix products, arithmetic and copies ran while one was open for 5% of the time, Pallas kernels for 6%

profile of v3, /device:TPU:0, one launch (start us, length us, event | category | flops | bytes accessed | tf_op | source)
XLA Modules:
  0.0 134.5 jit_solution(5184068098264888828)
XLA Ops:
  0.0 3.0 %collective-permute-start.2 = (bf16[256,2560]{1,0:T(8,128)(2,1)}, bf16[256,2560]{1,0:T(8,128)(2,1)S(1)}, u32[]{:S(2)}, u32[]{:S(2)}) collective-permute-start(bf16[256,2560]{1,0:T(8,128)(2,1)} %refs_0_.1), channel_id=1, source_target_pairs={{0,2},{1,3},{2,0},{3,1},{4,6},{5,7},{6,4},{7,5},{8,10},{9,11},{10,... | collective-permute-start | bytes 3932168 | tf_op jit(solution)/shard_map/ppermute | solution.py:22
  3.0 0.7 collective-permute-start.6
  3.7 4.4 %collective-permute-start.5 = (bf16[256,2560]{1,0:T(8,128)(2,1)}, bf16[256,2560]{1,0:T(8,128)(2,1)}, u32[]{:S(2)}, u32[]{:S(2)}) collective-permute-start(bf16[256,2560]{1,0:T(8,128)(2,1)} %refs_0_.1), channel_id=1, source_target_pairs={{0,4},{1,5},{2,6},{3,7},{4,0},{5,1},{6,2},{7,3},{8,12},{9,13},{10,... | collective-permute-start | bytes 3932168 | tf_op jit(solution)/shard_map/ppermute | solution.py:22
  8.1 23.9 %collective-permute-done.2.refs_3_ = bf16[256,2560]{1,0:T(8,128)(2,1)S(1)} collective-permute-done((bf16[256,2560]{1,0:T(8,128)(2,1)}, bf16[256,2560]{1,0:T(8,128)(2,1)S(1)}, u32[]{:S(2)}, u32[]{:S(2)}) %collective-permute-start.2) | collective-permute-done | bytes 1310752 | tf_op jit(solution)/shard_map/ppermute | solution.py:22
  32.0 1.7 %collective-permute-start.3 = (bf16[256,2560]{1,0:T(8,128)(2,1)}, bf16[256,2560]{1,0:T(8,128)(2,1)}, u32[]{:S(2)}, u32[]{:S(2)}) collective-permute-start(bf16[256,2560]{1,0:T(8,128)(2,1)} %refs_9_.1), channel_id=1, source_target_pairs={{0,2},{1,3},{2,0},{3,1},{4,6},{5,7},{6,4},{7,5},{8,10},{9,11},{10,... | collective-permute-start | bytes 3932168 | tf_op jit(solution)/shard_map/ppermute | solution.py:22
  33.7 1.6 %collective-permute-start.1 = (bf16[256,2560]{1,0:T(8,128)(2,1)}, bf16[256,2560]{1,0:T(8,128)(2,1)}, u32[]{:S(2)}, u32[]{:S(2)}) collective-permute-start(bf16[256,2560]{1,0:T(8,128)(2,1)} %refs_9_.1), channel_id=1, source_target_pairs={{0,4},{1,5},{2,6},{3,7},{4,0},{5,1},{6,2},{7,3},{8,12},{9,13},{10,... | collective-permute-start | bytes 3932168 | tf_op jit(solution)/shard_map/ppermute | solution.py:22
  35.3 1.7 %collective-permute-start = (bf16[256,2560]{1,0:T(8,128)(2,1)}, bf16[256,2560]{1,0:T(8,128)(2,1)}, u32[]{:S(2)}, u32[]{:S(2)}) collective-permute-start(bf16[256,2560]{1,0:T(8,128)(2,1)} %refs_9_.1), channel_id=1, source_target_pairs={{4,8},{5,9},{6,10},{7,11},{8,4},{9,5},{10,6},{11,7},{20,24},{21,25... | collective-permute-start | bytes 3932168 | tf_op jit(solution)/shard_map/ppermute | solution.py:22
  37.0 3.5 %collective-permute-start.10 = (bf16[256,2560]{1,0:T(8,128)(2,1)S(1)}, bf16[256,2560]{1,0:T(8,128)(2,1)}, u32[]{:S(2)}, u32[]{:S(2)}) collective-permute-start(bf16[256,2560]{1,0:T(8,128)(2,1)S(1)} %collective-permute-done.6.refs_6_), channel_id=1, source_target_pairs={{0,4},{1,5},{2,6},{3,7},{4,0},{5,1},{6,2},{7,3},{8,12},{9,13},{10,... | collective-permute-start | bytes 3932168 | tf_op jit(solution)/shard_map/ppermute | solution.py:22
  40.5 0.0 collective-permute-done.5.refs_5_
  40.5 1.7 %collective-permute-start.9 = (bf16[256,2560]{1,0:T(8,128)(2,1)}, bf16[256,2560]{1,0:T(8,128)(2,1)}, u32[]{:S(2)}, u32[]{:S(2)}) collective-permute-start(bf16[256,2560]{1,0:T(8,128)(2,1)} %collective-permute-done.5.refs_5_), channel_id=1, source_target_pairs={{4,8},{5,9},{6,10},{7,11},{8,4},{9,5},{10,6},{11,7},{20,24},{21,25... | collective-permute-start | bytes 3932168 | tf_op jit(solution)/shard_map/ppermute | solution.py:22
  42.2 2.5 %broadcast_select_fusion.2 = bf16[256,2560]{1,0:T(8,128)(2,1)} fusion(bf16[256,2560]{1,0:T(8,128)(2,1)} %collective-permute-done.5.refs_5_, bf16[256,2560]{1,0:T(8,128)(2,1)S(1)} %collective-permute-done.6.refs_6_, pred[]{:T(512)S(6)} %eq.10), kind=kLoop, calls=%fused_computation.2 | loop fusion | flops 655360 | bytes 3932161 | tf_op jit(solution)/shard_map/jit(_where)/select_n | solution.py:240
  44.7 17.6 %collective-permute-done.3.refs_11_ = bf16[256,2560]{1,0:T(8,128)(2,1)} collective-permute-done((bf16[256,2560]{1,0:T(8,128)(2,1)}, bf16[256,2560]{1,0:T(8,128)(2,1)}, u32[]{:S(2)}, u32[]{:S(2)}) %collective-permute-start.3) | collective-permute-done | bytes 1310752 | tf_op jit(solution)/shard_map/ppermute | solution.py:22
  62.3 1.4 %collective-permute-start.7 = (bf16[256,2560]{1,0:T(8,128)(2,1)}, bf16[256,2560]{1,0:T(8,128)(2,1)}, u32[]{:S(2)}, u32[]{:S(2)}) collective-permute-start(bf16[256,2560]{1,0:T(8,128)(2,1)} %broadcast_select_fusion.2), channel_id=1, source_target_pairs={{0,2},{1,3},{2,0},{3,1},{4,6},{5,7},{6,4},{7,5},{8,10},{9,11},{10,... | collective-permute-start | bytes 3932168 | tf_op jit(solution)/shard_map/ppermute | solution.py:22
  63.8 2.1 %collective-permute-done.1.refs_12_ = bf16[256,2560]{1,0:T(8,128)(2,1)} collective-permute-done((bf16[256,2560]{1,0:T(8,128)(2,1)}, bf16[256,2560]{1,0:T(8,128)(2,1)}, u32[]{:S(2)}, u32[]{:S(2)}) %collective-permute-start.1) | collective-permute-done | bytes 1310752 | tf_op jit(solution)/shard_map/ppermute | solution.py:22
  65.9 0.0 collective-permute-done.refs_13_
  65.9 2.5 %broadcast_select_fusion.3 = bf16[256,2560]{1,0:T(8,128)(2,1)} fusion(bf16[256,2560]{1,0:T(8,128)(2,1)} %collective-permute-done.1.refs_12_, bf16[256,2560]{1,0:T(8,128)(2,1)} %collective-permute-done.refs_13_, pred[]{:T(512)S(6)} %eq.10), kind=kLoop, calls=%fused_computation.3 | loop fusion | flops 655360 | bytes 3932161 | tf_op jit(solution)/shard_map/jit(_where)/select_n | solution.py:243
  68.4 0.5 collective-permute-start.4
  68.9 22.9 %collective-permute-done.7.refs_4_ = bf16[256,2560]{1,0:T(8,128)(2,1)} collective-permute-done((bf16[256,2560]{1,0:T(8,128)(2,1)}, bf16[256,2560]{1,0:T(8,128)(2,1)}, u32[]{:S(2)}, u32[]{:S(2)}) %collective-permute-start.7) | collective-permute-done | bytes 1310752 | tf_op jit(solution)/shard_map/ppermute | solution.py:22
  91.8 0.1 broadcast_select_fusion.1
  91.9 0.9 collective-permute-done.10.refs_7_
  92.8 0.1 collective-permute-start.11
  92.9 1.7 %collective-permute-start.12 = (bf16[256,2560]{1,0:T(8,128)(2,1)}, bf16[256,2560]{1,0:T(8,128)(2,1)S(1)}, u32[]{:S(2)}, u32[]{:S(2)}) collective-permute-start(bf16[256,2560]{1,0:T(8,128)(2,1)} %broadcast_select_fusion.3), channel_id=1, source_target_pairs={{0,2},{1,3},{2,0},{3,1},{4,6},{5,7},{6,4},{7,5},{8,10},{9,11},{10,... | collective-permute-start | bytes 3932168 | tf_op jit(solution)/shard_map/ppermute | solution.py:22
  94.6 2.2 %collective-permute-start.14 = (bf16[256,2560]{1,0:T(8,128)(2,1)}, bf16[256,2560]{1,0:T(8,128)(2,1)S(1)}, u32[]{:S(2)}, u32[]{:S(2)}) collective-permute-start(bf16[256,2560]{1,0:T(8,128)(2,1)} %collective-permute-done.refs_13_), channel_id=1, source_target_pairs={{0,4},{1,5},{2,6},{3,7},{4,0},{5,1},{6,2},{7,3},{8,12},{9,13},{10,... | collective-permute-start | bytes 3932168 | tf_op jit(solution)/shard_map/ppermute | solution.py:22
  96.8 0.7 collective-permute-start.15
  97.6 1.3 copy-done.1
  98.9 8.4 %weigh.1 = (bf16[20,256,1024]{2,1,0:T(8,128)(2,1)S(1)}, f32[20,256,128]{2,1,0:T(8,128)S(1)}, bf16[9,256,2560]{2,1,0:T(8,128)(2,1)S(1)}) custom-call(s32[1]{0:T(128)} %bitcast.place, s32[2,8]{1,0:T(2,128)S(1)} %copy-done.5, bf16[256,2560]{1,0:T(8,128)(2,1)S(1)} %copy-done.4, bf16[256,2560]{1,0:T(8,128)(2,1)} %refs_0_.1, ...), custom_call_target="tpu_custom_call" | custom-call | flops 1342177280 | bytes 23592960 | tf_op jit(solution)/shard_map/weigh/pallas_call | solution.py:174
  107.3 17.0 %collective-permute-done.12.refs_2_ = bf16[256,2560]{1,0:T(8,128)(2,1)S(1)} collective-permute-done((bf16[256,2560]{1,0:T(8,128)(2,1)}, bf16[256,2560]{1,0:T(8,128)(2,1)S(1)}, u32[]{:S(2)}, u32[]{:S(2)}) %collective-permute-start.12) | collective-permute-done | bytes 1310752 | tf_op jit(solution)/shard_map/ppermute | solution.py:22
  124.3 1.5 %broadcast_select_fusion = bf16[256,2560]{1,0:T(8,128)(2,1)S(1)} fusion(bf16[256,2560]{1,0:T(8,128)(2,1)} %collective-permute-done.3.refs_11_, bf16[256,2560]{1,0:T(8,128)(2,1)S(1)} %collective-permute-done.12.refs_2_, pred[]{:T(512)S(6)} %eq.11), kind=kLoop, calls=%fused_computation | loop fusion | flops 655360 | bytes 3932161 | tf_op jit(solution)/shard_map/jit(_where)/select_n | solution.py:258
  125.8 0.1 collective-permute-start.13
  125.8 0.2 collective-permute-done.14.refs_3_
  126.1 2.8 %collective-permute-done.13.refs_1_ = bf16[256,2560]{1,0:T(8,128)(2,1)S(1)} collective-permute-done((bf16[256,2560]{1,0:T(8,128)(2,1)S(1)}, bf16[256,2560]{1,0:T(8,128)(2,1)S(1)}, u32[]{:S(2)}, u32[]{:S(2)}) %collective-permute-start.13) | collective-permute-done | bytes 1310752 | tf_op jit(solution)/shard_map/ppermute | solution.py:22
  128.9 5.6 %combine.1 = (bf16[256,2560]{1,0:T(8,128)(2,1)}, bf16[9,256,2560]{2,1,0:T(8,128)(2,1)S(1)}) custom-call(s32[1]{0:T(128)} %bitcast.place, s32[2,8]{1,0:T(2,128)S(1)} %copy-done.5, bf16[20,256,1024]{2,1,0:T(8,128)(2,1)S(1)} %get-tuple-element.25.weights, f32[20,256,128]{2,1,0:T(8,128)S(1)} %get-tuple-element.26.totals, ...), custom_call_target="tpu_custom_call", output_to_operand_aliasing={{1}: (4, {})} | custom-call | flops 1342177280 | bytes 5242880 | tf_op jit(solution)/shard_map/combine/pallas_call | solution.py:204
  (18 shorter events, 0.0 us)
Async XLA Ops:
  0.0 32.0 %collective-permute-start.2 = (bf16[256,2560]{1,0:T(8,128)(2,1)}, bf16[256,2560]{1,0:T(8,128)(2,1)S(1)}, u32[]{:S(2)}, u32[]{:S(2)}) collective-permute-start(bf16[256,2560]{1,0:T(8,128)(2,1)} %refs_0_.1), channel_id=1, source_target_pairs={{0,2},{1,3},{2,0},{3,1},{4,6},{5,7},{6,4},{7,5},{8,10},{9,11},{10,... | collective-permute-start | bytes 3932168 | tf_op jit(solution)/shard_map/ppermute | solution.py:22
  3.0 34.0 %collective-permute-start.6 = (bf16[256,2560]{1,0:T(8,128)(2,1)}, bf16[256,2560]{1,0:T(8,128)(2,1)S(1)}, u32[]{:S(2)}, u32[]{:S(2)}) collective-permute-start(bf16[256,2560]{1,0:T(8,128)(2,1)} %refs_0_.1), channel_id=1, source_target_pairs={{4,8},{5,9},{6,10},{7,11},{8,4},{9,5},{10,6},{11,7},{20,24},{21,25... | collective-permute-start | bytes 3932168 | tf_op jit(solution)/shard_map/ppermute | solution.py:22
  3.7 36.8 %collective-permute-start.5 = (bf16[256,2560]{1,0:T(8,128)(2,1)}, bf16[256,2560]{1,0:T(8,128)(2,1)}, u32[]{:S(2)}, u32[]{:S(2)}) collective-permute-start(bf16[256,2560]{1,0:T(8,128)(2,1)} %refs_0_.1), channel_id=1, source_target_pairs={{0,4},{1,5},{2,6},{3,7},{4,0},{5,1},{6,2},{7,3},{8,12},{9,13},{10,... | collective-permute-start | bytes 3932168 | tf_op jit(solution)/shard_map/ppermute | solution.py:22
  32.0 59.9 %copy-start = (bf16[256,2560]{1,0:T(8,128)(2,1)}, bf16[256,2560]{1,0:T(8,128)(2,1)S(1)}, u32[]{:S(2)}) copy-start(bf16[256,2560]{1,0:T(8,128)(2,1)S(1)} %collective-permute-done.2.refs_3_) | copy-start | bytes 3932164
  32.0 30.4 %collective-permute-start.3 = (bf16[256,2560]{1,0:T(8,128)(2,1)}, bf16[256,2560]{1,0:T(8,128)(2,1)}, u32[]{:S(2)}, u32[]{:S(2)}) collective-permute-start(bf16[256,2560]{1,0:T(8,128)(2,1)} %refs_9_.1), channel_id=1, source_target_pairs={{0,2},{1,3},{2,0},{3,1},{4,6},{5,7},{6,4},{7,5},{8,10},{9,11},{10,... | collective-permute-start | bytes 3932168 | tf_op jit(solution)/shard_map/ppermute | solution.py:22
  33.7 32.2 %collective-permute-start.1 = (bf16[256,2560]{1,0:T(8,128)(2,1)}, bf16[256,2560]{1,0:T(8,128)(2,1)}, u32[]{:S(2)}, u32[]{:S(2)}) collective-permute-start(bf16[256,2560]{1,0:T(8,128)(2,1)} %refs_9_.1), channel_id=1, source_target_pairs={{0,4},{1,5},{2,6},{3,7},{4,0},{5,1},{6,2},{7,3},{8,12},{9,13},{10,... | collective-permute-start | bytes 3932168 | tf_op jit(solution)/shard_map/ppermute | solution.py:22
  35.3 30.6 %collective-permute-start = (bf16[256,2560]{1,0:T(8,128)(2,1)}, bf16[256,2560]{1,0:T(8,128)(2,1)}, u32[]{:S(2)}, u32[]{:S(2)}) collective-permute-start(bf16[256,2560]{1,0:T(8,128)(2,1)} %refs_9_.1), channel_id=1, source_target_pairs={{4,8},{5,9},{6,10},{7,11},{8,4},{9,5},{10,6},{11,7},{20,24},{21,25... | collective-permute-start | bytes 3932168 | tf_op jit(solution)/shard_map/ppermute | solution.py:22
  37.0 7.7 %copy-start.2 = (bf16[256,2560]{1,0:T(8,128)(2,1)}, bf16[256,2560]{1,0:T(8,128)(2,1)S(1)}, u32[]{:S(2)}) copy-start(bf16[256,2560]{1,0:T(8,128)(2,1)S(1)} %collective-permute-done.6.refs_6_) | copy-start | bytes 3932164
  37.0 55.8 %collective-permute-start.10 = (bf16[256,2560]{1,0:T(8,128)(2,1)S(1)}, bf16[256,2560]{1,0:T(8,128)(2,1)}, u32[]{:S(2)}, u32[]{:S(2)}) collective-permute-start(bf16[256,2560]{1,0:T(8,128)(2,1)S(1)} %collective-permute-done.6.refs_6_), channel_id=1, source_target_pairs={{0,4},{1,5},{2,6},{3,7},{4,0},{5,1},{6,2},{7,3},{8,12},{9,13},{10,... | collective-permute-start | bytes 3932168 | tf_op jit(solution)/shard_map/ppermute | solution.py:22
  40.5 52.3 %collective-permute-start.9 = (bf16[256,2560]{1,0:T(8,128)(2,1)}, bf16[256,2560]{1,0:T(8,128)(2,1)}, u32[]{:S(2)}, u32[]{:S(2)}) collective-permute-start(bf16[256,2560]{1,0:T(8,128)(2,1)} %collective-permute-done.5.refs_5_), channel_id=1, source_target_pairs={{4,8},{5,9},{6,10},{7,11},{8,4},{9,5},{10,6},{11,7},{20,24},{21,25... | collective-permute-start | bytes 3932168 | tf_op jit(solution)/shard_map/ppermute | solution.py:22
  62.3 29.5 %collective-permute-start.7 = (bf16[256,2560]{1,0:T(8,128)(2,1)}, bf16[256,2560]{1,0:T(8,128)(2,1)}, u32[]{:S(2)}, u32[]{:S(2)}) collective-permute-start(bf16[256,2560]{1,0:T(8,128)(2,1)} %broadcast_select_fusion.2), channel_id=1, source_target_pairs={{0,2},{1,3},{2,0},{3,1},{4,6},{5,7},{6,4},{7,5},{8,10},{9,11},{10,... | collective-permute-start | bytes 3932168 | tf_op jit(solution)/shard_map/ppermute | solution.py:22
  68.4 24.4 %collective-permute-start.8 = (bf16[256,2560]{1,0:T(8,128)(2,1)}, bf16[256,2560]{1,0:T(8,128)(2,1)}, u32[]{:S(2)}, u32[]{:S(2)}) collective-permute-start(bf16[256,2560]{1,0:T(8,128)(2,1)} %refs_9_.1), channel_id=1, source_target_pairs={{0,1},{1,0},{2,3},{3,2},{4,5},{5,4},{6,7},{7,6},{8,9},{9,8},{10,11... | collective-permute-start | bytes 3932168 | tf_op jit(solution)/shard_map/ppermute | solution.py:22
  68.4 24.4 %collective-permute-start.4 = (bf16[256,2560]{1,0:T(8,128)(2,1)}, bf16[256,2560]{1,0:T(8,128)(2,1)}, u32[]{:S(2)}, u32[]{:S(2)}) collective-permute-start(bf16[256,2560]{1,0:T(8,128)(2,1)} %refs_0_.1), channel_id=1, source_target_pairs={{0,1},{1,0},{2,3},{3,2},{4,5},{5,4},{6,7},{7,6},{8,9},{9,8},{10,11... | collective-permute-start | bytes 3932168 | tf_op jit(solution)/shard_map/ppermute | solution.py:22
  68.9 28.6 %copy-start.3 = (bf16[256,2560]{1,0:T(8,128)(2,1)S(1)}, bf16[256,2560]{1,0:T(8,128)(2,1)}, u32[]{:S(2)}) copy-start(bf16[256,2560]{1,0:T(8,128)(2,1)} %copy-done.2) | copy-start | bytes 3932164
  68.9 28.6 %copy-start.4 = (bf16[256,2560]{1,0:T(8,128)(2,1)S(1)}, bf16[256,2560]{1,0:T(8,128)(2,1)}, u32[]{:S(2)}) copy-start(bf16[256,2560]{1,0:T(8,128)(2,1)} %queries.1) | copy-start | bytes 3932164
  68.9 28.6 %copy-start.5 = (s32[2,8]{1,0:T(2,128)S(1)}, s32[2,8]{1,0:T(2,128)}, u32[]{:S(2)}) copy-start(s32[2,8]{1,0:T(2,128)} %kept.3) | copy-start | bytes 196
  92.8 4.7 %collective-permute-start.11 = (bf16[256,2560]{1,0:T(8,128)(2,1)S(1)}, bf16[256,2560]{1,0:T(8,128)(2,1)S(1)}, u32[]{:S(2)}, u32[]{:S(2)}) collective-permute-start(bf16[256,2560]{1,0:T(8,128)(2,1)S(1)} %broadcast_select_fusion.1), channel_id=1, source_target_pairs={{0,1},{1,0},{2,3},{3,2},{4,5},{5,4},{6,7},{7,6},{8,9},{9,8},{10,11... | collective-permute-start | bytes 3932168 | tf_op jit(solution)/shard_map/ppermute | solution.py:22
  92.9 31.4 %collective-permute-start.12 = (bf16[256,2560]{1,0:T(8,128)(2,1)}, bf16[256,2560]{1,0:T(8,128)(2,1)S(1)}, u32[]{:S(2)}, u32[]{:S(2)}) collective-permute-start(bf16[256,2560]{1,0:T(8,128)(2,1)} %broadcast_select_fusion.3), channel_id=1, source_target_pairs={{0,2},{1,3},{2,0},{3,1},{4,6},{5,7},{6,4},{7,5},{8,10},{9,11},{10,... | collective-permute-start | bytes 3932168 | tf_op jit(solution)/shard_map/ppermute | solution.py:22
  94.6 31.5 %collective-permute-start.14 = (bf16[256,2560]{1,0:T(8,128)(2,1)}, bf16[256,2560]{1,0:T(8,128)(2,1)S(1)}, u32[]{:S(2)}, u32[]{:S(2)}) collective-permute-start(bf16[256,2560]{1,0:T(8,128)(2,1)} %collective-permute-done.refs_13_), channel_id=1, source_target_pairs={{0,4},{1,5},{2,6},{3,7},{4,0},{5,1},{6,2},{7,3},{8,12},{9,13},{10,... | collective-permute-start | bytes 3932168 | tf_op jit(solution)/shard_map/ppermute | solution.py:22
  96.8 29.3 %collective-permute-start.15 = (bf16[256,2560]{1,0:T(8,128)(2,1)}, bf16[256,2560]{1,0:T(8,128)(2,1)S(1)}, u32[]{:S(2)}, u32[]{:S(2)}) collective-permute-start(bf16[256,2560]{1,0:T(8,128)(2,1)} %collective-permute-done.1.refs_12_), channel_id=1, source_target_pairs={{4,8},{5,9},{6,10},{7,11},{8,4},{9,5},{10,6},{11,7},{20,24},{21,25... | collective-permute-start | bytes 3932168 | tf_op jit(solution)/shard_map/ppermute | solution.py:22
  97.5 1.3 copy-start.1
  125.8 3.1 %collective-permute-start.13 = (bf16[256,2560]{1,0:T(8,128)(2,1)S(1)}, bf16[256,2560]{1,0:T(8,128)(2,1)S(1)}, u32[]{:S(2)}, u32[]{:S(2)}) collective-permute-start(bf16[256,2560]{1,0:T(8,128)(2,1)S(1)} %broadcast_select_fusion), channel_id=1, source_target_pairs={{0,1},{1,0},{2,3},{3,2},{4,5},{5,4},{6,7},{7,6},{8,9},{9,8},{10,11... | collective-permute-start | bytes 3932168 | tf_op jit(solution)/shard_map/ppermute | solution.py:22

commit v4 on v2

v4 whole, which is shorter than its diff:
```python
import functools
import math

import jax
import jax.numpy as jnp
from jax import lax
from jax.experimental import pallas as pl
from jax.experimental.pallas import tpu as pltpu
from jax.sharding import PartitionSpec as P

DH = 128
BLOCK = 128
LANES = 128
VALUE_SPLIT = (15, 5)
GROUP = 5
OWN_TILES = 6
FAR = (4, 5)
LENT_TILES = 4
SCALE = math.log2(math.e) / math.sqrt(DH)
MASKED = -1e30


def permuted(value, target):
    count = lax.axis_size("blk")
    pairs = [(i, target(i)) for i in range(count)]
    return lax.ppermute(value, "blk", [(i, t) for i, t in pairs if 0 <= t < count])


def swapped(value, bit):
    return permuted(value, lambda i: i ^ bit)


def swapped_odd(value):
    return permuted(value, lambda i: i + 4 if i & 4 else i - 4)


def after(value, *earlier):
    return lax.optimization_barrier((value, *earlier))[0]


def number(flag):
    return flag.astype(jnp.int32)


def own_entries(place, kept, block, local_blocks, keep):
    position = place[0]
    pair = position + 1 - 2 * (position % 2)
    level = (position // 4) % 2
    found = []
    for entry in range(keep):
        listed = kept[block, entry]
        device = listed // local_blocks
        offset = device - position
        near = jnp.abs(offset)
        side = 1 - (number(offset > 0) + level) % 2
        slot = jnp.where(near == 8, 4 + side, jnp.where(near == 4, 2 + side, number(device == pair)))
        lent = (near == 2) | ((near == 1) & (device != pair))
        slot = jnp.where(lent, 0, slot)
        bias = jnp.where(lent, jnp.float32(MASKED), jnp.float32(0))
        found.append((slot, pl.multiple_of((listed % local_blocks) * BLOCK, BLOCK), bias))
    return found


def lent_entries(place, kept, block, local_blocks, keep):
    position = place[0]
    client = position + 2 - 4 * ((position // 2) % 2)
    pair = position + 1 - 2 * (position % 2)
    client_pair = client + 1 - 2 * (client % 2)
    found = []
    for entry in range(keep):
        listed = kept[block, entry]
        device = listed // local_blocks
        near = jnp.abs(device - client)
        lent = (near == 2) | ((near == 1) & (device != client_pair))
        slot = jnp.where(near == 2, number(device != position), 2 + number(device != pair))
        slot = jnp.where(lent, slot, 0)
        bias = jnp.where(lent, jnp.float32(0), jnp.float32(MASKED))
        found.append((slot, pl.multiple_of((listed % local_blocks) * BLOCK, BLOCK), bias))
    return found


def weigh_block(query, keys, lanes, found):
    gathered = jnp.concatenate(
        [keys[slot, pl.ds(row, BLOCK), lanes] for slot, row, _ in found], axis=0
    )
    scores = lax.dot_general(
        query, gathered, (((1,), (1,)), ((), ())), preferred_element_type=jnp.float32
    )
    bias = jnp.concatenate([jnp.full((1, BLOCK), part, jnp.float32) for _, _, part in found], axis=1)
    scores = scores + bias
    top = jnp.max(scores, axis=1, keepdims=True)
    weight = jnp.exp2((scores - top) * SCALE)
    total = jnp.sum(weight, axis=1, keepdims=True)
    return top, total, weight.astype(jnp.bfloat16)


def sum_block(weight, values, lanes, found):
    gathered = jnp.concatenate(
        [values[slot, pl.ds(row, BLOCK), lanes] for slot, row, _ in found], axis=0
    )
    return jnp.dot(weight, gathered, preferred_element_type=jnp.float32)


def copied(sources, target, sems, lanes):
    copies = []
    for index, source in enumerate(sources):
        copies.append(
            pltpu.make_async_copy(source.at[:, lanes], target.at[index, :, lanes], sems.at[index])
        )
        copies[-1].start()
    return copies


def score_kernel(
    entries, local_blocks, keep, groups, tile_count, place, kept, queries, *refs
):
    key_tiles, near = refs[:tile_count], refs[tile_count:-6]
    weights, stats, values, keys, key_sems, value_sems = refs[-6:]
    copies = []
    for group, (first, count) in enumerate(groups):
        copies.append(copied(key_tiles, keys, key_sems.at[group], pl.ds(first * DH, count * DH)))
    value_copies = copied(near, values, value_sems, pl.ds(0, queries.shape[1]))
    found = [entries(place, kept, block, local_blocks, keep) for block in range(local_blocks)]
    for (first, count), arriving in zip(groups, copies):
        for copy in arriving:
            copy.wait()
        for head in range(first, first + count):
            lanes = pl.ds(head * DH, DH)
            for block in range(local_blocks):
                rows = pl.ds(block * BLOCK, BLOCK)
                top, total, weight = weigh_block(queries[rows, lanes], keys, lanes, found[block])
                weights[head, rows, :] = weight
                stats[0, rows, pl.ds(head, 1)] = top
                stats[1, rows, pl.ds(head, 1)] = total
    for copy in value_copies:
        copy.wait()


def lent_kernel(local_blocks, keep, groups, place, kept, weights, stats, *refs):
    tiles, (attended, values, sems) = refs[:LENT_TILES], refs[LENT_TILES:]
    copies = []
    for group, (first, count) in enumerate(groups):
        copies.append(copied(tiles, values, sems.at[group], pl.ds(first * DH, count * DH)))
    found = [lent_entries(place, kept, block, local_blocks, keep) for block in range(local_blocks)]
    shares = []
    for block in range(local_blocks):
        shares.append(1.0 / stats[1, pl.ds(block * BLOCK, BLOCK), :])
    for (first, count), arriving in zip(groups, copies):
        for copy in arriving:
            copy.wait()
        for head in range(first, first + count):
            lanes = pl.ds(head * DH, DH)
            for block in range(local_blocks):
                rows = pl.ds(block * BLOCK, BLOCK)
                numerator = sum_block(weights[head, rows, :], values, lanes, found[block])
                share = shares[block][:, head : head + 1]
                attended[rows, lanes] = (numerator * share).astype(jnp.bfloat16)


def value_kernel(local_blocks, keep, begin, groups, place, kept, weights, own, lent, *refs):
    borrowed, far = refs[1], refs[2 : 2 + len(FAR)]
    attended, values, result, far_sems, out_sems = refs[-5:]
    copies = []
    for group, (first, count) in enumerate(groups):
        lanes = pl.ds(first * DH, count * DH)
        part = pl.ds((first - begin) * DH, count * DH)
        copies.append([])
        for index, (slot, tile) in enumerate(zip(FAR, far)):
            copies[-1].append(
                pltpu.make_async_copy(
                    tile.at[:, part], values.at[slot, :, lanes], far_sems.at[group, index]
                )
            )
            copies[-1][-1].start()
    found = [own_entries(place, kept, block, local_blocks, keep) for block in range(local_blocks)]
    shares = []
    for block in range(local_blocks):
        rows = pl.ds(block * BLOCK, BLOCK)
        top = jnp.maximum(own[0, rows, :], lent[0, rows, :])
        own_scale = jnp.exp2((own[0, rows, :] - top) * SCALE)
        lent_total = lent[1, rows, :] * jnp.exp2((lent[0, rows, :] - top) * SCALE)
        total = own[1, rows, :] * own_scale + lent_total
        shares.append((own_scale / total, lent_total / total))
    leaving = []
    for group, (first, count) in enumerate(groups):
        for copy in copies[group]:
            copy.wait()
        for head in range(first, first + count):
            lanes = pl.ds(head * DH, DH)
            for block in range(local_blocks):
                rows = pl.ds(block * BLOCK, BLOCK)
                own_share, lent_share = (share[:, head : head + 1] for share in shares[block])
                numerator = sum_block(weights[head, rows, :], values, lanes, found[block])
                whole = numerator * own_share
                whole = whole + borrowed[rows, lanes].astype(jnp.float32) * lent_share
                result[rows, pl.ds((head - begin) * DH, DH)] = whole.astype(jnp.bfloat16)
        leaving.append(
            pltpu.make_async_copy(
                result.at[:, pl.ds((first - begin) * DH, count * DH)],
                attended.at[:, pl.ds(first * DH, count * DH)],
                out_sems.at[group],
            )
        )
        leaving[-1].start()
    for copy in leaving:
        copy.wait()


def in_vmem(arrays):
    return [pltpu.with_memory_space_constraint(array, pltpu.VMEM) for array in arrays]


def in_hbm(arrays):
    return [pltpu.with_memory_space_constraint(array, pltpu.HBM) for array in arrays]


SCALARS = pl.BlockSpec(memory_space=pltpu.SMEM)
HELD = pl.BlockSpec(memory_space=pltpu.VMEM)
ANYWHERE = pl.BlockSpec(memory_space=pl.ANY)


def cost(kept, heads, products, exponentials):
    pairs = kept.shape[0] * kept.shape[1] * heads * BLOCK * BLOCK
    return pl.CostEstimate(
        flops=2 * products * pairs * DH,
        bytes_accessed=2 * products * pairs,
        transcendentals=exponentials * pairs,
    )


def weigh(entries, place, kept, queries, tiles, near, stacked, groups, name):
    rows, columns = queries.shape
    heads = columns // DH
    return pl.pallas_call(
        functools.partial(score_kernel, entries, *kept.shape, groups, len(tiles)),
        out_shape=(
            pltpu.VMEM((heads, rows, kept.shape[1] * BLOCK), jnp.bfloat16),
            pltpu.VMEM((2, rows, LANES), jnp.float32),
            pltpu.VMEM((stacked, rows, columns), jnp.bfloat16),
        ),
        in_specs=[SCALARS, SCALARS, HELD] + [ANYWHERE] * (len(tiles) + len(near)),
        out_specs=(HELD, HELD, HELD),
        scratch_shapes=[
            pltpu.VMEM((len(tiles), rows, columns), jnp.bfloat16),
            pltpu.SemaphoreType.DMA((len(groups), len(tiles))),
            pltpu.SemaphoreType.DMA((max(1, len(near)),)),
        ],
        compiler_params=pltpu.CompilerParams(vmem_limit_bytes=14 * 1024 * 1024),
        cost_estimate=cost(kept, heads, 1, 1),
        name=name,
    )(place, kept, *in_vmem((queries,)), *in_hbm((*tiles, *near)))


def sum_lent(place, kept, weights, stats, tiles, groups):
    heads, rows, _ = weights.shape
    return pl.pallas_call(
        functools.partial(lent_kernel, *kept.shape, groups),
        out_shape=jax.ShapeDtypeStruct((rows, heads * DH), jnp.bfloat16),
        in_specs=[SCALARS, SCALARS, HELD, HELD] + [ANYWHERE] * LENT_TILES,
        out_specs=HELD,
        scratch_shapes=[
            pltpu.VMEM((LENT_TILES, rows, heads * DH), jnp.bfloat16),
            pltpu.SemaphoreType.DMA((len(groups), LENT_TILES)),
        ],
        compiler_params=pltpu.CompilerParams(vmem_limit_bytes=10 * 1024 * 1024),
        cost_estimate=cost(kept, heads, 1, 0),
        name="sum_lent",
    )(place, kept, *in_vmem((weights, stats)), *in_hbm(tiles))


def combine(place, kept, weights, own, lent, values, borrowed, far, begin, groups, before):
    heads, rows, _ = weights.shape
    operands = [place, kept, *in_vmem((weights, own, lent, values, borrowed)), *far]
    in_specs = [SCALARS, SCALARS] + [HELD] * 5 + [ANYWHERE] * len(far)
    aliases = {5: 1}
    if before is not None:
        aliases[len(operands)] = 0
        operands.append(before)
        in_specs.append(ANYWHERE)
    count = sum(count for _, count in groups)
    return pl.pallas_call(
        functools.partial(value_kernel, *kept.shape, begin, groups),
        out_shape=(
            jax.ShapeDtypeStruct((rows, heads * DH), jnp.bfloat16),
            pltpu.VMEM(values.shape, values.dtype),
        ),
        in_specs=in_specs,
        out_specs=(ANYWHERE, HELD),
        input_output_aliases=aliases,
        scratch_shapes=[
            pltpu.VMEM((rows, count * DH), jnp.bfloat16),
            pltpu.SemaphoreType.DMA((len(groups), len(FAR))),
            pltpu.SemaphoreType.DMA((len(groups),)),
        ],
        compiler_params=pltpu.CompilerParams(vmem_limit_bytes=6 * 1024 * 1024),
        cost_estimate=cost(kept, count, 1, 0),
        name=f"combine_{begin}",
    )(*operands)


def grouped(begin, count, size):
    return [(first, min(size, begin + count - first)) for first in range(begin, begin + count, size)]


def per_device(queries, keys, values, kept):
    position = lax.axis_index("blk").astype(jnp.int32)
    place = position.reshape(1)
    same_side = (position // 2) % 2 == (position // 4) % 2
    heads = queries.shape[1] // DH
    groups = grouped(0, heads, GROUP)

    k_odd, k_even = swapped_odd(keys), swapped(keys, 4)
    asked, asked_kept = swapped(queries, 2), swapped(kept, 2)
    later = after(values, asked_kept)
    v_odd, v_even = swapped_odd(later), swapped(later, 4)
    k_odd_far, k_even_far = swapped_odd(k_even), swapped(k_odd, 4)
    k_level = jnp.where(same_side, k_even, k_odd)
    v_level = jnp.where(same_side, v_even, v_odd)
    k_pair, k_pair_level = swapped(after(keys, k_level), 1), swapped(k_level, 1)
    v_pair, v_pair_level = swapped(after(values, v_level), 1), swapped(v_level, 1)
    lent_weights, lent_stats, _ = weigh(
        lent_entries, place, asked_kept, asked, (keys, k_level, k_pair, k_pair_level), (), 1,
        groups, "weigh_lent",
    )
    lent = swapped(lent_stats, 2)
    answer = sum_lent(
        place, asked_kept, lent_weights, lent_stats, (values, v_level, v_pair, v_pair_level), groups
    )
    borrowed = swapped(after(answer, lent), 2)
    weights, own, staged = weigh(
        own_entries, place, kept, after(queries, answer),
        (keys, k_pair, k_even, k_odd, k_even_far, k_odd_far),
        (values, v_pair, v_even, v_odd), OWN_TILES, groups, "weigh_own",
    )
    attended, begin, hold = None, 0, lent
    hops = []
    for count in VALUE_SPLIT:
        lanes = slice(begin * DH, (begin + count) * DH)
        hops.append(
            (swapped(after(v_odd[:, lanes], hold), 4), swapped_odd(after(v_even[:, lanes], hold)))
        )
        begin, hold = begin + count, own
    begin = 0
    for count, far in zip(VALUE_SPLIT, hops):
        attended, staged = combine(
            place, kept, weights, own, lent, staged, borrowed, far,
            begin, grouped(begin, count, GROUP), attended,
        )
        begin += count
    return attended


def solution(mesh):
    placed = P(("clip", "blk"), None)
    return jax.shard_map(
        per_device, mesh=mesh, in_specs=(placed,) * 4, out_specs=placed, check_vma=False
    )
```

time: 142 us -> 128 us (0.901)
  waiting for transfers between devices: 84.8 us -> 60.2 us
  local copies, waits for them, and re-layouts: 0.01 us -> 7.38 us
  Pallas kernels: 22.9 us -> 30.1 us
  other arithmetic: 5.41 us -> 2.95 us
  starting transfers between devices: 27.7 us -> 26.2 us
    ppermute x16 -> x18, waiting for transfers between devices: 84.8 us -> 60.2 us  [permuted(): lax.ppermute(value, 'blk', [(i, t) for i, t in pairs if 0 <= t < count])]
    pallas_call x2 -> x5, Pallas kernels: 22.9 us -> 30.1 us  [the longest x2 17.8 us: weigh(): pl.pallas_call(functools.partial(score_kernel, entries, *kept.shape, grou...]
    unnamed x6 -> x26, local copies, waits for them, and re-layouts: 0.01 us -> 4.91 us
    slice x0 -> x4, local copies, waits for them, and re-layouts: none -> 2.48 us  [the longest x2 2.38 us: per_device(): v_even[:, lanes]]
    select_n x4 -> x2, other arithmetic: 5.41 us -> 2.95 us  [the longest x1 1.49 us: per_device(): v_level = jnp.where(same_side, v_even, v_odd)]
    ppermute x16 -> x18, starting transfers between devices: 27.7 us -> 26.2 us  [permuted(): lax.ppermute(value, 'blk', [(i, t) for i, t in pairs if 0 <= t < count])]
  transfers between devices with their start and end apart: 16 -> 18, of which waited for: 5 -> 6; matrix products, arithmetic and copies ran while one was open for 4% -> 4% of each run, Pallas kernels for 9% -> 22%
where the time goes in v4:
time: 128 us; the launch traced here: 127 us
  waiting for transfers between devices  60.2 us (47%)
  Pallas kernels  30.1 us (24%)
  starting transfers between devices  26.2 us (20%)
  local copies, waits for them, and re-layouts  7.38 us (6%)
  other arithmetic  2.95 us (2%)
    ppermute x18, waiting for transfers between devices, permuted(): lax.ppermute(value, 'blk', [(i, t) for i, t in pairs if 0 <= t < count])  60.2 us
    ppermute x18, starting transfers between devices, permuted(): lax.ppermute(value, 'blk', [(i, t) for i, t in pairs if 0 <= t < count])  26.2 us
    pallas_call x2, Pallas kernels, weigh(): pl.pallas_call(functools.partial(score_kernel, entries, *kept.shape, grou...  17.8 us
    pallas_call x2, Pallas kernels, combine(): pl.pallas_call(functools.partial(value_kernel, *kept.shape, begin, groups...  6.93 us
    pallas_call x1, Pallas kernels, sum_lent(): pl.pallas_call(functools.partial(lent_kernel, *kept.shape, groups), out_s...  5.38 us
    unnamed x26, local copies, waits for them, and re-layouts  4.91 us
  transfers between devices with their start and end apart: 18, of which 6 were waited for; matrix products, arithmetic and copies ran while one was open for 4% of the time, Pallas kernels for 22%

profile of v4, /device:TPU:0, one launch (start us, length us, event | category | flops | bytes accessed | tf_op | source)
XLA Modules:
  0.0 127.3 jit_solution(10801331910256585491)
XLA Ops:
  0.0 1.7 %collective-permute-start.3 = (bf16[256,2560]{1,0:T(8,128)(2,1)}, bf16[256,2560]{1,0:T(8,128)(2,1)}, u32[]{:S(2)}, u32[]{:S(2)}) collective-permute-start(bf16[256,2560]{1,0:T(8,128)(2,1)} %refs_0_.5), channel_id=1, source_target_pairs={{4,8},{5,9},{6,10},{7,11},{8,4},{9,5},{10,6},{11,7},{20,24},{21,25... | collective-permute-start | bytes 3932168 | tf_op jit(solution)/shard_map/ppermute | solution.py:26
  1.7 4.8 %collective-permute-start.2 = (bf16[256,2560]{1,0:T(8,128)(2,1)}, bf16[256,2560]{1,0:T(8,128)(2,1)}, u32[]{:S(2)}, u32[]{:S(2)}) collective-permute-start(bf16[256,2560]{1,0:T(8,128)(2,1)} %refs_0_.5), channel_id=1, source_target_pairs={{0,4},{1,5},{2,6},{3,7},{4,0},{5,1},{6,2},{7,3},{8,12},{9,13},{10,... | collective-permute-start | bytes 3932168 | tf_op jit(solution)/shard_map/ppermute | solution.py:26
  6.6 1.5 %collective-permute-start = (s32[2,8]{1,0:T(2,128)}, s32[2,8]{1,0:T(2,128)S(1)}, u32[]{:S(2)}, u32[]{:S(2)}) collective-permute-start(s32[2,8]{1,0:T(2,128)} %kept.5), channel_id=1, source_target_pairs={{0,2},{1,3},{2,0},{3,1},{4,6},{5,7},{6,4},{7,5},{8,10},{9,11},{10,... | collective-permute-start | bytes 200 | tf_op jit(solution)/shard_map/ppermute | solution.py:26
  8.1 2.3 %collective-permute-done.kept = s32[2,8]{1,0:T(2,128)S(1)} collective-permute-done((s32[2,8]{1,0:T(2,128)}, s32[2,8]{1,0:T(2,128)S(1)}, u32[]{:S(2)}, u32[]{:S(2)}) %collective-permute-start) | collective-permute-done | bytes 96 | tf_op jit(solution)/shard_map/ppermute | solution.py:26
  10.4 0.7 collective-permute-start.7
  11.1 2.6 %collective-permute-start.6 = (bf16[256,2560]{1,0:T(8,128)(2,1)}, bf16[256,2560]{1,0:T(8,128)(2,1)}, u32[]{:S(2)}, u32[]{:S(2)}) collective-permute-start(bf16[256,2560]{1,0:T(8,128)(2,1)} %refs_6_.1), channel_id=1, source_target_pairs={{0,4},{1,5},{2,6},{3,7},{4,0},{5,1},{6,2},{7,3},{8,12},{9,13},{10,... | collective-permute-start | bytes 3932168 | tf_op jit(solution)/shard_map/ppermute | solution.py:26
  13.7 1.5 %collective-permute-start.1 = (bf16[256,2560]{1,0:T(8,128)(2,1)}, bf16[256,2560]{1,0:T(8,128)(2,1)S(1)}, u32[]{:S(2)}, u32[]{:S(2)}) collective-permute-start(bf16[256,2560]{1,0:T(8,128)(2,1)} %queries), channel_id=1, source_target_pairs={{0,2},{1,3},{2,0},{3,1},{4,6},{5,7},{6,4},{7,5},{8,10},{9,11},{10,... | collective-permute-start | bytes 3932168 | tf_op jit(solution)/shard_map/ppermute | solution.py:26
  15.2 21.3 %collective-permute-done.2.refs_2_ = bf16[256,2560]{1,0:T(8,128)(2,1)} collective-permute-done((bf16[256,2560]{1,0:T(8,128)(2,1)}, bf16[256,2560]{1,0:T(8,128)(2,1)}, u32[]{:S(2)}, u32[]{:S(2)}) %collective-permute-start.2) | collective-permute-done | bytes 1310752 | tf_op jit(solution)/shard_map/ppermute | solution.py:26
  36.5 1.5 %broadcast_select_fusion.1.refs_1_ = bf16[256,2560]{1,0:T(8,128)(2,1)S(1)} fusion(bf16[256,2560]{1,0:T(8,128)(2,1)} %collective-permute-done.2.refs_2_, bf16[256,2560]{1,0:T(8,128)(2,1)} %collective-permute-done.3.refs_3_, pred[]{:T(512)S(6)} %eq.6), kind=kLoop, calls=%fused_computation.1 | loop fusion | flops 655360 | bytes 3932161 | tf_op jit(solution)/shard_map/jit(_where)/select_n | solution.py:317
  38.6 24.9 %collective-permute-done.6.refs_8_ = bf16[256,2560]{1,0:T(8,128)(2,1)} collective-permute-done((bf16[256,2560]{1,0:T(8,128)(2,1)}, bf16[256,2560]{1,0:T(8,128)(2,1)}, u32[]{:S(2)}, u32[]{:S(2)}) %collective-permute-start.6) | collective-permute-done | bytes 1310752 | tf_op jit(solution)/shard_map/ppermute | solution.py:26
  63.5 1.5 %broadcast_select_fusion.refs_1_ = bf16[256,2560]{1,0:T(8,128)(2,1)S(1)} fusion(bf16[256,2560]{1,0:T(8,128)(2,1)} %collective-permute-done.6.refs_8_, bf16[256,2560]{1,0:T(8,128)(2,1)S(1)} %collective-permute-done.7.refs_9_, pred[]{:T(512)S(6)} %eq.6), kind=kLoop, calls=%fused_computation | loop fusion | flops 655360 | bytes 3932161 | tf_op jit(solution)/shard_map/jit(_where)/select_n | solution.py:318
  66.0 0.7 collective-permute-start.11
  67.1 0.8 copy-done.12
  67.9 9.1 %weigh_lent.1 = (bf16[20,256,1024]{2,1,0:T(8,128)(2,1)S(1)}, f32[2,256,128]{2,1,0:T(8,128)S(1)}, bf16[1,256,2560]{2,1,0:T(8,128)(2,1)}) custom-call(s32[1]{0:T(128)} %bitcast.place, s32[2,8]{1,0:T(2,128)S(1)} %collective-permute-done.kept, bf16[256,2560]{1,0:T(8,128)(2,1)S(1)} %collective-permute-done.1.queries, bf16[256,2560]{1,0:T(8,128)(2,1)} %refs_0_.5, ...), custom_call_target="tpu_custom_call" | custom-call | flops 1342177280 | bytes 10485760 | tf_op jit(solution)/shard_map/weigh_lent/pallas_call | solution.py:234
  77.0 2.9 %collective-permute-start.12 = (f32[2,256,128]{2,1,0:T(8,128)S(1)}, f32[2,256,128]{2,1,0:T(8,128)S(1)}, u32[]{:S(2)}, u32[]{:S(2)}) collective-permute-start(f32[2,256,128]{2,1,0:T(8,128)S(1)} %get-tuple-element.24.stats), channel_id=1, source_target_pairs={{0,2},{1,3},{2,0},{3,1},{4,6},{5,7},{6,4},{7,5},{8,10},{9,11},{10,... | collective-permute-start | bytes 786440 | tf_op jit(solution)/shard_map/ppermute | solution.py:26
  79.9 1.1 copy-done.4
  81.5 5.4 %sum_lent.1 = bf16[256,2560]{1,0:T(8,128)(2,1)S(1)} custom-call(s32[1]{0:T(128)} %bitcast.place, s32[2,8]{1,0:T(2,128)S(1)} %collective-permute-done.kept, bf16[20,256,1024]{2,1,0:T(8,128)(2,1)S(1)} %get-tuple-element.23.weights, f32[2,256,128]{2,1,0:T(8,128)S(1)} %get-tuple-element.24.stats, bf16[256,2560]{1,0:T(8,128)(2,1)} %refs_6_.1, ...), custom_call_target="tpu_custom_call" | custom-call | flops 1342177280 | bytes 10485760 | tf_op jit(solution)/shard_map/sum_lent/pallas_call | solution.py:256
  86.9 1.0 collective-permute-start.13
  88.0 1.4 %slice.17 = bf16[256,1920]{1,0:T(8,128)(2,1)S(1)} slice(bf16[256,2560]{1,0:T(8,128)(2,1)} %collective-permute-done.6.refs_8_), slice={[0:256], [0:1920]} | slice | bytes 1966080 | tf_op jit(solution)/shard_map/slice | solution.py:340
  89.4 2.6 %collective-permute-start.14 = (bf16[256,1920]{1,0:T(8,128)(2,1)S(1)}, bf16[256,1920]{1,0:T(8,128)(2,1)S(1)}, u32[]{:S(2)}, u32[]{:S(2)}) collective-permute-start(bf16[256,1920]{1,0:T(8,128)(2,1)S(1)} %slice.16), channel_id=1, source_target_pairs={{0,4},{1,5},{2,6},{3,7},{4,0},{5,1},{6,2},{7,3},{8,12},{9,13},{10,... | collective-permute-start | bytes 2949128 | tf_op jit(solution)/shard_map/ppermute | solution.py:26
  91.9 0.9 collective-permute-start.15
  92.9 1.0 slice.19
  93.9 3.5 %collective-permute-done.10.refs_4_ = bf16[256,2560]{1,0:T(8,128)(2,1)S(1)} collective-permute-done((bf16[256,2560]{1,0:T(8,128)(2,1)}, bf16[256,2560]{1,0:T(8,128)(2,1)S(1)}, u32[]{:S(2)}, u32[]{:S(2)}) %collective-permute-start.10) | collective-permute-done | bytes 1310752 | tf_op jit(solution)/shard_map/ppermute | solution.py:26
  97.4 1.1 copy-done.8
  98.5 1.1 copy-done.9
  99.6 8.8 %weigh_own.1 = (bf16[20,256,1024]{2,1,0:T(8,128)(2,1)S(1)}, f32[2,256,128]{2,1,0:T(8,128)S(1)}, bf16[6,256,2560]{2,1,0:T(8,128)(2,1)S(1)}) custom-call(s32[1]{0:T(128)} %bitcast.place, s32[2,8]{1,0:T(2,128)S(1)} %copy-done.1, bf16[256,2560]{1,0:T(8,128)(2,1)S(1)} %copy-done, bf16[256,2560]{1,0:T(8,128)(2,1)} %refs_0_.5, bf16[256,2560]{1,0:T(8,128)(2,1)} %copy-done.7, ...), custom_call_target="tpu_custom_call" | custom-call | flops 1342177280 | bytes 10485760 | tf_op jit(solution)/shard_map/weigh_own/pallas_call | solution.py:234
  108.4 3.0 %collective-permute-start.16 = (bf16[256,640]{1,0:T(8,128)(2,1)S(1)}, bf16[256,640]{1,0:T(8,128)(2,1)S(1)}, u32[]{:S(2)}, u32[]{:S(2)}) collective-permute-start(bf16[256,640]{1,0:T(8,128)(2,1)S(1)} %slice.18), channel_id=1, source_target_pairs={{0,4},{1,5},{2,6},{3,7},{4,0},{5,1},{6,2},{7,3},{8,12},{9,13},{10,... | collective-permute-start | bytes 983048 | tf_op jit(solution)/shard_map/ppermute | solution.py:26
  111.3 0.7 collective-permute-start.17
  112.0 6.5 %collective-permute-done.14.refs_2_ = bf16[256,1920]{1,0:T(8,128)(2,1)S(1)} collective-permute-done((bf16[256,1920]{1,0:T(8,128)(2,1)S(1)}, bf16[256,1920]{1,0:T(8,128)(2,1)S(1)}, u32[]{:S(2)}, u32[]{:S(2)}) %collective-permute-start.14) | collective-permute-done | bytes 983072 | tf_op jit(solution)/shard_map/ppermute | solution.py:26
  118.5 4.4 %combine_0.1 = (bf16[256,2560]{1,0:T(8,128)(2,1)}, bf16[6,256,2560]{2,1,0:T(8,128)(2,1)S(1)}) custom-call(s32[1]{0:T(128)} %bitcast.place, s32[2,8]{1,0:T(2,128)S(1)} %copy-done.1, bf16[20,256,1024]{2,1,0:T(8,128)(2,1)S(1)} %get-tuple-element.28.weights, f32[2,256,128]{2,1,0:T(8,128)S(1)} %get-tuple-element.29.own, ...), custom_call_target="tpu_custom_call", output_to_operand_aliasing={{1}: (5, {})} | custom-call | flops 1006632960 | bytes 7864320 | tf_op jit(solution)/shard_map/combine_0/pallas_call | solution.py:281
  122.9 1.7 %collective-permute-done.16.refs_2_ = bf16[256,640]{1,0:T(8,128)(2,1)S(1)} collective-permute-done((bf16[256,640]{1,0:T(8,128)(2,1)S(1)}, bf16[256,640]{1,0:T(8,128)(2,1)S(1)}, u32[]{:S(2)}, u32[]{:S(2)}) %collective-permute-start.16) | collective-permute-done | bytes 327712 | tf_op jit(solution)/shard_map/ppermute | solution.py:26
  124.6 2.5 %combine_15.1 = (bf16[256,2560]{1,0:T(8,128)(2,1)}, bf16[6,256,2560]{2,1,0:T(8,128)(2,1)S(1)}) custom-call(s32[1]{0:T(128)} %bitcast.place, s32[2,8]{1,0:T(2,128)S(1)} %copy-done.1, bf16[20,256,1024]{2,1,0:T(8,128)(2,1)S(1)} %get-tuple-element.28.weights, f32[2,256,128]{2,1,0:T(8,128)S(1)} %get-tuple-element.29.own, ...), custom_call_target="tpu_custom_call", output_to_operand_aliasing={{1}: (5, {}), {0}: (9, {})} | custom-call | flops 335544320 | bytes 2621440 | tf_op jit(solution)/shard_map/combine_15/pallas_call | solution.py:281
  (41 shorter events, 2.5 us)
Async XLA Ops:
  0.0 15.2 %collective-permute-start.3 = (bf16[256,2560]{1,0:T(8,128)(2,1)}, bf16[256,2560]{1,0:T(8,128)(2,1)}, u32[]{:S(2)}, u32[]{:S(2)}) collective-permute-start(bf16[256,2560]{1,0:T(8,128)(2,1)} %refs_0_.5), channel_id=1, source_target_pairs={{4,8},{5,9},{6,10},{7,11},{8,4},{9,5},{10,6},{11,7},{20,24},{21,25... | collective-permute-start | bytes 3932168 | tf_op jit(solution)/shard_map/ppermute | solution.py:26
  1.7 34.8 %collective-permute-start.2 = (bf16[256,2560]{1,0:T(8,128)(2,1)}, bf16[256,2560]{1,0:T(8,128)(2,1)}, u32[]{:S(2)}, u32[]{:S(2)}) collective-permute-start(bf16[256,2560]{1,0:T(8,128)(2,1)} %refs_0_.5), channel_id=1, source_target_pairs={{0,4},{1,5},{2,6},{3,7},{4,0},{5,1},{6,2},{7,3},{8,12},{9,13},{10,... | collective-permute-start | bytes 3932168 | tf_op jit(solution)/shard_map/ppermute | solution.py:26
  6.6 3.8 %collective-permute-start = (s32[2,8]{1,0:T(2,128)}, s32[2,8]{1,0:T(2,128)S(1)}, u32[]{:S(2)}, u32[]{:S(2)}) collective-permute-start(s32[2,8]{1,0:T(2,128)} %kept.5), channel_id=1, source_target_pairs={{0,2},{1,3},{2,0},{3,1},{4,6},{5,7},{6,4},{7,5},{8,10},{9,11},{10,... | collective-permute-start | bytes 200 | tf_op jit(solution)/shard_map/ppermute | solution.py:26
  10.4 28.2 %collective-permute-start.7 = (bf16[256,2560]{1,0:T(8,128)(2,1)}, bf16[256,2560]{1,0:T(8,128)(2,1)S(1)}, u32[]{:S(2)}, u32[]{:S(2)}) collective-permute-start(bf16[256,2560]{1,0:T(8,128)(2,1)} %refs_6_.1), channel_id=1, source_target_pairs={{4,8},{5,9},{6,10},{7,11},{8,4},{9,5},{10,6},{11,7},{20,24},{21,25... | collective-permute-start | bytes 3932168 | tf_op jit(solution)/shard_map/ppermute | solution.py:26
  11.1 52.4 %collective-permute-start.6 = (bf16[256,2560]{1,0:T(8,128)(2,1)}, bf16[256,2560]{1,0:T(8,128)(2,1)}, u32[]{:S(2)}, u32[]{:S(2)}) collective-permute-start(bf16[256,2560]{1,0:T(8,128)(2,1)} %refs_6_.1), channel_id=1, source_target_pairs={{0,4},{1,5},{2,6},{3,7},{4,0},{5,1},{6,2},{7,3},{8,12},{9,13},{10,... | collective-permute-start | bytes 3932168 | tf_op jit(solution)/shard_map/ppermute | solution.py:26
  13.7 51.9 %collective-permute-start.1 = (bf16[256,2560]{1,0:T(8,128)(2,1)}, bf16[256,2560]{1,0:T(8,128)(2,1)S(1)}, u32[]{:S(2)}, u32[]{:S(2)}) collective-permute-start(bf16[256,2560]{1,0:T(8,128)(2,1)} %queries), channel_id=1, source_target_pairs={{0,2},{1,3},{2,0},{3,1},{4,6},{5,7},{6,4},{7,5},{8,10},{9,11},{10,... | collective-permute-start | bytes 3932168 | tf_op jit(solution)/shard_map/ppermute | solution.py:26
  15.2 22.9 %copy-start.6 = (bf16[256,2560]{1,0:T(8,128)(2,1)S(1)}, bf16[256,2560]{1,0:T(8,128)(2,1)}, u32[]{:S(2)}) copy-start(bf16[256,2560]{1,0:T(8,128)(2,1)} %refs_0_.5) | copy-start | bytes 3932164
  38.0 27.0 %copy-start.10 = (bf16[256,2560]{1,0:T(8,128)(2,1)}, bf16[256,2560]{1,0:T(8,128)(2,1)S(1)}, u32[]{:S(2)}) copy-start(bf16[256,2560]{1,0:T(8,128)(2,1)S(1)} %broadcast_select_fusion.1.refs_1_) | copy-start | bytes 3932164
  38.0 27.0 %copy-start.3 = (bf16[256,2560]{1,0:T(8,128)(2,1)S(1)}, bf16[256,2560]{1,0:T(8,128)(2,1)}, u32[]{:S(2)}) copy-start(bf16[256,2560]{1,0:T(8,128)(2,1)} %refs_6_.1) | copy-start | bytes 3932164
  38.0 28.7 %collective-permute-start.5 = (bf16[256,2560]{1,0:T(8,128)(2,1)S(1)}, bf16[256,2560]{1,0:T(8,128)(2,1)S(1)}, u32[]{:S(2)}, u32[]{:S(2)}) collective-permute-start(bf16[256,2560]{1,0:T(8,128)(2,1)S(1)} %broadcast_select_fusion.1.refs_1_), channel_id=1, source_target_pairs={{0,1},{1,0},{2,3},{3,2},{4,5},{5,4},{6,7},{7,6},{8,9},{9,8},{10,11... | collective-permute-start | bytes 3932168 | tf_op jit(solution)/shard_map/ppermute | solution.py:26
  38.1 27.9 %collective-permute-start.4 = (bf16[256,2560]{1,0:T(8,128)(2,1)S(1)}, bf16[256,2560]{1,0:T(8,128)(2,1)S(1)}, u32[]{:S(2)}, u32[]{:S(2)}) collective-permute-start(bf16[256,2560]{1,0:T(8,128)(2,1)S(1)} %copy-done.6), channel_id=1, source_target_pairs={{0,1},{1,0},{2,3},{3,2},{4,5},{5,4},{6,7},{7,6},{8,9},{9,8},{10,11... | collective-permute-start | bytes 3932168 | tf_op jit(solution)/shard_map/ppermute | solution.py:26
  38.6 54.2 %copy-start.2 = (bf16[256,2560]{1,0:T(8,128)(2,1)}, bf16[256,2560]{1,0:T(8,128)(2,1)S(1)}, u32[]{:S(2)}) copy-start(bf16[256,2560]{1,0:T(8,128)(2,1)S(1)} %collective-permute-done.7.refs_9_) | copy-start | bytes 3932164
  65.0 12.0 %copy-start.5 = (bf16[256,2560]{1,0:T(8,128)(2,1)}, bf16[256,2560]{1,0:T(8,128)(2,1)S(1)}, u32[]{:S(2)}) copy-start(bf16[256,2560]{1,0:T(8,128)(2,1)S(1)} %broadcast_select_fusion.refs_1_) | copy-start | bytes 3932164
  65.0 14.9 %collective-permute-start.8 = (bf16[256,2560]{1,0:T(8,128)(2,1)S(1)}, bf16[256,2560]{1,0:T(8,128)(2,1)S(1)}, u32[]{:S(2)}, u32[]{:S(2)}) collective-permute-start(bf16[256,2560]{1,0:T(8,128)(2,1)S(1)} %copy-done.3), channel_id=1, source_target_pairs={{0,1},{1,0},{2,3},{3,2},{4,5},{5,4},{6,7},{7,6},{8,9},{9,8},{10,11... | collective-permute-start | bytes 3932168 | tf_op jit(solution)/shard_map/ppermute | solution.py:26
  65.1 14.8 %collective-permute-start.9 = (bf16[256,2560]{1,0:T(8,128)(2,1)S(1)}, bf16[256,2560]{1,0:T(8,128)(2,1)S(1)}, u32[]{:S(2)}, u32[]{:S(2)}) collective-permute-start(bf16[256,2560]{1,0:T(8,128)(2,1)S(1)} %broadcast_select_fusion.refs_1_), channel_id=1, source_target_pairs={{0,1},{1,0},{2,3},{3,2},{4,5},{5,4},{6,7},{7,6},{8,9},{9,8},{10,11... | collective-permute-start | bytes 3932168 | tf_op jit(solution)/shard_map/ppermute | solution.py:26
  65.6 31.8 %collective-permute-start.10 = (bf16[256,2560]{1,0:T(8,128)(2,1)}, bf16[256,2560]{1,0:T(8,128)(2,1)S(1)}, u32[]{:S(2)}, u32[]{:S(2)}) collective-permute-start(bf16[256,2560]{1,0:T(8,128)(2,1)} %collective-permute-done.3.refs_3_), channel_id=1, source_target_pairs={{0,4},{1,5},{2,6},{3,7},{4,0},{5,1},{6,2},{7,3},{8,12},{9,13},{10,... | collective-permute-start | bytes 3932168 | tf_op jit(solution)/shard_map/ppermute | solution.py:26
  66.0 1.1 copy-start.7
  66.0 31.4 %collective-permute-start.11 = (bf16[256,2560]{1,0:T(8,128)(2,1)}, bf16[256,2560]{1,0:T(8,128)(2,1)S(1)}, u32[]{:S(2)}, u32[]{:S(2)}) collective-permute-start(bf16[256,2560]{1,0:T(8,128)(2,1)} %collective-permute-done.2.refs_2_), channel_id=1, source_target_pairs={{4,8},{5,9},{6,10},{7,11},{8,4},{9,5},{10,6},{11,7},{20,24},{21,25... | collective-permute-start | bytes 3932168 | tf_op jit(solution)/shard_map/ppermute | solution.py:26
  66.8 1.1 copy-start.12
  77.0 9.9 %collective-permute-start.12 = (f32[2,256,128]{2,1,0:T(8,128)S(1)}, f32[2,256,128]{2,1,0:T(8,128)S(1)}, u32[]{:S(2)}, u32[]{:S(2)}) collective-permute-start(f32[2,256,128]{2,1,0:T(8,128)S(1)} %get-tuple-element.24.stats), channel_id=1, source_target_pairs={{0,2},{1,3},{2,0},{3,1},{4,6},{5,7},{6,4},{7,5},{8,10},{9,11},{10,... | collective-permute-start | bytes 786440 | tf_op jit(solution)/shard_map/ppermute | solution.py:26
  79.9 1.1 copy-start.4
  79.9 1.6 %copy-start.11 = (bf16[256,2560]{1,0:T(8,128)(2,1)}, bf16[256,2560]{1,0:T(8,128)(2,1)S(1)}, u32[]{:S(2)}) copy-start(bf16[256,2560]{1,0:T(8,128)(2,1)S(1)} %collective-permute-done.9.refs_3_) | copy-start | bytes 3932164
  86.9 31.6 %collective-permute-start.13 = (bf16[256,2560]{1,0:T(8,128)(2,1)S(1)}, bf16[256,2560]{1,0:T(8,128)(2,1)S(1)}, u32[]{:S(2)}, u32[]{:S(2)}) collective-permute-start(bf16[256,2560]{1,0:T(8,128)(2,1)S(1)} %sum_lent.1), channel_id=1, source_target_pairs={{0,2},{1,3},{2,0},{3,1},{4,6},{5,7},{6,4},{7,5},{8,10},{9,11},{10,... | collective-permute-start | bytes 3932168 | tf_op jit(solution)/shard_map/ppermute | solution.py:26
  88.0 11.7 %copy-start = (bf16[256,2560]{1,0:T(8,128)(2,1)S(1)}, bf16[256,2560]{1,0:T(8,128)(2,1)}, u32[]{:S(2)}) copy-start(bf16[256,2560]{1,0:T(8,128)(2,1)} %queries) | copy-start | bytes 3932164
  88.0 11.6 %copy-start.1 = (s32[2,8]{1,0:T(2,128)S(1)}, s32[2,8]{1,0:T(2,128)}, u32[]{:S(2)}) copy-start(s32[2,8]{1,0:T(2,128)} %kept.5) | copy-start | bytes 196
  89.4 29.1 %collective-permute-start.14 = (bf16[256,1920]{1,0:T(8,128)(2,1)S(1)}, bf16[256,1920]{1,0:T(8,128)(2,1)S(1)}, u32[]{:S(2)}, u32[]{:S(2)}) collective-permute-start(bf16[256,1920]{1,0:T(8,128)(2,1)S(1)} %slice.16), channel_id=1, source_target_pairs={{0,4},{1,5},{2,6},{3,7},{4,0},{5,1},{6,2},{7,3},{8,12},{9,13},{10,... | collective-permute-start | bytes 2949128 | tf_op jit(solution)/shard_map/ppermute | solution.py:26
  91.9 26.6 %collective-permute-start.15 = (bf16[256,1920]{1,0:T(8,128)(2,1)S(1)}, bf16[256,1920]{1,0:T(8,128)(2,1)S(1)}, u32[]{:S(2)}, u32[]{:S(2)}) collective-permute-start(bf16[256,1920]{1,0:T(8,128)(2,1)S(1)} %slice.17), channel_id=1, source_target_pairs={{4,8},{5,9},{6,10},{7,11},{8,4},{9,5},{10,6},{11,7},{20,24},{21,25... | collective-permute-start | bytes 2949128 | tf_op jit(solution)/shard_map/ppermute | solution.py:26
  97.4 1.1 copy-start.8
  98.5 1.1 copy-start.9
  108.4 16.3 %collective-permute-start.16 = (bf16[256,640]{1,0:T(8,128)(2,1)S(1)}, bf16[256,640]{1,0:T(8,128)(2,1)S(1)}, u32[]{:S(2)}, u32[]{:S(2)}) collective-permute-start(bf16[256,640]{1,0:T(8,128)(2,1)S(1)} %slice.18), channel_id=1, source_target_pairs={{0,4},{1,5},{2,6},{3,7},{4,0},{5,1},{6,2},{7,3},{8,12},{9,13},{10,... | collective-permute-start | bytes 983048 | tf_op jit(solution)/shard_map/ppermute | solution.py:26
  111.3 13.3 %collective-permute-start.17 = (bf16[256,640]{1,0:T(8,128)(2,1)S(1)}, bf16[256,640]{1,0:T(8,128)(2,1)S(1)}, u32[]{:S(2)}, u32[]{:S(2)}) collective-permute-start(bf16[256,640]{1,0:T(8,128)(2,1)S(1)} %slice.19), channel_id=1, source_target_pairs={{4,8},{5,9},{6,10},{7,11},{8,4},{9,5},{10,6},{11,7},{20,24},{21,25... | collective-permute-start | bytes 983048 | tf_op jit(solution)/shard_map/ppermute | solution.py:26

commit v5 on v4

--- a/solution.py
+++ b/solution.py
@@ -101,25 +101,38 @@
     return jnp.dot(weight, gathered, preferred_element_type=jnp.float32)
 
 
-def copied(sources, target, sems, lanes):
+def copied(sources, target, sems, run, begin=0, slots=None):
+    first, count = run
     copies = []
-    for index, source in enumerate(sources):
-        copies.append(
-            pltpu.make_async_copy(source.at[:, lanes], target.at[index, :, lanes], sems.at[index])
-        )
-        copies[-1].start()
+    for index, pieces in enumerate(sources):
+        slot, start = index if slots is None else slots[index], (first - begin) * DH
+        for piece in pieces:
+            if 0 <= start < piece.shape[1]:
+                copies.append(
+                    pltpu.make_async_copy(
+                        piece.at[:, pl.ds(start, count * DH)],
+                        target.at[slot, :, pl.ds(first * DH, count * DH)],
+                        sems.at[index],
+                    )
+                )
+                copies[-1].start()
+            start = start - piece.shape[1]
     return copies
 
 
 def score_kernel(
-    entries, local_blocks, keep, groups, tile_count, place, kept, queries, *refs
+    entries, local_blocks, keep, groups, pieces, place, kept, queries, *refs
 ):
-    key_tiles, near = refs[:tile_count], refs[tile_count:-6]
+    key_tiles, taken = [], 0
+    for piece_count in pieces:
+        key_tiles.append(refs[taken : taken + piece_count])
+        taken += piece_count
+    near = [(tile,) for tile in refs[taken:-6]]
     weights, stats, values, keys, key_sems, value_sems = refs[-6:]
     copies = []
     for group, (first, count) in enumerate(groups):
-        copies.append(copied(key_tiles, keys, key_sems.at[group], pl.ds(first * DH, count * DH)))
-    value_copies = copied(near, values, value_sems, pl.ds(0, queries.shape[1]))
+        copies.append(copied(key_tiles, keys, key_sems.at[group], (first, count)))
+    value_copies = copied(near, values, value_sems, (0, queries.shape[1] // DH))
     found = [entries(place, kept, block, local_blocks, keep) for block in range(local_blocks)]
     for (first, count), arriving in zip(groups, copies):
         for copy in arriving:
@@ -136,16 +149,17 @@
         copy.wait()
 
 
-def lent_kernel(local_blocks, keep, groups, place, kept, weights, stats, *refs):
-    tiles, (attended, values, sems) = refs[:LENT_TILES], refs[LENT_TILES:]
+def lent_kernel(local_blocks, keep, groups, taken, place, kept, weights, stats, *refs):
+    tiles, answers, (values, sems) = refs[:taken], refs[taken:-2], refs[-2:]
+    tiles = [(tile,) for tile in tiles[: LENT_TILES - 1]] + [tiles[LENT_TILES - 1 :]]
     copies = []
-    for group, (first, count) in enumerate(groups):
-        copies.append(copied(tiles, values, sems.at[group], pl.ds(first * DH, count * DH)))
+    for group, run in enumerate(groups):
+        copies.append(copied(tiles, values, sems.at[group], run))
     found = [lent_entries(place, kept, block, local_blocks, keep) for block in range(local_blocks)]
     shares = []
     for block in range(local_blocks):
         shares.append(1.0 / stats[1, pl.ds(block * BLOCK, BLOCK), :])
-    for (first, count), arriving in zip(groups, copies):
+    for (first, count), arriving, answer in zip(groups, copies, answers):
         for copy in arriving:
             copy.wait()
         for head in range(first, first + count):
@@ -154,24 +168,21 @@
                 rows = pl.ds(block * BLOCK, BLOCK)
                 numerator = sum_block(weights[head, rows, :], values, lanes, found[block])
                 share = shares[block][:, head : head + 1]
-                attended[rows, lanes] = (numerator * share).astype(jnp.bfloat16)
-
-
-def value_kernel(local_blocks, keep, begin, groups, place, kept, weights, own, lent, *refs):
-    borrowed, far = refs[1], refs[2 : 2 + len(FAR)]
+                answer[rows, pl.ds((head - first) * DH, DH)] = (numerator * share).astype(
+                    jnp.bfloat16
+                )
+
+
+def value_kernel(
+    local_blocks, keep, begin, groups, parts, runs, place, kept, weights, own, lent, *refs
+):
+    borrowed = dict(zip(runs, refs[1 : 1 + len(runs)]))
+    far = refs[1 + len(runs) : 1 + len(runs) + len(FAR) * parts]
     attended, values, result, far_sems, out_sems = refs[-5:]
+    far = [far[index * parts : (index + 1) * parts] for index in range(len(FAR))]
     copies = []
-    for group, (first, count) in enumerate(groups):
-        lanes = pl.ds(first * DH, count * DH)
-        part = pl.ds((first - begin) * DH, count * DH)
-        copies.append([])
-        for index, (slot, tile) in enumerate(zip(FAR, far)):
-            copies[-1].append(
-                pltpu.make_async_copy(
-                    tile.at[:, part], values.at[slot, :, lanes], far_sems.at[group, index]
-                )
-            )
-            copies[-1][-1].start()
+    for group, run in enumerate(groups):
+        copies.append(copied(far, values, far_sems.at[group], run, begin, FAR))
     found = [own_entries(place, kept, block, local_blocks, keep) for block in range(local_blocks)]
     shares = []
     for block in range(local_blocks):
@@ -191,8 +202,9 @@
                 rows = pl.ds(block * BLOCK, BLOCK)
                 own_share, lent_share = (share[:, head : head + 1] for share in shares[block])
                 numerator = sum_block(weights[head, rows, :], values, lanes, found[block])
-                whole = numerator * own_share
-                whole = whole + borrowed[rows, lanes].astype(jnp.float32) * lent_share
+                run = max(run for run in runs if run <= head)
+                answer = borrowed[run][rows, pl.ds((head - run) * DH, DH)]
+                whole = numerator * own_share + answer.astype(jnp.float32) * lent_share
                 result[rows, pl.ds((head - begin) * DH, DH)] = whole.astype(jnp.bfloat16)
         leaving.append(
             pltpu.make_async_copy(
@@ -210,10 +222,6 @@
     return [pltpu.with_memory_space_constraint(array, pltpu.VMEM) for array in arrays]
 
 
-def in_hbm(arrays):
-    return [pltpu.with_memory_space_constraint(array, pltpu.HBM) for array in arrays]
-
-
 SCALARS = pl.BlockSpec(memory_space=pltpu.SMEM)
 HELD = pl.BlockSpec(memory_space=pltpu.VMEM)
 ANYWHERE = pl.BlockSpec(memory_space=pl.ANY)
@@ -231,14 +239,15 @@
 def weigh(entries, place, kept, queries, tiles, near, stacked, groups, name):
     rows, columns = queries.shape
     heads = columns // DH
+    pieces = [piece for tile in tiles for piece in tile]
     return pl.pallas_call(
-        functools.partial(score_kernel, entries, *kept.shape, groups, len(tiles)),
+        functools.partial(score_kernel, entries, *kept.shape, groups, [len(t) for t in tiles]),
         out_shape=(
             pltpu.VMEM((heads, rows, kept.shape[1] * BLOCK), jnp.bfloat16),
             pltpu.VMEM((2, rows, LANES), jnp.float32),
             pltpu.VMEM((stacked, rows, columns), jnp.bfloat16),
         ),
-        in_specs=[SCALARS, SCALARS, HELD] + [ANYWHERE] * (len(tiles) + len(near)),
+        in_specs=[SCALARS, SCALARS, HELD] + [ANYWHERE] * (len(pieces) + len(near)),
         out_specs=(HELD, HELD, HELD),
         scratch_shapes=[
             pltpu.VMEM((len(tiles), rows, columns), jnp.bfloat16),
@@ -248,16 +257,18 @@
         compiler_params=pltpu.CompilerParams(vmem_limit_bytes=14 * 1024 * 1024),
         cost_estimate=cost(kept, heads, 1, 1),
         name=name,
-    )(place, kept, *in_vmem((queries,)), *in_hbm((*tiles, *near)))
+    )(place, kept, *in_vmem((queries,)), *pieces, *near)
 
 
 def sum_lent(place, kept, weights, stats, tiles, groups):
     heads, rows, _ = weights.shape
     return pl.pallas_call(
-        functools.partial(lent_kernel, *kept.shape, groups),
-        out_shape=jax.ShapeDtypeStruct((rows, heads * DH), jnp.bfloat16),
-        in_specs=[SCALARS, SCALARS, HELD, HELD] + [ANYWHERE] * LENT_TILES,
-        out_specs=HELD,
+        functools.partial(lent_kernel, *kept.shape, groups, len(tiles)),
+        out_shape=[
+            jax.ShapeDtypeStruct((rows, count * DH), jnp.bfloat16) for _, count in groups
+        ],
+        in_specs=[SCALARS, SCALARS, HELD, HELD] + [ANYWHERE] * len(tiles),
+        out_specs=[HELD] * len(groups),
         scratch_shapes=[
             pltpu.VMEM((LENT_TILES, rows, heads * DH), jnp.bfloat16),
             pltpu.SemaphoreType.DMA((len(groups), LENT_TILES)),
@@ -265,13 +276,18 @@
         compiler_params=pltpu.CompilerParams(vmem_limit_bytes=10 * 1024 * 1024),
         cost_estimate=cost(kept, heads, 1, 0),
         name="sum_lent",
-    )(place, kept, *in_vmem((weights, stats)), *in_hbm(tiles))
+    )(place, kept, *in_vmem((weights, stats)), *tiles)
 
 
 def combine(place, kept, weights, own, lent, values, borrowed, far, begin, groups, before):
     heads, rows, _ = weights.shape
-    operands = [place, kept, *in_vmem((weights, own, lent, values, borrowed)), *far]
-    in_specs = [SCALARS, SCALARS] + [HELD] * 5 + [ANYWHERE] * len(far)
+    pieces = [piece for tile in far for piece in tile]
+    last = begin + sum(count for _, count in groups)
+    borrowed = [(run, piece) for run, piece in borrowed if begin < run + piece.shape[1] // DH and run < last]
+    runs = [run for run, _ in borrowed]
+    held = in_vmem((weights, own, lent, values, *(piece for _, piece in borrowed)))
+    operands = [place, kept, *held, *pieces]
+    in_specs = [SCALARS, SCALARS] + [HELD] * len(held) + [ANYWHERE] * len(pieces)
     aliases = {5: 1}
     if before is not None:
         aliases[len(operands)] = 0
@@ -279,7 +295,7 @@
         in_specs.append(ANYWHERE)
     count = sum(count for _, count in groups)
     return pl.pallas_call(
-        functools.partial(value_kernel, *kept.shape, begin, groups),
+        functools.partial(value_kernel, *kept.shape, begin, groups, len(far[0]), runs),
         out_shape=(
             jax.ShapeDtypeStruct((rows, heads * DH), jnp.bfloat16),
             pltpu.VMEM(values.shape, values.dtype),
@@ -310,26 +326,31 @@
     groups = grouped(0, heads, GROUP)
 
     k_odd, k_even = swapped_odd(keys), swapped(keys, 4)
-    asked, asked_kept = swapped(queries, 2), swapped(kept, 2)
-    later = after(values, asked_kept)
+    asked_kept = swapped(kept, 2)
+    k_pair, v_pair = swapped(keys, 1), swapped(values, 1)
+    asked = swapped(after(queries, asked_kept, k_pair, v_pair), 2)
+    later = after(values, asked_kept, k_pair, v_pair)
     v_odd, v_even = swapped_odd(later), swapped(later, 4)
     k_odd_far, k_even_far = swapped_odd(k_even), swapped(k_odd, 4)
     k_level = jnp.where(same_side, k_even, k_odd)
     v_level = jnp.where(same_side, v_even, v_odd)
-    k_pair, k_pair_level = swapped(after(keys, k_level), 1), swapped(k_level, 1)
-    v_pair, v_pair_level = swapped(after(values, v_level), 1), swapped(v_level, 1)
+    k_pair_level = swapped(after(k_level, asked), 1)
+    half = GROUP * (heads // (2 * GROUP)) * DH
+    v_pair_level = (swapped(v_level[:, :half], 1), swapped(v_level[:, half:], 1))
     lent_weights, lent_stats, _ = weigh(
-        lent_entries, place, asked_kept, asked, (keys, k_level, k_pair, k_pair_level), (), 1,
+        lent_entries, place, asked_kept, asked, ((keys,), (k_level,), (k_pair,), (k_pair_level,)), (), 1,
         groups, "weigh_lent",
     )
     lent = swapped(lent_stats, 2)
     answer = sum_lent(
-        place, asked_kept, lent_weights, lent_stats, (values, v_level, v_pair, v_pair_level), groups
-    )
-    borrowed = swapped(after(answer, lent), 2)
+        place, asked_kept, lent_weights, lent_stats, (values, v_level, v_pair, *v_pair_level), groups
+    )
+    borrowed = [
+        (first, swapped(after(piece, lent), 2)) for (first, _), piece in zip(groups, answer)
+    ]
     weights, own, staged = weigh(
-        own_entries, place, kept, after(queries, answer),
-        (keys, k_pair, k_even, k_odd, k_even_far, k_odd_far),
+        own_entries, place, kept, after(queries, *answer),
+        ((keys,), (k_pair,), (k_even,), (k_odd,), (k_even_far,), (k_odd_far,)),
         (values, v_pair, v_even, v_odd), OWN_TILES, groups, "weigh_own",
     )
     attended, begin, hold = None, 0, lent
@@ -343,7 +364,7 @@
     begin = 0
     for count, far in zip(VALUE_SPLIT, hops):
         attended, staged = combine(
-            place, kept, weights, own, lent, staged, borrowed, far,
+            place, kept, weights, own, lent, staged, borrowed, tuple((tile,) for tile in far),
             begin, grouped(begin, count, GROUP), attended,
         )
         begin += count

time: 128 us -> 123 us (0.961)
  starting transfers between devices: 26.2 us -> 47 us
  waiting for transfers between devices: 60.2 us -> 41.2 us
  local copies, waits for them, and re-layouts: 7.38 us -> 3.47 us
  other arithmetic: 2.95 us -> 1.6 us
    ppermute x18 -> x22, starting transfers between devices: 26.2 us -> 47 us  [permuted(): lax.ppermute(value, 'blk', [(i, t) for i, t in pairs if 0 <= t < count])]
    ppermute x18 -> x22, waiting for transfers between devices: 60.2 us -> 41.2 us  [permuted(): lax.ppermute(value, 'blk', [(i, t) for i, t in pairs if 0 <= t < count])]
    slice x2, local copies, waits for them, and re-layouts: 2.38 us -> 0.1 us  [per_device(): v_even[:, lanes]]
    unnamed x26 -> x16, local copies, waits for them, and re-layouts: 4.91 us -> 3.18 us
    select_n x1, other arithmetic: 1.49 us -> 0.14 us  [per_device(): v_level = jnp.where(same_side, v_even, v_odd)]
  transfers between devices with their start and end apart: 18 -> 22, of which waited for: 6 -> 8; matrix products, arithmetic and copies ran while one was open for 4% -> 2% of each run, Pallas kernels for 22% -> 22%
where the time goes in v5:
time: 123 us
  starting transfers between devices  47 us (38%)
  waiting for transfers between devices  41.2 us (33%)
  Pallas kernels  29.3 us (24%)
  local copies, waits for them, and re-layouts  3.47 us (3%)
  other arithmetic  1.6 us (1%)
    ppermute x22, starting transfers between devices, permuted(): lax.ppermute(value, 'blk', [(i, t) for i, t in pairs if 0 <= t < count])  47 us
    ppermute x22, waiting for transfers between devices, permuted(): lax.ppermute(value, 'blk', [(i, t) for i, t in pairs if 0 <= t < count])  41.2 us
    pallas_call x2, Pallas kernels, weigh(): pl.pallas_call(functools.partial(score_kernel, entries, *kept.shape, grou...  17.6 us
    pallas_call x2, Pallas kernels, combine(): pl.pallas_call(functools.partial(value_kernel, *kept.shape, begin, groups...  6.95 us
    pallas_call x1, Pallas kernels, sum_lent(): pl.pallas_call(functools.partial(lent_kernel, *kept.shape, groups, len(ti...  4.79 us
    unnamed x16, local copies, waits for them, and re-layouts  3.18 us
  transfers between devices with their start and end apart: 22, of which 8 were waited for; matrix products, arithmetic and copies ran while one was open for 2% of the time, Pallas kernels for 22%

profile of v5, /device:TPU:0, one launch (start us, length us, event | category | flops | bytes accessed | tf_op | source)
XLA Modules:
  0.0 122.9 jit_solution(5459650225595929444)
XLA Ops:
  0.5 1.7 %collective-permute-start.5 = (bf16[256,2560]{1,0:T(8,128)(2,1)}, bf16[256,2560]{1,0:T(8,128)(2,1)}, u32[]{:S(2)}, u32[]{:S(2)}) collective-permute-start(bf16[256,2560]{1,0:T(8,128)(2,1)} %refs_0_.5), channel_id=1, source_target_pairs={{4,8},{5,9},{6,10},{7,11},{8,4},{9,5},{10,6},{11,7},{20,24},{21,25... | collective-permute-start | bytes 3932168 | tf_op jit(solution)/shard_map/ppermute | solution.py:26
  2.2 4.8 %collective-permute-start.4 = (bf16[256,2560]{1,0:T(8,128)(2,1)}, bf16[256,2560]{1,0:T(8,128)(2,1)}, u32[]{:S(2)}, u32[]{:S(2)}) collective-permute-start(bf16[256,2560]{1,0:T(8,128)(2,1)} %refs_0_.5), channel_id=1, source_target_pairs={{0,4},{1,5},{2,6},{3,7},{4,0},{5,1},{6,2},{7,3},{8,12},{9,13},{10,... | collective-permute-start | bytes 3932168 | tf_op jit(solution)/shard_map/ppermute | solution.py:26
  7.1 1.5 %collective-permute-start = (s32[2,8]{1,0:T(2,128)}, s32[2,8]{1,0:T(2,128)S(1)}, u32[]{:S(2)}, u32[]{:S(2)}) collective-permute-start(s32[2,8]{1,0:T(2,128)} %kept.5), channel_id=1, source_target_pairs={{0,2},{1,3},{2,0},{3,1},{4,6},{5,7},{6,4},{7,5},{8,10},{9,11},{10,... | collective-permute-start | bytes 200 | tf_op jit(solution)/shard_map/ppermute | solution.py:26
  8.6 2.3 %collective-permute-done.kept = s32[2,8]{1,0:T(2,128)S(1)} collective-permute-done((s32[2,8]{1,0:T(2,128)}, s32[2,8]{1,0:T(2,128)S(1)}, u32[]{:S(2)}, u32[]{:S(2)}) %collective-permute-start) | collective-permute-done | bytes 96 | tf_op jit(solution)/shard_map/ppermute | solution.py:26
  10.9 1.1 copy-done.1
  12.0 1.1 copy-done.5
  13.0 1.5 %collective-permute-start.3 = (bf16[256,2560]{1,0:T(8,128)(2,1)}, bf16[256,2560]{1,0:T(8,128)(2,1)}, u32[]{:S(2)}, u32[]{:S(2)}) collective-permute-start(bf16[256,2560]{1,0:T(8,128)(2,1)} %queries), channel_id=1, source_target_pairs={{0,2},{1,3},{2,0},{3,1},{4,6},{5,7},{6,4},{7,5},{8,10},{9,11},{10,... | collective-permute-start | bytes 3932168 | tf_op jit(solution)/shard_map/ppermute | solution.py:26
  14.5 0.7 collective-permute-start.8
  15.3 2.6 %collective-permute-start.7 = (bf16[256,2560]{1,0:T(8,128)(2,1)}, bf16[256,2560]{1,0:T(8,128)(2,1)S(1)}, u32[]{:S(2)}, u32[]{:S(2)}) collective-permute-start(bf16[256,2560]{1,0:T(8,128)(2,1)} %refs_6_.1), channel_id=1, source_target_pairs={{0,4},{1,5},{2,6},{3,7},{4,0},{5,1},{6,2},{7,3},{8,12},{9,13},{10,... | collective-permute-start | bytes 3932168 | tf_op jit(solution)/shard_map/ppermute | solution.py:26
  17.8 19.5 %collective-permute-start.11 = (bf16[256,2560]{1,0:T(8,128)(2,1)}, bf16[256,2560]{1,0:T(8,128)(2,1)S(1)}, u32[]{:S(2)}, u32[]{:S(2)}) collective-permute-start(bf16[256,2560]{1,0:T(8,128)(2,1)} %collective-permute-done.5.refs_3_), channel_id=1, source_target_pairs={{0,4},{1,5},{2,6},{3,7},{4,0},{5,1},{6,2},{7,3},{8,12},{9,13},{10,... | collective-permute-start | bytes 3932168 | tf_op jit(solution)/shard_map/ppermute | solution.py:26
  37.4 0.7 collective-permute-start.12
  38.1 1.5 %broadcast_select_fusion.1.refs_1_ = bf16[256,2560]{1,0:T(8,128)(2,1)S(1)} fusion(bf16[256,2560]{1,0:T(8,128)(2,1)} %collective-permute-done.4.refs_2_, bf16[256,2560]{1,0:T(8,128)(2,1)} %collective-permute-done.5.refs_3_, pred[]{:T(512)S(6)} %eq.6), kind=kLoop, calls=%fused_computation.1 | loop fusion | flops 655360 | bytes 3932161 | tf_op jit(solution)/shard_map/jit(_where)/select_n | solution.py:335
  39.6 3.1 %collective-permute-done.3.queries = bf16[256,2560]{1,0:T(8,128)(2,1)} collective-permute-done((bf16[256,2560]{1,0:T(8,128)(2,1)}, bf16[256,2560]{1,0:T(8,128)(2,1)}, u32[]{:S(2)}, u32[]{:S(2)}) %collective-permute-start.3) | collective-permute-done | bytes 1310752 | tf_op jit(solution)/shard_map/ppermute | solution.py:26
  42.7 22.3 %collective-permute-done.7.refs_8_ = bf16[256,2560]{1,0:T(8,128)(2,1)S(1)} collective-permute-done((bf16[256,2560]{1,0:T(8,128)(2,1)}, bf16[256,2560]{1,0:T(8,128)(2,1)S(1)}, u32[]{:S(2)}, u32[]{:S(2)}) %collective-permute-start.7) | collective-permute-done | bytes 1310752 | tf_op jit(solution)/shard_map/ppermute | solution.py:26
  65.9 0.6 copy-done.4
  66.9 9.1 %weigh_lent.1 = (bf16[20,256,1024]{2,1,0:T(8,128)(2,1)S(1)}, f32[2,256,128]{2,1,0:T(8,128)S(1)}, bf16[1,256,2560]{2,1,0:T(8,128)(2,1)}) custom-call(s32[1]{0:T(128)} %bitcast.place, s32[2,8]{1,0:T(2,128)S(1)} %collective-permute-done.kept, bf16[256,2560]{1,0:T(8,128)(2,1)} %collective-permute-done.3.queries, bf16[256,2560]{1,0:T(8,128)(2,1)S(1)} %copy-done.4, ...), custom_call_target="tpu_custom_call" | custom-call | flops 1342177280 | bytes 10485760 | tf_op jit(solution)/shard_map/weigh_lent/pallas_call | solution.py:243
  76.0 1.6 %collective-permute-start.13 = (f32[2,256,128]{2,1,0:T(8,128)S(1)}, f32[2,256,128]{2,1,0:T(8,128)S(1)}, u32[]{:S(2)}, u32[]{:S(2)}) collective-permute-start(f32[2,256,128]{2,1,0:T(8,128)S(1)} %get-tuple-element.32.stats), channel_id=1, source_target_pairs={{0,2},{1,3},{2,0},{3,1},{4,6},{5,7},{6,4},{7,5},{8,10},{9,11},{10,... | collective-permute-start | bytes 786440 | tf_op jit(solution)/shard_map/ppermute | solution.py:26
  77.8 5.6 %collective-permute-done.13.lent = f32[2,256,128]{2,1,0:T(8,128)S(1)} collective-permute-done((f32[2,256,128]{2,1,0:T(8,128)S(1)}, f32[2,256,128]{2,1,0:T(8,128)S(1)}, u32[]{:S(2)}, u32[]{:S(2)}) %collective-permute-start.13) | collective-permute-done | bytes 262176 | tf_op jit(solution)/shard_map/ppermute | solution.py:26
  83.4 2.1 %collective-permute-start.17 = (bf16[256,1920]{1,0:T(8,128)(2,1)S(1)}, bf16[256,1920]{1,0:T(8,128)(2,1)S(1)}, u32[]{:S(2)}, u32[]{:S(2)}) collective-permute-start(bf16[256,1920]{1,0:T(8,128)(2,1)S(1)} %slice.26), channel_id=1, source_target_pairs={{0,4},{1,5},{2,6},{3,7},{4,0},{5,1},{6,2},{7,3},{8,12},{9,13},{10,... | collective-permute-start | bytes 2949128 | tf_op jit(solution)/shard_map/ppermute | solution.py:26
  85.4 0.9 collective-permute-start.18
  86.3 4.8 %sum_lent.1 = (bf16[256,640]{1,0:T(8,128)(2,1)S(1)}, bf16[256,640]{1,0:T(8,128)(2,1)S(1)}, bf16[256,640]{1,0:T(8,128)(2,1)S(1)}, bf16[256,640]{1,0:T(8,128)(2,1)S(1)}) custom-call(s32[1]{0:T(128)} %bitcast.place, s32[2,8]{1,0:T(2,128)S(1)} %collective-permute-done.kept, bf16[20,256,1024]{2,1,0:T(8,128)(2,1)S(1)} %get-tuple-element.31.weights, ...), custom_call_target="tpu_custom_call" | custom-call | flops 1342177280 | bytes 10485760 | tf_op jit(solution)/shard_map/sum_lent/pallas_call | solution.py:265
  91.2 1.6 %collective-permute-start.14 = (bf16[256,640]{1,0:T(8,128)(2,1)S(1)}, bf16[256,640]{1,0:T(8,128)(2,1)S(1)}, u32[]{:S(2)}, u32[]{:S(2)}) collective-permute-start(bf16[256,640]{1,0:T(8,128)(2,1)S(1)} %get-tuple-element.42), channel_id=1, source_target_pairs={{0,2},{1,3},{2,0},{3,1},{4,6},{5,7},{6,4},{7,5},{8,10},{9,11},{10,... | collective-permute-start | bytes 983048 | tf_op jit(solution)/shard_map/ppermute | solution.py:26
  93.1 1.5 %collective-permute-start.15 = (bf16[256,640]{1,0:T(8,128)(2,1)S(1)}, bf16[256,640]{1,0:T(8,128)(2,1)S(1)}, u32[]{:S(2)}, u32[]{:S(2)}) collective-permute-start(bf16[256,640]{1,0:T(8,128)(2,1)S(1)} %get-tuple-element.43), channel_id=1, source_target_pairs={{0,2},{1,3},{2,0},{3,1},{4,6},{5,7},{6,4},{7,5},{8,10},{9,11},{10,... | collective-permute-start | bytes 983048 | tf_op jit(solution)/shard_map/ppermute | solution.py:26
  95.2 8.4 %weigh_own.1 = (bf16[20,256,1024]{2,1,0:T(8,128)(2,1)S(1)}, f32[2,256,128]{2,1,0:T(8,128)S(1)}, bf16[6,256,2560]{2,1,0:T(8,128)(2,1)S(1)}) custom-call(s32[1]{0:T(128)} %bitcast.place, s32[2,8]{1,0:T(2,128)S(1)} %copy-done.7, bf16[256,2560]{1,0:T(8,128)(2,1)S(1)} %copy-done.3, bf16[256,2560]{1,0:T(8,128)(2,1)S(1)} %copy-done.4, ...), custom_call_target="tpu_custom_call" | custom-call | flops 1342177280 | bytes 10485760 | tf_op jit(solution)/shard_map/weigh_own/pallas_call | solution.py:243
  103.7 2.2 %collective-permute-start.20 = (bf16[256,640]{1,0:T(8,128)(2,1)S(1)}, bf16[256,640]{1,0:T(8,128)(2,1)S(1)}, u32[]{:S(2)}, u32[]{:S(2)}) collective-permute-start(bf16[256,640]{1,0:T(8,128)(2,1)S(1)} %slice.28), channel_id=1, source_target_pairs={{0,4},{1,5},{2,6},{3,7},{4,0},{5,1},{6,2},{7,3},{8,12},{9,13},{10,... | collective-permute-start | bytes 983048 | tf_op jit(solution)/shard_map/ppermute | solution.py:26
  105.9 3.0 %collective-permute-done.15.refs_2_ = bf16[256,640]{1,0:T(8,128)(2,1)S(1)} collective-permute-done((bf16[256,640]{1,0:T(8,128)(2,1)S(1)}, bf16[256,640]{1,0:T(8,128)(2,1)S(1)}, u32[]{:S(2)}, u32[]{:S(2)}) %collective-permute-start.15) | collective-permute-done | bytes 327712 | tf_op jit(solution)/shard_map/ppermute | solution.py:26
  108.9 0.9 collective-permute-start.21
  109.8 3.4 %collective-permute-done.16.refs_3_ = bf16[256,640]{1,0:T(8,128)(2,1)S(1)} collective-permute-done((bf16[256,640]{1,0:T(8,128)(2,1)S(1)}, bf16[256,640]{1,0:T(8,128)(2,1)S(1)}, u32[]{:S(2)}, u32[]{:S(2)}) %collective-permute-start.16) | collective-permute-done | bytes 327712 | tf_op jit(solution)/shard_map/ppermute | solution.py:26
  113.2 1.5 %collective-permute-start.19 = (bf16[256,640]{1,0:T(8,128)(2,1)S(1)}, bf16[256,640]{1,0:T(8,128)(2,1)S(1)}, u32[]{:S(2)}, u32[]{:S(2)}) collective-permute-start(bf16[256,640]{1,0:T(8,128)(2,1)S(1)} %get-tuple-element.48), channel_id=1, source_target_pairs={{0,2},{1,3},{2,0},{3,1},{4,6},{5,7},{6,4},{7,5},{8,10},{9,11},{10,... | collective-permute-start | bytes 983048 | tf_op jit(solution)/shard_map/ppermute | solution.py:26
  114.7 4.4 %combine_0.1 = (bf16[256,2560]{1,0:T(8,128)(2,1)}, bf16[6,256,2560]{2,1,0:T(8,128)(2,1)S(1)}) custom-call(s32[1]{0:T(128)} %bitcast.place, s32[2,8]{1,0:T(2,128)S(1)} %copy-done.7, bf16[20,256,1024]{2,1,0:T(8,128)(2,1)S(1)} %get-tuple-element.39.weights, f32[2,256,128]{2,1,0:T(8,128)S(1)} %get-tuple-element.40.own, ...), custom_call_target="tpu_custom_call", output_to_operand_aliasing={{1}: (5, {})} | custom-call | flops 1006632960 | bytes 7864320 | tf_op jit(solution)/shard_map/combine_0/pallas_call | solution.py:297
  119.1 1.1 collective-permute-done.20.refs_2_
  120.2 2.5 %combine_15.1 = (bf16[256,2560]{1,0:T(8,128)(2,1)}, bf16[6,256,2560]{2,1,0:T(8,128)(2,1)S(1)}) custom-call(s32[1]{0:T(128)} %bitcast.place, s32[2,8]{1,0:T(2,128)S(1)} %copy-done.7, bf16[20,256,1024]{2,1,0:T(8,128)(2,1)S(1)} %get-tuple-element.39.weights, f32[2,256,128]{2,1,0:T(8,128)S(1)} %get-tuple-element.40.own, ...), custom_call_target="tpu_custom_call", output_to_operand_aliasing={{1}: (5, {}), {0}: (9, {})} | custom-call | flops 335544320 | bytes 2621440 | tf_op jit(solution)/shard_map/combine_15/pallas_call | solution.py:297
  (40 shorter events, 2.8 us)
Async XLA Ops:
  0.0 10.9 %collective-permute-start.2 = (bf16[256,2560]{1,0:T(8,128)(2,1)}, bf16[256,2560]{1,0:T(8,128)(2,1)S(1)}, u32[]{:S(2)}, u32[]{:S(2)}) collective-permute-start(bf16[256,2560]{1,0:T(8,128)(2,1)} %refs_6_.1), channel_id=1, source_target_pairs={{0,1},{1,0},{2,3},{3,2},{4,5},{5,4},{6,7},{7,6},{8,9},{9,8},{10,11... | collective-permute-start | bytes 3932168 | tf_op jit(solution)/shard_map/ppermute | solution.py:26
  0.5 11.5 %collective-permute-start.1 = (bf16[256,2560]{1,0:T(8,128)(2,1)}, bf16[256,2560]{1,0:T(8,128)(2,1)S(1)}, u32[]{:S(2)}, u32[]{:S(2)}) collective-permute-start(bf16[256,2560]{1,0:T(8,128)(2,1)} %refs_0_.5), channel_id=1, source_target_pairs={{0,1},{1,0},{2,3},{3,2},{4,5},{5,4},{6,7},{7,6},{8,9},{9,8},{10,11... | collective-permute-start | bytes 3932168 | tf_op jit(solution)/shard_map/ppermute | solution.py:26
  0.5 17.3 %collective-permute-start.5 = (bf16[256,2560]{1,0:T(8,128)(2,1)}, bf16[256,2560]{1,0:T(8,128)(2,1)}, u32[]{:S(2)}, u32[]{:S(2)}) collective-permute-start(bf16[256,2560]{1,0:T(8,128)(2,1)} %refs_0_.5), channel_id=1, source_target_pairs={{4,8},{5,9},{6,10},{7,11},{8,4},{9,5},{10,6},{11,7},{20,24},{21,25... | collective-permute-start | bytes 3932168 | tf_op jit(solution)/shard_map/ppermute | solution.py:26
  2.2 35.1 %collective-permute-start.4 = (bf16[256,2560]{1,0:T(8,128)(2,1)}, bf16[256,2560]{1,0:T(8,128)(2,1)}, u32[]{:S(2)}, u32[]{:S(2)}) collective-permute-start(bf16[256,2560]{1,0:T(8,128)(2,1)} %refs_0_.5), channel_id=1, source_target_pairs={{0,4},{1,5},{2,6},{3,7},{4,0},{5,1},{6,2},{7,3},{8,12},{9,13},{10,... | collective-permute-start | bytes 3932168 | tf_op jit(solution)/shard_map/ppermute | solution.py:26
  7.1 3.8 %collective-permute-start = (s32[2,8]{1,0:T(2,128)}, s32[2,8]{1,0:T(2,128)S(1)}, u32[]{:S(2)}, u32[]{:S(2)}) collective-permute-start(s32[2,8]{1,0:T(2,128)} %kept.5), channel_id=1, source_target_pairs={{0,2},{1,3},{2,0},{3,1},{4,6},{5,7},{6,4},{7,5},{8,10},{9,11},{10,... | collective-permute-start | bytes 200 | tf_op jit(solution)/shard_map/ppermute | solution.py:26
  10.9 1.1 copy-start.1
  12.0 1.1 copy-start.5
  13.0 29.7 %collective-permute-start.3 = (bf16[256,2560]{1,0:T(8,128)(2,1)}, bf16[256,2560]{1,0:T(8,128)(2,1)}, u32[]{:S(2)}, u32[]{:S(2)}) collective-permute-start(bf16[256,2560]{1,0:T(8,128)(2,1)} %queries), channel_id=1, source_target_pairs={{0,2},{1,3},{2,0},{3,1},{4,6},{5,7},{6,4},{7,5},{8,10},{9,11},{10,... | collective-permute-start | bytes 3932168 | tf_op jit(solution)/shard_map/ppermute | solution.py:26
  14.5 28.2 %collective-permute-start.8 = (bf16[256,2560]{1,0:T(8,128)(2,1)}, bf16[256,2560]{1,0:T(8,128)(2,1)S(1)}, u32[]{:S(2)}, u32[]{:S(2)}) collective-permute-start(bf16[256,2560]{1,0:T(8,128)(2,1)} %refs_6_.1), channel_id=1, source_target_pairs={{4,8},{5,9},{6,10},{7,11},{8,4},{9,5},{10,6},{11,7},{20,24},{21,25... | collective-permute-start | bytes 3932168 | tf_op jit(solution)/shard_map/ppermute | solution.py:26
  15.3 49.7 %collective-permute-start.7 = (bf16[256,2560]{1,0:T(8,128)(2,1)}, bf16[256,2560]{1,0:T(8,128)(2,1)S(1)}, u32[]{:S(2)}, u32[]{:S(2)}) collective-permute-start(bf16[256,2560]{1,0:T(8,128)(2,1)} %refs_6_.1), channel_id=1, source_target_pairs={{0,4},{1,5},{2,6},{3,7},{4,0},{5,1},{6,2},{7,3},{8,12},{9,13},{10,... | collective-permute-start | bytes 3932168 | tf_op jit(solution)/shard_map/ppermute | solution.py:26
  17.8 75.3 %collective-permute-start.11 = (bf16[256,2560]{1,0:T(8,128)(2,1)}, bf16[256,2560]{1,0:T(8,128)(2,1)S(1)}, u32[]{:S(2)}, u32[]{:S(2)}) collective-permute-start(bf16[256,2560]{1,0:T(8,128)(2,1)} %collective-permute-done.5.refs_3_), channel_id=1, source_target_pairs={{0,4},{1,5},{2,6},{3,7},{4,0},{5,1},{6,2},{7,3},{8,12},{9,13},{10,... | collective-permute-start | bytes 3932168 | tf_op jit(solution)/shard_map/ppermute | solution.py:26
  37.4 57.2 %collective-permute-start.12 = (bf16[256,2560]{1,0:T(8,128)(2,1)}, bf16[256,2560]{1,0:T(8,128)(2,1)S(1)}, u32[]{:S(2)}, u32[]{:S(2)}) collective-permute-start(bf16[256,2560]{1,0:T(8,128)(2,1)} %collective-permute-done.4.refs_2_), channel_id=1, source_target_pairs={{4,8},{5,9},{6,10},{7,11},{8,4},{9,5},{10,6},{11,7},{20,24},{21,25... | collective-permute-start | bytes 3932168 | tf_op jit(solution)/shard_map/ppermute | solution.py:26
  42.7 23.1 %collective-permute-start.6 = (bf16[256,2560]{1,0:T(8,128)(2,1)S(1)}, bf16[256,2560]{1,0:T(8,128)(2,1)S(1)}, u32[]{:S(2)}, u32[]{:S(2)}) collective-permute-start(bf16[256,2560]{1,0:T(8,128)(2,1)S(1)} %broadcast_select_fusion.1.refs_1_), channel_id=1, source_target_pairs={{0,1},{1,0},{2,3},{3,2},{4,5},{5,4},{6,7},{7,6},{8,9},{9,8},{10,11... | collective-permute-start | bytes 3932168 | tf_op jit(solution)/shard_map/ppermute | solution.py:26
  65.2 1.3 %copy-start.4 = (bf16[256,2560]{1,0:T(8,128)(2,1)S(1)}, bf16[256,2560]{1,0:T(8,128)(2,1)}, u32[]{:S(2)}) copy-start(bf16[256,2560]{1,0:T(8,128)(2,1)} %refs_0_.5) | copy-start | bytes 3932164
  65.2 1.7 %copy-start.6 = (bf16[256,2560]{1,0:T(8,128)(2,1)S(1)}, bf16[256,2560]{1,0:T(8,128)(2,1)}, u32[]{:S(2)}) copy-start(bf16[256,2560]{1,0:T(8,128)(2,1)} %copy-done.5) | copy-start | bytes 3932164
  65.3 20.1 %collective-permute-start.10 = (bf16[256,1280]{1,0:T(8,128)(2,1)S(1)}, bf16[256,1280]{1,0:T(8,128)(2,1)S(1)}, u32[]{:S(2)}, u32[]{:S(2)}) collective-permute-start(bf16[256,1280]{1,0:T(8,128)(2,1)S(1)} %get-tuple-element.53), channel_id=1, source_target_pairs={{0,1},{1,0},{2,3},{3,2},{4,5},{5,4},{6,7},{7,6},{8,9},{9,8},{10,11... | collective-permute-start | bytes 1966088 | tf_op jit(solution)/shard_map/ppermute | solution.py:26
  65.3 21.0 %collective-permute-start.9 = (bf16[256,1280]{1,0:T(8,128)(2,1)S(1)}, bf16[256,1280]{1,0:T(8,128)(2,1)S(1)}, u32[]{:S(2)}, u32[]{:S(2)}) collective-permute-start(bf16[256,1280]{1,0:T(8,128)(2,1)S(1)} %get-tuple-element.54), channel_id=1, source_target_pairs={{0,1},{1,0},{2,3},{3,2},{4,5},{5,4},{6,7},{7,6},{8,9},{9,8},{10,11... | collective-permute-start | bytes 1966088 | tf_op jit(solution)/shard_map/ppermute | solution.py:26
  76.0 7.4 %collective-permute-start.13 = (f32[2,256,128]{2,1,0:T(8,128)S(1)}, f32[2,256,128]{2,1,0:T(8,128)S(1)}, u32[]{:S(2)}, u32[]{:S(2)}) collective-permute-start(f32[2,256,128]{2,1,0:T(8,128)S(1)} %get-tuple-element.32.stats), channel_id=1, source_target_pairs={{0,2},{1,3},{2,0},{3,1},{4,6},{5,7},{6,4},{7,5},{8,10},{9,11},{10,... | collective-permute-start | bytes 786440 | tf_op jit(solution)/shard_map/ppermute | solution.py:26
  77.6 8.7 %copy-start.2 = (bf16[256,2560]{1,0:T(8,128)(2,1)S(1)}, bf16[256,2560]{1,0:T(8,128)(2,1)}, u32[]{:S(2)}) copy-start(bf16[256,2560]{1,0:T(8,128)(2,1)} %copy-done.1) | copy-start | bytes 3932164
  77.7 8.7 %copy-start = (bf16[256,2560]{1,0:T(8,128)(2,1)S(1)}, bf16[256,2560]{1,0:T(8,128)(2,1)}, u32[]{:S(2)}) copy-start(bf16[256,2560]{1,0:T(8,128)(2,1)} %refs_6_.1) | copy-start | bytes 3932164
  83.4 31.3 %collective-permute-start.17 = (bf16[256,1920]{1,0:T(8,128)(2,1)S(1)}, bf16[256,1920]{1,0:T(8,128)(2,1)S(1)}, u32[]{:S(2)}, u32[]{:S(2)}) collective-permute-start(bf16[256,1920]{1,0:T(8,128)(2,1)S(1)} %slice.26), channel_id=1, source_target_pairs={{0,4},{1,5},{2,6},{3,7},{4,0},{5,1},{6,2},{7,3},{8,12},{9,13},{10,... | collective-permute-start | bytes 2949128 | tf_op jit(solution)/shard_map/ppermute | solution.py:26
  85.4 29.3 %collective-permute-start.18 = (bf16[256,1920]{1,0:T(8,128)(2,1)S(1)}, bf16[256,1920]{1,0:T(8,128)(2,1)S(1)}, u32[]{:S(2)}, u32[]{:S(2)}) collective-permute-start(bf16[256,1920]{1,0:T(8,128)(2,1)S(1)} %slice.27), channel_id=1, source_target_pairs={{4,8},{5,9},{6,10},{7,11},{8,4},{9,5},{10,6},{11,7},{20,24},{21,25... | collective-permute-start | bytes 2949128 | tf_op jit(solution)/shard_map/ppermute | solution.py:26
  91.1 4.1 %copy-start.3 = (bf16[256,2560]{1,0:T(8,128)(2,1)S(1)}, bf16[256,2560]{1,0:T(8,128)(2,1)}, u32[]{:S(2)}) copy-start(bf16[256,2560]{1,0:T(8,128)(2,1)} %queries) | copy-start | bytes 3932164
  91.2 4.1 %copy-start.7 = (s32[2,8]{1,0:T(2,128)S(1)}, s32[2,8]{1,0:T(2,128)}, u32[]{:S(2)}) copy-start(s32[2,8]{1,0:T(2,128)} %kept.5) | copy-start | bytes 196
  91.2 12.5 %collective-permute-start.14 = (bf16[256,640]{1,0:T(8,128)(2,1)S(1)}, bf16[256,640]{1,0:T(8,128)(2,1)S(1)}, u32[]{:S(2)}, u32[]{:S(2)}) collective-permute-start(bf16[256,640]{1,0:T(8,128)(2,1)S(1)} %get-tuple-element.42), channel_id=1, source_target_pairs={{0,2},{1,3},{2,0},{3,1},{4,6},{5,7},{6,4},{7,5},{8,10},{9,11},{10,... | collective-permute-start | bytes 983048 | tf_op jit(solution)/shard_map/ppermute | solution.py:26
  93.1 15.8 %collective-permute-start.15 = (bf16[256,640]{1,0:T(8,128)(2,1)S(1)}, bf16[256,640]{1,0:T(8,128)(2,1)S(1)}, u32[]{:S(2)}, u32[]{:S(2)}) collective-permute-start(bf16[256,640]{1,0:T(8,128)(2,1)S(1)} %get-tuple-element.43), channel_id=1, source_target_pairs={{0,2},{1,3},{2,0},{3,1},{4,6},{5,7},{6,4},{7,5},{8,10},{9,11},{10,... | collective-permute-start | bytes 983048 | tf_op jit(solution)/shard_map/ppermute | solution.py:26
  94.6 18.5 %collective-permute-start.16 = (bf16[256,640]{1,0:T(8,128)(2,1)S(1)}, bf16[256,640]{1,0:T(8,128)(2,1)S(1)}, u32[]{:S(2)}, u32[]{:S(2)}) collective-permute-start(bf16[256,640]{1,0:T(8,128)(2,1)S(1)} %get-tuple-element.44), channel_id=1, source_target_pairs={{0,2},{1,3},{2,0},{3,1},{4,6},{5,7},{6,4},{7,5},{8,10},{9,11},{10,... | collective-permute-start | bytes 983048 | tf_op jit(solution)/shard_map/ppermute | solution.py:26
  103.7 16.6 %collective-permute-start.20 = (bf16[256,640]{1,0:T(8,128)(2,1)S(1)}, bf16[256,640]{1,0:T(8,128)(2,1)S(1)}, u32[]{:S(2)}, u32[]{:S(2)}) collective-permute-start(bf16[256,640]{1,0:T(8,128)(2,1)S(1)} %slice.28), channel_id=1, source_target_pairs={{0,4},{1,5},{2,6},{3,7},{4,0},{5,1},{6,2},{7,3},{8,12},{9,13},{10,... | collective-permute-start | bytes 983048 | tf_op jit(solution)/shard_map/ppermute | solution.py:26
  108.9 11.3 %collective-permute-start.21 = (bf16[256,640]{1,0:T(8,128)(2,1)S(1)}, bf16[256,640]{1,0:T(8,128)(2,1)S(1)}, u32[]{:S(2)}, u32[]{:S(2)}) collective-permute-start(bf16[256,640]{1,0:T(8,128)(2,1)S(1)} %slice.29), channel_id=1, source_target_pairs={{4,8},{5,9},{6,10},{7,11},{8,4},{9,5},{10,6},{11,7},{20,24},{21,25... | collective-permute-start | bytes 983048 | tf_op jit(solution)/shard_map/ppermute | solution.py:26
  113.2 7.1 %collective-permute-start.19 = (bf16[256,640]{1,0:T(8,128)(2,1)S(1)}, bf16[256,640]{1,0:T(8,128)(2,1)S(1)}, u32[]{:S(2)}, u32[]{:S(2)}) collective-permute-start(bf16[256,640]{1,0:T(8,128)(2,1)S(1)} %get-tuple-element.48), channel_id=1, source_target_pairs={{0,2},{1,3},{2,0},{3,1},{4,6},{5,7},{6,4},{7,5},{8,10},{9,11},{10,... | collective-permute-start | bytes 983048 | tf_op jit(solution)/shard_map/ppermute | solution.py:26

commit v6 on v5

--- a/solution.py
+++ b/solution.py
@@ -11,6 +11,7 @@
 DH = 128
 BLOCK = 128
 LANES = 128
+TOTALS = LANES // 2
 VALUE_SPLIT = (15, 5)
 GROUP = 5
 OWN_TILES = 6
@@ -143,8 +144,8 @@
                 rows = pl.ds(block * BLOCK, BLOCK)
                 top, total, weight = weigh_block(queries[rows, lanes], keys, lanes, found[block])
                 weights[head, rows, :] = weight
-                stats[0, rows, pl.ds(head, 1)] = top
-                stats[1, rows, pl.ds(head, 1)] = total
+                stats[rows, pl.ds(head, 1)] = top
+                stats[rows, pl.ds(TOTALS + head, 1)] = total
     for copy in value_copies:
         copy.wait()
 
@@ -158,7 +159,7 @@
     found = [lent_entries(place, kept, block, local_blocks, keep) for block in range(local_blocks)]
     shares = []
     for block in range(local_blocks):
-        shares.append(1.0 / stats[1, pl.ds(block * BLOCK, BLOCK), :])
+        shares.append(1.0 / stats[pl.ds(block * BLOCK, BLOCK), pl.ds(TOTALS, TOTALS)])
     for (first, count), arriving, answer in zip(groups, copies, answers):
         for copy in arriving:
             copy.wait()
@@ -174,7 +175,7 @@
 
 
 def value_kernel(
-    local_blocks, keep, begin, groups, parts, runs, place, kept, weights, own, lent, *refs
+    local_blocks, keep, begin, groups, parts, runs, direct, place, kept, weights, own, lent, *refs
 ):
     borrowed = dict(zip(runs, refs[1 : 1 + len(runs)]))
     far = refs[1 + len(runs) : 1 + len(runs) + len(FAR) * parts]
@@ -182,15 +183,25 @@
     far = [far[index * parts : (index + 1) * parts] for index in range(len(FAR))]
     copies = []
     for group, run in enumerate(groups):
-        copies.append(copied(far, values, far_sems.at[group], run, begin, FAR))
+        if direct:
+            first, count = run
+            for slot, (piece,) in zip(FAR, far):
+                values[slot, :, pl.ds(first * DH, count * DH)] = piece[
+                    :, pl.ds((first - begin) * DH, count * DH)
+                ]
+            copies.append([])
+        else:
+            copies.append(copied(far, values, far_sems.at[group], run, begin, FAR))
     found = [own_entries(place, kept, block, local_blocks, keep) for block in range(local_blocks)]
     shares = []
     for block in range(local_blocks):
         rows = pl.ds(block * BLOCK, BLOCK)
-        top = jnp.maximum(own[0, rows, :], lent[0, rows, :])
-        own_scale = jnp.exp2((own[0, rows, :] - top) * SCALE)
-        lent_total = lent[1, rows, :] * jnp.exp2((lent[0, rows, :] - top) * SCALE)
-        total = own[1, rows, :] * own_scale + lent_total
+        own_top, lent_top = own[rows, pl.ds(0, TOTALS)], lent[rows, pl.ds(0, TOTALS)]
+        top = jnp.maximum(own_top, lent_top)
+        own_scale = jnp.exp2((own_top - top) * SCALE)
+        lent_scale = jnp.exp2((lent_top - top) * SCALE)
+        lent_total = lent[rows, pl.ds(TOTALS, TOTALS)] * lent_scale
+        total = own[rows, pl.ds(TOTALS, TOTALS)] * own_scale + lent_total
         shares.append((own_scale / total, lent_total / total))
     leaving = []
     for group, (first, count) in enumerate(groups):
@@ -244,7 +255,7 @@
         functools.partial(score_kernel, entries, *kept.shape, groups, [len(t) for t in tiles]),
         out_shape=(
             pltpu.VMEM((heads, rows, kept.shape[1] * BLOCK), jnp.bfloat16),
-            pltpu.VMEM((2, rows, LANES), jnp.float32),
+            pltpu.VMEM((rows, LANES), jnp.float32),
             pltpu.VMEM((stacked, rows, columns), jnp.bfloat16),
         ),
         in_specs=[SCALARS, SCALARS, HELD] + [ANYWHERE] * (len(pieces) + len(near)),
@@ -286,8 +297,10 @@
     borrowed = [(run, piece) for run, piece in borrowed if begin < run + piece.shape[1] // DH and run < last]
     runs = [run for run, _ in borrowed]
     held = in_vmem((weights, own, lent, values, *(piece for _, piece in borrowed)))
-    operands = [place, kept, *held, *pieces]
-    in_specs = [SCALARS, SCALARS] + [HELD] * len(held) + [ANYWHERE] * len(pieces)
+    direct = before is not None
+    operands = [place, kept, *held, *(in_vmem(pieces) if direct else pieces)]
+    in_specs = [SCALARS, SCALARS] + [HELD] * len(held)
+    in_specs += [HELD if direct else ANYWHERE] * len(pieces)
     aliases = {5: 1}
     if before is not None:
         aliases[len(operands)] = 0
@@ -295,7 +308,7 @@
         in_specs.append(ANYWHERE)
     count = sum(count for _, count in groups)
     return pl.pallas_call(
-        functools.partial(value_kernel, *kept.shape, begin, groups, len(far[0]), runs),
+        functools.partial(value_kernel, *kept.shape, begin, groups, len(far[0]), runs, direct),
         out_shape=(
             jax.ShapeDtypeStruct((rows, heads * DH), jnp.bfloat16),
             pltpu.VMEM(values.shape, values.dtype),

time: 123 us -> 123 us (level)
  transfers between devices with their start and end apart: 22 -> 22, of which waited for: 8 -> 9; matrix products, arithmetic and copies ran while one was open for 2% -> 2% of each run, Pallas kernels for 22% -> 22%
where the time goes in v6:
time: 123 us
  starting transfers between devices  46.9 us (38%)
  waiting for transfers between devices  40.6 us (33%)
  Pallas kernels  29.8 us (24%)
  local copies, waits for them, and re-layouts  3.47 us (3%)
  other arithmetic  1.6 us (1%)
    ppermute x22, starting transfers between devices, permuted(): lax.ppermute(value, 'blk', [(i, t) for i, t in pairs if 0 <= t < count])  46.9 us
    ppermute x22, waiting for transfers between devices, permuted(): lax.ppermute(value, 'blk', [(i, t) for i, t in pairs if 0 <= t < count])  40.6 us
    pallas_call x2, Pallas kernels, weigh(): pl.pallas_call(functools.partial(score_kernel, entries, *kept.shape, grou...  18.1 us
    pallas_call x2, Pallas kernels, combine(): pl.pallas_call(functools.partial(value_kernel, *kept.shape, begin, groups...  6.93 us
    pallas_call x1, Pallas kernels, sum_lent(): pl.pallas_call(functools.partial(lent_kernel, *kept.shape, groups, len(ti...  4.79 us
    unnamed x16, local copies, waits for them, and re-layouts  3.18 us
  transfers between devices with their start and end apart: 22, of which 9 were waited for; matrix products, arithmetic and copies ran while one was open for 2% of the time, Pallas kernels for 22%

profile of v6, /device:TPU:0, one launch (start us, length us, event | category | flops | bytes accessed | tf_op | source)
XLA Modules:
  0.0 122.8 jit_solution(11619569872748939756)
XLA Ops:
  0.5 1.7 %collective-permute-start.5 = (bf16[256,2560]{1,0:T(8,128)(2,1)}, bf16[256,2560]{1,0:T(8,128)(2,1)}, u32[]{:S(2)}, u32[]{:S(2)}) collective-permute-start(bf16[256,2560]{1,0:T(8,128)(2,1)} %refs_0_.5), channel_id=1, source_target_pairs={{4,8},{5,9},{6,10},{7,11},{8,4},{9,5},{10,6},{11,7},{20,24},{21,25... | collective-permute-start | bytes 3932168 | tf_op jit(solution)/shard_map/ppermute | solution.py:27
  2.2 4.8 %collective-permute-start.4 = (bf16[256,2560]{1,0:T(8,128)(2,1)}, bf16[256,2560]{1,0:T(8,128)(2,1)}, u32[]{:S(2)}, u32[]{:S(2)}) collective-permute-start(bf16[256,2560]{1,0:T(8,128)(2,1)} %refs_0_.5), channel_id=1, source_target_pairs={{0,4},{1,5},{2,6},{3,7},{4,0},{5,1},{6,2},{7,3},{8,12},{9,13},{10,... | collective-permute-start | bytes 3932168 | tf_op jit(solution)/shard_map/ppermute | solution.py:27
  7.1 1.5 %collective-permute-start = (s32[2,8]{1,0:T(2,128)}, s32[2,8]{1,0:T(2,128)S(1)}, u32[]{:S(2)}, u32[]{:S(2)}) collective-permute-start(s32[2,8]{1,0:T(2,128)} %kept.5), channel_id=1, source_target_pairs={{0,2},{1,3},{2,0},{3,1},{4,6},{5,7},{6,4},{7,5},{8,10},{9,11},{10,... | collective-permute-start | bytes 200 | tf_op jit(solution)/shard_map/ppermute | solution.py:27
  8.6 2.3 %collective-permute-done.kept = s32[2,8]{1,0:T(2,128)S(1)} collective-permute-done((s32[2,8]{1,0:T(2,128)}, s32[2,8]{1,0:T(2,128)S(1)}, u32[]{:S(2)}, u32[]{:S(2)}) %collective-permute-start) | collective-permute-done | bytes 96 | tf_op jit(solution)/shard_map/ppermute | solution.py:27
  10.9 1.1 copy-done.1
  12.0 1.1 copy-done.5
  13.0 1.5 %collective-permute-start.3 = (bf16[256,2560]{1,0:T(8,128)(2,1)}, bf16[256,2560]{1,0:T(8,128)(2,1)}, u32[]{:S(2)}, u32[]{:S(2)}) collective-permute-start(bf16[256,2560]{1,0:T(8,128)(2,1)} %queries), channel_id=1, source_target_pairs={{0,2},{1,3},{2,0},{3,1},{4,6},{5,7},{6,4},{7,5},{8,10},{9,11},{10,... | collective-permute-start | bytes 3932168 | tf_op jit(solution)/shard_map/ppermute | solution.py:27
  15.3 2.6 %collective-permute-start.7 = (bf16[256,2560]{1,0:T(8,128)(2,1)}, bf16[256,2560]{1,0:T(8,128)(2,1)S(1)}, u32[]{:S(2)}, u32[]{:S(2)}) collective-permute-start(bf16[256,2560]{1,0:T(8,128)(2,1)} %refs_6_.1), channel_id=1, source_target_pairs={{0,4},{1,5},{2,6},{3,7},{4,0},{5,1},{6,2},{7,3},{8,12},{9,13},{10,... | collective-permute-start | bytes 3932168 | tf_op jit(solution)/shard_map/ppermute | solution.py:27
  17.8 19.5 %collective-permute-start.11 = (bf16[256,2560]{1,0:T(8,128)(2,1)}, bf16[256,2560]{1,0:T(8,128)(2,1)S(1)}, u32[]{:S(2)}, u32[]{:S(2)}) collective-permute-start(bf16[256,2560]{1,0:T(8,128)(2,1)} %collective-permute-done.5.refs_3_), channel_id=1, source_target_pairs={{0,4},{1,5},{2,6},{3,7},{4,0},{5,1},{6,2},{7,3},{8,12},{9,13},{10,... | collective-permute-start | bytes 3932168 | tf_op jit(solution)/shard_map/ppermute | solution.py:27
  37.4 0.7 collective-permute-start.12
  38.1 1.5 %broadcast_select_fusion.1.refs_1_ = bf16[256,2560]{1,0:T(8,128)(2,1)S(1)} fusion(bf16[256,2560]{1,0:T(8,128)(2,1)} %collective-permute-done.4.refs_2_, bf16[256,2560]{1,0:T(8,128)(2,1)} %collective-permute-done.5.refs_3_, pred[]{:T(512)S(6)} %eq.6), kind=kLoop, calls=%fused_computation.1 | loop fusion | flops 655360 | bytes 3932161 | tf_op jit(solution)/shard_map/jit(_where)/select_n | solution.py:348
  39.6 3.1 %collective-permute-done.3.queries = bf16[256,2560]{1,0:T(8,128)(2,1)} collective-permute-done((bf16[256,2560]{1,0:T(8,128)(2,1)}, bf16[256,2560]{1,0:T(8,128)(2,1)}, u32[]{:S(2)}, u32[]{:S(2)}) %collective-permute-start.3) | collective-permute-done | bytes 1310752 | tf_op jit(solution)/shard_map/ppermute | solution.py:27
  42.7 22.3 %collective-permute-done.7.refs_8_ = bf16[256,2560]{1,0:T(8,128)(2,1)S(1)} collective-permute-done((bf16[256,2560]{1,0:T(8,128)(2,1)}, bf16[256,2560]{1,0:T(8,128)(2,1)S(1)}, u32[]{:S(2)}, u32[]{:S(2)}) %collective-permute-start.7) | collective-permute-done | bytes 1310752 | tf_op jit(solution)/shard_map/ppermute | solution.py:27
  66.9 9.6 %weigh_lent.1 = (bf16[20,256,1024]{2,1,0:T(8,128)(2,1)S(1)}, f32[256,128]{1,0:T(8,128)S(1)}, bf16[1,256,2560]{2,1,0:T(8,128)(2,1)}) custom-call(s32[1]{0:T(128)} %bitcast.place, s32[2,8]{1,0:T(2,128)S(1)} %collective-permute-done.kept, bf16[256,2560]{1,0:T(8,128)(2,1)} %collective-permute-done.3.queries, bf16[256,2560]{1,0:T(8,128)(2,1)S(1)} %copy-done.4, ...), custom_call_target="tpu_custom_call" | custom-call | flops 1342177280 | bytes 10485760 | tf_op jit(solution)/shard_map/weigh_lent/pallas_call | solution.py:254
  76.5 1.6 %collective-permute-start.13 = (f32[256,128]{1,0:T(8,128)S(1)}, f32[256,128]{1,0:T(8,128)S(1)}, u32[]{:S(2)}, u32[]{:S(2)}) collective-permute-start(f32[256,128]{1,0:T(8,128)S(1)} %get-tuple-element.32.stats), channel_id=1, source_target_pairs={{0,2},{1,3},{2,0},{3,1},{4,6},{5,7},{6,4},{7,5},{8,10},{9,11},{10,... | collective-permute-start | bytes 393224 | tf_op jit(solution)/shard_map/ppermute | solution.py:27
  78.3 3.3 %collective-permute-done.13.lent = f32[256,128]{1,0:T(8,128)S(1)} collective-permute-done((f32[256,128]{1,0:T(8,128)S(1)}, f32[256,128]{1,0:T(8,128)S(1)}, u32[]{:S(2)}, u32[]{:S(2)}) %collective-permute-start.13) | collective-permute-done | bytes 131104 | tf_op jit(solution)/shard_map/ppermute | solution.py:27
  81.5 2.0 %collective-permute-start.17 = (bf16[256,1920]{1,0:T(8,128)(2,1)S(1)}, bf16[256,1920]{1,0:T(8,128)(2,1)S(1)}, u32[]{:S(2)}, u32[]{:S(2)}) collective-permute-start(bf16[256,1920]{1,0:T(8,128)(2,1)S(1)} %slice.26), channel_id=1, source_target_pairs={{0,4},{1,5},{2,6},{3,7},{4,0},{5,1},{6,2},{7,3},{8,12},{9,13},{10,... | collective-permute-start | bytes 2949128 | tf_op jit(solution)/shard_map/ppermute | solution.py:27
  83.6 0.9 collective-permute-start.18
  84.5 4.8 %sum_lent.1 = (bf16[256,640]{1,0:T(8,128)(2,1)S(1)}, bf16[256,640]{1,0:T(8,128)(2,1)S(1)}, bf16[256,640]{1,0:T(8,128)(2,1)S(1)}, bf16[256,640]{1,0:T(8,128)(2,1)S(1)}) custom-call(s32[1]{0:T(128)} %bitcast.place, s32[2,8]{1,0:T(2,128)S(1)} %collective-permute-done.kept, bf16[20,256,1024]{2,1,0:T(8,128)(2,1)S(1)} %get-tuple-element.31.weights, ...), custom_call_target="tpu_custom_call" | custom-call | flops 1342177280 | bytes 10485760 | tf_op jit(solution)/shard_map/sum_lent/pallas_call | solution.py:276
  89.3 1.6 %collective-permute-start.14 = (bf16[256,640]{1,0:T(8,128)(2,1)S(1)}, bf16[256,640]{1,0:T(8,128)(2,1)S(1)}, u32[]{:S(2)}, u32[]{:S(2)}) collective-permute-start(bf16[256,640]{1,0:T(8,128)(2,1)S(1)} %get-tuple-element.42), channel_id=1, source_target_pairs={{0,2},{1,3},{2,0},{3,1},{4,6},{5,7},{6,4},{7,5},{8,10},{9,11},{10,... | collective-permute-start | bytes 983048 | tf_op jit(solution)/shard_map/ppermute | solution.py:27
  90.9 2.2 %collective-permute-done.11.refs_4_ = bf16[256,2560]{1,0:T(8,128)(2,1)S(1)} collective-permute-done((bf16[256,2560]{1,0:T(8,128)(2,1)}, bf16[256,2560]{1,0:T(8,128)(2,1)S(1)}, u32[]{:S(2)}, u32[]{:S(2)}) %collective-permute-start.11) | collective-permute-done | bytes 1310752 | tf_op jit(solution)/shard_map/ppermute | solution.py:27
  93.1 1.5 %collective-permute-start.15 = (bf16[256,640]{1,0:T(8,128)(2,1)S(1)}, bf16[256,640]{1,0:T(8,128)(2,1)S(1)}, u32[]{:S(2)}, u32[]{:S(2)}) collective-permute-start(bf16[256,640]{1,0:T(8,128)(2,1)S(1)} %get-tuple-element.43), channel_id=1, source_target_pairs={{0,2},{1,3},{2,0},{3,1},{4,6},{5,7},{6,4},{7,5},{8,10},{9,11},{10,... | collective-permute-start | bytes 983048 | tf_op jit(solution)/shard_map/ppermute | solution.py:27
  95.2 8.4 %weigh_own.1 = (bf16[20,256,1024]{2,1,0:T(8,128)(2,1)S(1)}, f32[256,128]{1,0:T(8,128)S(1)}, bf16[6,256,2560]{2,1,0:T(8,128)(2,1)S(1)}) custom-call(s32[1]{0:T(128)} %bitcast.place, s32[2,8]{1,0:T(2,128)S(1)} %copy-done.7, bf16[256,2560]{1,0:T(8,128)(2,1)S(1)} %copy-done.3, bf16[256,2560]{1,0:T(8,128)(2,1)S(1)} %copy-done.4, bf16[256,2560]{1,0:T(8,128)(2,1)S(1)} %copy-done.6, ...), custom_call_target="tpu_custom_call" | custom-call | flops 1342177280 | bytes 10485760 | tf_op jit(solution)/shard_map/weigh_own/pallas_call | solution.py:254
  103.7 2.1 %collective-permute-start.20 = (bf16[256,640]{1,0:T(8,128)(2,1)S(1)}, bf16[256,640]{1,0:T(8,128)(2,1)S(1)}, u32[]{:S(2)}, u32[]{:S(2)}) collective-permute-start(bf16[256,640]{1,0:T(8,128)(2,1)S(1)} %slice.28), channel_id=1, source_target_pairs={{0,4},{1,5},{2,6},{3,7},{4,0},{5,1},{6,2},{7,3},{8,12},{9,13},{10,... | collective-permute-start | bytes 983048 | tf_op jit(solution)/shard_map/ppermute | solution.py:27
  105.8 1.3 %collective-permute-done.15.refs_2_ = bf16[256,640]{1,0:T(8,128)(2,1)S(1)} collective-permute-done((bf16[256,640]{1,0:T(8,128)(2,1)S(1)}, bf16[256,640]{1,0:T(8,128)(2,1)S(1)}, u32[]{:S(2)}, u32[]{:S(2)}) %collective-permute-start.15) | collective-permute-done | bytes 327712 | tf_op jit(solution)/shard_map/ppermute | solution.py:27
  107.1 0.9 collective-permute-start.21
  108.0 3.4 %collective-permute-done.16.refs_3_ = bf16[256,640]{1,0:T(8,128)(2,1)S(1)} collective-permute-done((bf16[256,640]{1,0:T(8,128)(2,1)S(1)}, bf16[256,640]{1,0:T(8,128)(2,1)S(1)}, u32[]{:S(2)}, u32[]{:S(2)}) %collective-permute-start.16) | collective-permute-done | bytes 327712 | tf_op jit(solution)/shard_map/ppermute | solution.py:27
  111.3 1.5 %collective-permute-start.19 = (bf16[256,640]{1,0:T(8,128)(2,1)S(1)}, bf16[256,640]{1,0:T(8,128)(2,1)S(1)}, u32[]{:S(2)}, u32[]{:S(2)}) collective-permute-start(bf16[256,640]{1,0:T(8,128)(2,1)S(1)} %get-tuple-element.48), channel_id=1, source_target_pairs={{0,2},{1,3},{2,0},{3,1},{4,6},{5,7},{6,4},{7,5},{8,10},{9,11},{10,... | collective-permute-start | bytes 983048 | tf_op jit(solution)/shard_map/ppermute | solution.py:27
  112.9 1.3 %collective-permute-done.17.refs_4_ = bf16[256,1920]{1,0:T(8,128)(2,1)S(1)} collective-permute-done((bf16[256,1920]{1,0:T(8,128)(2,1)S(1)}, bf16[256,1920]{1,0:T(8,128)(2,1)S(1)}, u32[]{:S(2)}, u32[]{:S(2)}) %collective-permute-start.17) | collective-permute-done | bytes 983072 | tf_op jit(solution)/shard_map/ppermute | solution.py:27
  114.2 4.5 %combine_0.1 = (bf16[256,2560]{1,0:T(8,128)(2,1)}, bf16[6,256,2560]{2,1,0:T(8,128)(2,1)S(1)}) custom-call(s32[1]{0:T(128)} %bitcast.place, s32[2,8]{1,0:T(2,128)S(1)} %copy-done.7, bf16[20,256,1024]{2,1,0:T(8,128)(2,1)S(1)} %get-tuple-element.39.weights, f32[256,128]{1,0:T(8,128)S(1)} %get-tuple-element.40.own, ...), custom_call_target="tpu_custom_call", output_to_operand_aliasing={{1}: (5, {})} | custom-call | flops 1006632960 | bytes 7864320 | tf_op jit(solution)/shard_map/combine_0/pallas_call | solution.py:310
  118.7 1.5 %collective-permute-done.20.refs_2_ = bf16[256,640]{1,0:T(8,128)(2,1)S(1)} collective-permute-done((bf16[256,640]{1,0:T(8,128)(2,1)S(1)}, bf16[256,640]{1,0:T(8,128)(2,1)S(1)}, u32[]{:S(2)}, u32[]{:S(2)}) %collective-permute-start.20) | collective-permute-done | bytes 327712 | tf_op jit(solution)/shard_map/ppermute | solution.py:27
  120.2 2.4 %combine_15.1 = (bf16[256,2560]{1,0:T(8,128)(2,1)}, bf16[6,256,2560]{2,1,0:T(8,128)(2,1)S(1)}) custom-call(s32[1]{0:T(128)} %bitcast.place, s32[2,8]{1,0:T(2,128)S(1)} %copy-done.7, bf16[20,256,1024]{2,1,0:T(8,128)(2,1)S(1)} %get-tuple-element.39.weights, f32[256,128]{1,0:T(8,128)S(1)} %get-tuple-element.40.own, ...), custom_call_target="tpu_custom_call", output_to_operand_aliasing={{1}: (5, {}), {0}: (9, {})} | custom-call | flops 335544320 | bytes 2621440 | tf_op jit(solution)/shard_map/combine_15/pallas_call | solution.py:310
  (40 shorter events, 3.8 us)
Async XLA Ops:
  0.0 10.9 %collective-permute-start.2 = (bf16[256,2560]{1,0:T(8,128)(2,1)}, bf16[256,2560]{1,0:T(8,128)(2,1)S(1)}, u32[]{:S(2)}, u32[]{:S(2)}) collective-permute-start(bf16[256,2560]{1,0:T(8,128)(2,1)} %refs_6_.1), channel_id=1, source_target_pairs={{0,1},{1,0},{2,3},{3,2},{4,5},{5,4},{6,7},{7,6},{8,9},{9,8},{10,11... | collective-permute-start | bytes 3932168 | tf_op jit(solution)/shard_map/ppermute | solution.py:27
  0.5 11.5 %collective-permute-start.1 = (bf16[256,2560]{1,0:T(8,128)(2,1)}, bf16[256,2560]{1,0:T(8,128)(2,1)S(1)}, u32[]{:S(2)}, u32[]{:S(2)}) collective-permute-start(bf16[256,2560]{1,0:T(8,128)(2,1)} %refs_0_.5), channel_id=1, source_target_pairs={{0,1},{1,0},{2,3},{3,2},{4,5},{5,4},{6,7},{7,6},{8,9},{9,8},{10,11... | collective-permute-start | bytes 3932168 | tf_op jit(solution)/shard_map/ppermute | solution.py:27
  0.5 17.3 %collective-permute-start.5 = (bf16[256,2560]{1,0:T(8,128)(2,1)}, bf16[256,2560]{1,0:T(8,128)(2,1)}, u32[]{:S(2)}, u32[]{:S(2)}) collective-permute-start(bf16[256,2560]{1,0:T(8,128)(2,1)} %refs_0_.5), channel_id=1, source_target_pairs={{4,8},{5,9},{6,10},{7,11},{8,4},{9,5},{10,6},{11,7},{20,24},{21,25... | collective-permute-start | bytes 3932168 | tf_op jit(solution)/shard_map/ppermute | solution.py:27
  2.2 35.1 %collective-permute-start.4 = (bf16[256,2560]{1,0:T(8,128)(2,1)}, bf16[256,2560]{1,0:T(8,128)(2,1)}, u32[]{:S(2)}, u32[]{:S(2)}) collective-permute-start(bf16[256,2560]{1,0:T(8,128)(2,1)} %refs_0_.5), channel_id=1, source_target_pairs={{0,4},{1,5},{2,6},{3,7},{4,0},{5,1},{6,2},{7,3},{8,12},{9,13},{10,... | collective-permute-start | bytes 3932168 | tf_op jit(solution)/shard_map/ppermute | solution.py:27
  7.1 3.8 %collective-permute-start = (s32[2,8]{1,0:T(2,128)}, s32[2,8]{1,0:T(2,128)S(1)}, u32[]{:S(2)}, u32[]{:S(2)}) collective-permute-start(s32[2,8]{1,0:T(2,128)} %kept.5), channel_id=1, source_target_pairs={{0,2},{1,3},{2,0},{3,1},{4,6},{5,7},{6,4},{7,5},{8,10},{9,11},{10,... | collective-permute-start | bytes 200 | tf_op jit(solution)/shard_map/ppermute | solution.py:27
  10.9 1.1 copy-start.1
  12.0 1.1 copy-start.5
  13.0 29.7 %collective-permute-start.3 = (bf16[256,2560]{1,0:T(8,128)(2,1)}, bf16[256,2560]{1,0:T(8,128)(2,1)}, u32[]{:S(2)}, u32[]{:S(2)}) collective-permute-start(bf16[256,2560]{1,0:T(8,128)(2,1)} %queries), channel_id=1, source_target_pairs={{0,2},{1,3},{2,0},{3,1},{4,6},{5,7},{6,4},{7,5},{8,10},{9,11},{10,... | collective-permute-start | bytes 3932168 | tf_op jit(solution)/shard_map/ppermute | solution.py:27
  14.5 28.2 %collective-permute-start.8 = (bf16[256,2560]{1,0:T(8,128)(2,1)}, bf16[256,2560]{1,0:T(8,128)(2,1)S(1)}, u32[]{:S(2)}, u32[]{:S(2)}) collective-permute-start(bf16[256,2560]{1,0:T(8,128)(2,1)} %refs_6_.1), channel_id=1, source_target_pairs={{4,8},{5,9},{6,10},{7,11},{8,4},{9,5},{10,6},{11,7},{20,24},{21,25... | collective-permute-start | bytes 3932168 | tf_op jit(solution)/shard_map/ppermute | solution.py:27
  15.3 49.7 %collective-permute-start.7 = (bf16[256,2560]{1,0:T(8,128)(2,1)}, bf16[256,2560]{1,0:T(8,128)(2,1)S(1)}, u32[]{:S(2)}, u32[]{:S(2)}) collective-permute-start(bf16[256,2560]{1,0:T(8,128)(2,1)} %refs_6_.1), channel_id=1, source_target_pairs={{0,4},{1,5},{2,6},{3,7},{4,0},{5,1},{6,2},{7,3},{8,12},{9,13},{10,... | collective-permute-start | bytes 3932168 | tf_op jit(solution)/shard_map/ppermute | solution.py:27
  17.8 75.3 %collective-permute-start.11 = (bf16[256,2560]{1,0:T(8,128)(2,1)}, bf16[256,2560]{1,0:T(8,128)(2,1)S(1)}, u32[]{:S(2)}, u32[]{:S(2)}) collective-permute-start(bf16[256,2560]{1,0:T(8,128)(2,1)} %collective-permute-done.5.refs_3_), channel_id=1, source_target_pairs={{0,4},{1,5},{2,6},{3,7},{4,0},{5,1},{6,2},{7,3},{8,12},{9,13},{10,... | collective-permute-start | bytes 3932168 | tf_op jit(solution)/shard_map/ppermute | solution.py:27
  37.4 57.2 %collective-permute-start.12 = (bf16[256,2560]{1,0:T(8,128)(2,1)}, bf16[256,2560]{1,0:T(8,128)(2,1)S(1)}, u32[]{:S(2)}, u32[]{:S(2)}) collective-permute-start(bf16[256,2560]{1,0:T(8,128)(2,1)} %collective-permute-done.4.refs_2_), channel_id=1, source_target_pairs={{4,8},{5,9},{6,10},{7,11},{8,4},{9,5},{10,6},{11,7},{20,24},{21,25... | collective-permute-start | bytes 3932168 | tf_op jit(solution)/shard_map/ppermute | solution.py:27
  42.7 23.1 %collective-permute-start.6 = (bf16[256,2560]{1,0:T(8,128)(2,1)S(1)}, bf16[256,2560]{1,0:T(8,128)(2,1)S(1)}, u32[]{:S(2)}, u32[]{:S(2)}) collective-permute-start(bf16[256,2560]{1,0:T(8,128)(2,1)S(1)} %broadcast_select_fusion.1.refs_1_), channel_id=1, source_target_pairs={{0,1},{1,0},{2,3},{3,2},{4,5},{5,4},{6,7},{7,6},{8,9},{9,8},{10,11... | collective-permute-start | bytes 3932168 | tf_op jit(solution)/shard_map/ppermute | solution.py:27
  65.2 1.3 %copy-start.4 = (bf16[256,2560]{1,0:T(8,128)(2,1)S(1)}, bf16[256,2560]{1,0:T(8,128)(2,1)}, u32[]{:S(2)}) copy-start(bf16[256,2560]{1,0:T(8,128)(2,1)} %refs_0_.5) | copy-start | bytes 3932164
  65.2 1.7 %copy-start.6 = (bf16[256,2560]{1,0:T(8,128)(2,1)S(1)}, bf16[256,2560]{1,0:T(8,128)(2,1)}, u32[]{:S(2)}) copy-start(bf16[256,2560]{1,0:T(8,128)(2,1)} %copy-done.5) | copy-start | bytes 3932164
  65.3 18.3 %collective-permute-start.10 = (bf16[256,1280]{1,0:T(8,128)(2,1)S(1)}, bf16[256,1280]{1,0:T(8,128)(2,1)S(1)}, u32[]{:S(2)}, u32[]{:S(2)}) collective-permute-start(bf16[256,1280]{1,0:T(8,128)(2,1)S(1)} %get-tuple-element.53), channel_id=1, source_target_pairs={{0,1},{1,0},{2,3},{3,2},{4,5},{5,4},{6,7},{7,6},{8,9},{9,8},{10,11... | collective-permute-start | bytes 1966088 | tf_op jit(solution)/shard_map/ppermute | solution.py:27
  65.3 19.1 %collective-permute-start.9 = (bf16[256,1280]{1,0:T(8,128)(2,1)S(1)}, bf16[256,1280]{1,0:T(8,128)(2,1)S(1)}, u32[]{:S(2)}, u32[]{:S(2)}) collective-permute-start(bf16[256,1280]{1,0:T(8,128)(2,1)S(1)} %get-tuple-element.54), channel_id=1, source_target_pairs={{0,1},{1,0},{2,3},{3,2},{4,5},{5,4},{6,7},{7,6},{8,9},{9,8},{10,11... | collective-permute-start | bytes 1966088 | tf_op jit(solution)/shard_map/ppermute | solution.py:27
  76.5 5.0 %collective-permute-start.13 = (f32[256,128]{1,0:T(8,128)S(1)}, f32[256,128]{1,0:T(8,128)S(1)}, u32[]{:S(2)}, u32[]{:S(2)}) collective-permute-start(f32[256,128]{1,0:T(8,128)S(1)} %get-tuple-element.32.stats), channel_id=1, source_target_pairs={{0,2},{1,3},{2,0},{3,1},{4,6},{5,7},{6,4},{7,5},{8,10},{9,11},{10,... | collective-permute-start | bytes 393224 | tf_op jit(solution)/shard_map/ppermute | solution.py:27
  78.1 6.4 %copy-start.2 = (bf16[256,2560]{1,0:T(8,128)(2,1)S(1)}, bf16[256,2560]{1,0:T(8,128)(2,1)}, u32[]{:S(2)}) copy-start(bf16[256,2560]{1,0:T(8,128)(2,1)} %copy-done.1) | copy-start | bytes 3932164
  78.2 6.3 %copy-start = (bf16[256,2560]{1,0:T(8,128)(2,1)S(1)}, bf16[256,2560]{1,0:T(8,128)(2,1)}, u32[]{:S(2)}) copy-start(bf16[256,2560]{1,0:T(8,128)(2,1)} %refs_6_.1) | copy-start | bytes 3932164
  81.5 32.6 %collective-permute-start.17 = (bf16[256,1920]{1,0:T(8,128)(2,1)S(1)}, bf16[256,1920]{1,0:T(8,128)(2,1)S(1)}, u32[]{:S(2)}, u32[]{:S(2)}) collective-permute-start(bf16[256,1920]{1,0:T(8,128)(2,1)S(1)} %slice.26), channel_id=1, source_target_pairs={{0,4},{1,5},{2,6},{3,7},{4,0},{5,1},{6,2},{7,3},{8,12},{9,13},{10,... | collective-permute-start | bytes 2949128 | tf_op jit(solution)/shard_map/ppermute | solution.py:27
  83.6 30.6 %collective-permute-start.18 = (bf16[256,1920]{1,0:T(8,128)(2,1)S(1)}, bf16[256,1920]{1,0:T(8,128)(2,1)S(1)}, u32[]{:S(2)}, u32[]{:S(2)}) collective-permute-start(bf16[256,1920]{1,0:T(8,128)(2,1)S(1)} %slice.27), channel_id=1, source_target_pairs={{4,8},{5,9},{6,10},{7,11},{8,4},{9,5},{10,6},{11,7},{20,24},{21,25... | collective-permute-start | bytes 2949128 | tf_op jit(solution)/shard_map/ppermute | solution.py:27
  89.3 5.9 %copy-start.3 = (bf16[256,2560]{1,0:T(8,128)(2,1)S(1)}, bf16[256,2560]{1,0:T(8,128)(2,1)}, u32[]{:S(2)}) copy-start(bf16[256,2560]{1,0:T(8,128)(2,1)} %queries) | copy-start | bytes 3932164
  89.3 5.9 %copy-start.7 = (s32[2,8]{1,0:T(2,128)S(1)}, s32[2,8]{1,0:T(2,128)}, u32[]{:S(2)}) copy-start(s32[2,8]{1,0:T(2,128)} %kept.5) | copy-start | bytes 196
  89.3 14.3 %collective-permute-start.14 = (bf16[256,640]{1,0:T(8,128)(2,1)S(1)}, bf16[256,640]{1,0:T(8,128)(2,1)S(1)}, u32[]{:S(2)}, u32[]{:S(2)}) collective-permute-start(bf16[256,640]{1,0:T(8,128)(2,1)S(1)} %get-tuple-element.42), channel_id=1, source_target_pairs={{0,2},{1,3},{2,0},{3,1},{4,6},{5,7},{6,4},{7,5},{8,10},{9,11},{10,... | collective-permute-start | bytes 983048 | tf_op jit(solution)/shard_map/ppermute | solution.py:27
  93.1 14.0 %collective-permute-start.15 = (bf16[256,640]{1,0:T(8,128)(2,1)S(1)}, bf16[256,640]{1,0:T(8,128)(2,1)S(1)}, u32[]{:S(2)}, u32[]{:S(2)}) collective-permute-start(bf16[256,640]{1,0:T(8,128)(2,1)S(1)} %get-tuple-element.43), channel_id=1, source_target_pairs={{0,2},{1,3},{2,0},{3,1},{4,6},{5,7},{6,4},{7,5},{8,10},{9,11},{10,... | collective-permute-start | bytes 983048 | tf_op jit(solution)/shard_map/ppermute | solution.py:27
  94.6 16.7 %collective-permute-start.16 = (bf16[256,640]{1,0:T(8,128)(2,1)S(1)}, bf16[256,640]{1,0:T(8,128)(2,1)S(1)}, u32[]{:S(2)}, u32[]{:S(2)}) collective-permute-start(bf16[256,640]{1,0:T(8,128)(2,1)S(1)} %get-tuple-element.44), channel_id=1, source_target_pairs={{0,2},{1,3},{2,0},{3,1},{4,6},{5,7},{6,4},{7,5},{8,10},{9,11},{10,... | collective-permute-start | bytes 983048 | tf_op jit(solution)/shard_map/ppermute | solution.py:27
  103.7 16.6 %collective-permute-start.20 = (bf16[256,640]{1,0:T(8,128)(2,1)S(1)}, bf16[256,640]{1,0:T(8,128)(2,1)S(1)}, u32[]{:S(2)}, u32[]{:S(2)}) collective-permute-start(bf16[256,640]{1,0:T(8,128)(2,1)S(1)} %slice.28), channel_id=1, source_target_pairs={{0,4},{1,5},{2,6},{3,7},{4,0},{5,1},{6,2},{7,3},{8,12},{9,13},{10,... | collective-permute-start | bytes 983048 | tf_op jit(solution)/shard_map/ppermute | solution.py:27
  107.1 13.2 %collective-permute-start.21 = (bf16[256,640]{1,0:T(8,128)(2,1)S(1)}, bf16[256,640]{1,0:T(8,128)(2,1)S(1)}, u32[]{:S(2)}, u32[]{:S(2)}) collective-permute-start(bf16[256,640]{1,0:T(8,128)(2,1)S(1)} %slice.29), channel_id=1, source_target_pairs={{4,8},{5,9},{6,10},{7,11},{8,4},{9,5},{10,6},{11,7},{20,24},{21,25... | collective-permute-start | bytes 983048 | tf_op jit(solution)/shard_map/ppermute | solution.py:27
  111.3 8.9 %collective-permute-start.19 = (bf16[256,640]{1,0:T(8,128)(2,1)S(1)}, bf16[256,640]{1,0:T(8,128)(2,1)S(1)}, u32[]{:S(2)}, u32[]{:S(2)}) collective-permute-start(bf16[256,640]{1,0:T(8,128)(2,1)S(1)} %get-tuple-element.48), channel_id=1, source_target_pairs={{0,2},{1,3},{2,0},{3,1},{4,6},{5,7},{6,4},{7,5},{8,10},{9,11},{10,... | collective-permute-start | bytes 983048 | tf_op jit(solution)/shard_map/ppermute | solution.py:27

commit v7 on v6

--- a/solution.py
+++ b/solution.py
@@ -340,9 +340,10 @@
 
     k_odd, k_even = swapped_odd(keys), swapped(keys, 4)
     asked_kept = swapped(kept, 2)
-    k_pair, v_pair = swapped(keys, 1), swapped(values, 1)
-    asked = swapped(after(queries, asked_kept, k_pair, v_pair), 2)
-    later = after(values, asked_kept, k_pair, v_pair)
+    v_pair = swapped(values, 1)
+    k_pair = swapped(after(keys, k_even, k_odd), 1)
+    asked = swapped(after(queries, asked_kept, v_pair), 2)
+    later = after(values, asked_kept, v_pair)
     v_odd, v_even = swapped_odd(later), swapped(later, 4)
     k_odd_far, k_even_far = swapped_odd(k_even), swapped(k_odd, 4)
     k_level = jnp.where(same_side, k_even, k_odd)

time: 123 us -> 123 us (level)
  waiting for transfers between devices: 40.6 us -> 59.6 us
  starting transfers between devices: 46.9 us -> 29.5 us
  local copies, waits for them, and re-layouts: 3.47 us -> 2 us
    ppermute x22, waiting for transfers between devices: 40.6 us -> 59.6 us  [permuted(): lax.ppermute(value, 'blk', [(i, t) for i, t in pairs if 0 <= t < count])]
    ppermute x22, starting transfers between devices: 46.9 us -> 29.5 us  [permuted(): lax.ppermute(value, 'blk', [(i, t) for i, t in pairs if 0 <= t < count])]
    unnamed x16 -> x12, local copies, waits for them, and re-layouts: 3.18 us -> 1.71 us
  transfers between devices with their start and end apart: 22 -> 22, of which waited for: 9 -> 10; matrix products, arithmetic and copies ran while one was open for 2% -> 2% of each run, Pallas kernels for 22% -> 22%
where the time goes in v7:
time: 123 us
  waiting for transfers between devices  59.6 us (48%)
  Pallas kernels  29.7 us (24%)
  starting transfers between devices  29.5 us (24%)
  local copies, waits for them, and re-layouts  2 us (2%)
  other arithmetic  1.59 us (1%)
    ppermute x22, waiting for transfers between devices, permuted(): lax.ppermute(value, 'blk', [(i, t) for i, t in pairs if 0 <= t < count])  59.6 us
    ppermute x22, starting transfers between devices, permuted(): lax.ppermute(value, 'blk', [(i, t) for i, t in pairs if 0 <= t < count])  29.5 us
    pallas_call x2, Pallas kernels, weigh(): pl.pallas_call(functools.partial(score_kernel, entries, *kept.shape, grou...  18.1 us
    pallas_call x2, Pallas kernels, combine(): pl.pallas_call(functools.partial(value_kernel, *kept.shape, begin, groups...  6.84 us
    pallas_call x1, Pallas kernels, sum_lent(): pl.pallas_call(functools.partial(lent_kernel, *kept.shape, groups, len(ti...  4.78 us
  transfers between devices with their start and end apart: 22, of which 10 were waited for; matrix products, arithmetic and copies ran while one was open for 2% of the time, Pallas kernels for 22%

profile of v7, /device:TPU:0, one launch (start us, length us, event | category | flops | bytes accessed | tf_op | source)
XLA Modules:
  0.0 122.8 jit_solution(11431776823417037558)
XLA Ops:
  0.5 1.7 %collective-permute-start.4 = (bf16[256,2560]{1,0:T(8,128)(2,1)}, bf16[256,2560]{1,0:T(8,128)(2,1)}, u32[]{:S(2)}, u32[]{:S(2)}) collective-permute-start(bf16[256,2560]{1,0:T(8,128)(2,1)} %refs_0_.5), channel_id=1, source_target_pairs={{4,8},{5,9},{6,10},{7,11},{8,4},{9,5},{10,6},{11,7},{20,24},{21,25... | collective-permute-start | bytes 3932168 | tf_op jit(solution)/shard_map/ppermute | solution.py:27
  2.2 4.4 %collective-permute-start.3 = (bf16[256,2560]{1,0:T(8,128)(2,1)}, bf16[256,2560]{1,0:T(8,128)(2,1)}, u32[]{:S(2)}, u32[]{:S(2)}) collective-permute-start(bf16[256,2560]{1,0:T(8,128)(2,1)} %refs_0_.5), channel_id=1, source_target_pairs={{0,4},{1,5},{2,6},{3,7},{4,0},{5,1},{6,2},{7,3},{8,12},{9,13},{10,... | collective-permute-start | bytes 3932168 | tf_op jit(solution)/shard_map/ppermute | solution.py:27
  6.6 1.5 %collective-permute-start = (s32[2,8]{1,0:T(2,128)}, s32[2,8]{1,0:T(2,128)S(1)}, u32[]{:S(2)}, u32[]{:S(2)}) collective-permute-start(s32[2,8]{1,0:T(2,128)} %kept.5), channel_id=1, source_target_pairs={{0,2},{1,3},{2,0},{3,1},{4,6},{5,7},{6,4},{7,5},{8,10},{9,11},{10,... | collective-permute-start | bytes 200 | tf_op jit(solution)/shard_map/ppermute | solution.py:27
  8.1 2.3 %collective-permute-done.kept = s32[2,8]{1,0:T(2,128)S(1)} collective-permute-done((s32[2,8]{1,0:T(2,128)}, s32[2,8]{1,0:T(2,128)S(1)}, u32[]{:S(2)}, u32[]{:S(2)}) %collective-permute-start) | collective-permute-done | bytes 96 | tf_op jit(solution)/shard_map/ppermute | solution.py:27
  10.4 1.1 copy-done.1
  11.4 1.5 %collective-permute-start.2 = (bf16[256,2560]{1,0:T(8,128)(2,1)}, bf16[256,2560]{1,0:T(8,128)(2,1)}, u32[]{:S(2)}, u32[]{:S(2)}) collective-permute-start(bf16[256,2560]{1,0:T(8,128)(2,1)} %queries), channel_id=1, source_target_pairs={{0,2},{1,3},{2,0},{3,1},{4,6},{5,7},{6,4},{7,5},{8,10},{9,11},{10,... | collective-permute-start | bytes 3932168 | tf_op jit(solution)/shard_map/ppermute | solution.py:27
  12.9 0.7 collective-permute-start.8
  13.7 2.6 %collective-permute-start.7 = (bf16[256,2560]{1,0:T(8,128)(2,1)}, bf16[256,2560]{1,0:T(8,128)(2,1)S(1)}, u32[]{:S(2)}, u32[]{:S(2)}) collective-permute-start(bf16[256,2560]{1,0:T(8,128)(2,1)} %refs_6_.1), channel_id=1, source_target_pairs={{0,4},{1,5},{2,6},{3,7},{4,0},{5,1},{6,2},{7,3},{8,12},{9,13},{10,... | collective-permute-start | bytes 3932168 | tf_op jit(solution)/shard_map/ppermute | solution.py:27
  16.2 20.2 %collective-permute-done.3.refs_2_ = bf16[256,2560]{1,0:T(8,128)(2,1)} collective-permute-done((bf16[256,2560]{1,0:T(8,128)(2,1)}, bf16[256,2560]{1,0:T(8,128)(2,1)}, u32[]{:S(2)}, u32[]{:S(2)}) %collective-permute-start.3) | collective-permute-done | bytes 1310752 | tf_op jit(solution)/shard_map/ppermute | solution.py:27
  36.5 2.1 %collective-permute-start.11 = (bf16[256,2560]{1,0:T(8,128)(2,1)}, bf16[256,2560]{1,0:T(8,128)(2,1)S(1)}, u32[]{:S(2)}, u32[]{:S(2)}) collective-permute-start(bf16[256,2560]{1,0:T(8,128)(2,1)} %collective-permute-done.4.refs_3_), channel_id=1, source_target_pairs={{0,4},{1,5},{2,6},{3,7},{4,0},{5,1},{6,2},{7,3},{8,12},{9,13},{10,... | collective-permute-start | bytes 3932168 | tf_op jit(solution)/shard_map/ppermute | solution.py:27
  38.5 1.5 %broadcast_select_fusion.1.refs_1_ = bf16[256,2560]{1,0:T(8,128)(2,1)S(1)} fusion(bf16[256,2560]{1,0:T(8,128)(2,1)} %collective-permute-done.3.refs_2_, bf16[256,2560]{1,0:T(8,128)(2,1)} %collective-permute-done.4.refs_3_, pred[]{:T(512)S(6)} %eq.6), kind=kLoop, calls=%fused_computation.1 | loop fusion | flops 655360 | bytes 3932161 | tf_op jit(solution)/shard_map/jit(_where)/select_n | solution.py:349
  40.0 1.6 %collective-permute-done.2.queries = bf16[256,2560]{1,0:T(8,128)(2,1)} collective-permute-done((bf16[256,2560]{1,0:T(8,128)(2,1)}, bf16[256,2560]{1,0:T(8,128)(2,1)}, u32[]{:S(2)}, u32[]{:S(2)}) %collective-permute-start.2) | collective-permute-done | bytes 1310752 | tf_op jit(solution)/shard_map/ppermute | solution.py:27
  41.6 0.7 collective-permute-start.12
  42.4 22.0 %collective-permute-done.7.refs_8_ = bf16[256,2560]{1,0:T(8,128)(2,1)S(1)} collective-permute-done((bf16[256,2560]{1,0:T(8,128)(2,1)}, bf16[256,2560]{1,0:T(8,128)(2,1)S(1)}, u32[]{:S(2)}, u32[]{:S(2)}) %collective-permute-start.7) | collective-permute-done | bytes 1310752 | tf_op jit(solution)/shard_map/ppermute | solution.py:27
  65.9 9.7 %weigh_lent.1 = (bf16[20,256,1024]{2,1,0:T(8,128)(2,1)S(1)}, f32[256,128]{1,0:T(8,128)S(1)}, bf16[1,256,2560]{2,1,0:T(8,128)(2,1)}) custom-call(s32[1]{0:T(128)} %bitcast.place, s32[2,8]{1,0:T(2,128)S(1)} %collective-permute-done.kept, bf16[256,2560]{1,0:T(8,128)(2,1)} %collective-permute-done.2.queries, bf16[256,2560]{1,0:T(8,128)(2,1)S(1)} %copy-done.4, ...), custom_call_target="tpu_custom_call" | custom-call | flops 1342177280 | bytes 10485760 | tf_op jit(solution)/shard_map/weigh_lent/pallas_call | solution.py:254
  75.6 1.6 %collective-permute-start.13 = (f32[256,128]{1,0:T(8,128)S(1)}, f32[256,128]{1,0:T(8,128)S(1)}, u32[]{:S(2)}, u32[]{:S(2)}) collective-permute-start(f32[256,128]{1,0:T(8,128)S(1)} %get-tuple-element.34.stats), channel_id=1, source_target_pairs={{0,2},{1,3},{2,0},{3,1},{4,6},{5,7},{6,4},{7,5},{8,10},{9,11},{10,... | collective-permute-start | bytes 393224 | tf_op jit(solution)/shard_map/ppermute | solution.py:27
  77.3 3.3 %collective-permute-done.13.lent = f32[256,128]{1,0:T(8,128)S(1)} collective-permute-done((f32[256,128]{1,0:T(8,128)S(1)}, f32[256,128]{1,0:T(8,128)S(1)}, u32[]{:S(2)}, u32[]{:S(2)}) %collective-permute-start.13) | collective-permute-done | bytes 131104 | tf_op jit(solution)/shard_map/ppermute | solution.py:27
  80.6 2.5 %collective-permute-start.17 = (bf16[256,1920]{1,0:T(8,128)(2,1)S(1)}, bf16[256,1920]{1,0:T(8,128)(2,1)S(1)}, u32[]{:S(2)}, u32[]{:S(2)}) collective-permute-start(bf16[256,1920]{1,0:T(8,128)(2,1)S(1)} %slice.26), channel_id=1, source_target_pairs={{0,4},{1,5},{2,6},{3,7},{4,0},{5,1},{6,2},{7,3},{8,12},{9,13},{10,... | collective-permute-start | bytes 2949128 | tf_op jit(solution)/shard_map/ppermute | solution.py:27
  83.1 0.9 collective-permute-start.18
  84.0 4.8 %sum_lent.1 = (bf16[256,640]{1,0:T(8,128)(2,1)S(1)}, bf16[256,640]{1,0:T(8,128)(2,1)S(1)}, bf16[256,640]{1,0:T(8,128)(2,1)S(1)}, bf16[256,640]{1,0:T(8,128)(2,1)S(1)}) custom-call(s32[1]{0:T(128)} %bitcast.place, s32[2,8]{1,0:T(2,128)S(1)} %collective-permute-done.kept, bf16[20,256,1024]{2,1,0:T(8,128)(2,1)S(1)} %get-tuple-element.33.weights, ...), custom_call_target="tpu_custom_call" | custom-call | flops 1342177280 | bytes 10485760 | tf_op jit(solution)/shard_map/sum_lent/pallas_call | solution.py:276
  88.9 1.6 %collective-permute-start.14 = (bf16[256,640]{1,0:T(8,128)(2,1)S(1)}, bf16[256,640]{1,0:T(8,128)(2,1)S(1)}, u32[]{:S(2)}, u32[]{:S(2)}) collective-permute-start(bf16[256,640]{1,0:T(8,128)(2,1)S(1)} %get-tuple-element.44), channel_id=1, source_target_pairs={{0,2},{1,3},{2,0},{3,1},{4,6},{5,7},{6,4},{7,5},{8,10},{9,11},{10,... | collective-permute-start | bytes 983048 | tf_op jit(solution)/shard_map/ppermute | solution.py:27
  90.4 2.1 %collective-permute-done.11.refs_4_ = bf16[256,2560]{1,0:T(8,128)(2,1)S(1)} collective-permute-done((bf16[256,2560]{1,0:T(8,128)(2,1)}, bf16[256,2560]{1,0:T(8,128)(2,1)S(1)}, u32[]{:S(2)}, u32[]{:S(2)}) %collective-permute-start.11) | collective-permute-done | bytes 1310752 | tf_op jit(solution)/shard_map/ppermute | solution.py:27
  92.5 1.5 %collective-permute-start.15 = (bf16[256,640]{1,0:T(8,128)(2,1)S(1)}, bf16[256,640]{1,0:T(8,128)(2,1)S(1)}, u32[]{:S(2)}, u32[]{:S(2)}) collective-permute-start(bf16[256,640]{1,0:T(8,128)(2,1)S(1)} %get-tuple-element.45), channel_id=1, source_target_pairs={{0,2},{1,3},{2,0},{3,1},{4,6},{5,7},{6,4},{7,5},{8,10},{9,11},{10,... | collective-permute-start | bytes 983048 | tf_op jit(solution)/shard_map/ppermute | solution.py:27
  94.6 8.4 %weigh_own.1 = (bf16[20,256,1024]{2,1,0:T(8,128)(2,1)S(1)}, f32[256,128]{1,0:T(8,128)S(1)}, bf16[6,256,2560]{2,1,0:T(8,128)(2,1)S(1)}) custom-call(s32[1]{0:T(128)} %bitcast.place, s32[2,8]{1,0:T(2,128)S(1)} %copy-done.5, bf16[256,2560]{1,0:T(8,128)(2,1)S(1)} %copy-done.3, bf16[256,2560]{1,0:T(8,128)(2,1)S(1)} %copy-done.4, ...), custom_call_target="tpu_custom_call" | custom-call | flops 1342177280 | bytes 10485760 | tf_op jit(solution)/shard_map/weigh_own/pallas_call | solution.py:254
  103.1 2.1 %collective-permute-start.20 = (bf16[256,640]{1,0:T(8,128)(2,1)S(1)}, bf16[256,640]{1,0:T(8,128)(2,1)S(1)}, u32[]{:S(2)}, u32[]{:S(2)}) collective-permute-start(bf16[256,640]{1,0:T(8,128)(2,1)S(1)} %slice.28), channel_id=1, source_target_pairs={{0,4},{1,5},{2,6},{3,7},{4,0},{5,1},{6,2},{7,3},{8,12},{9,13},{10,... | collective-permute-start | bytes 983048 | tf_op jit(solution)/shard_map/ppermute | solution.py:27
  105.2 1.4 %collective-permute-done.15.refs_2_ = bf16[256,640]{1,0:T(8,128)(2,1)S(1)} collective-permute-done((bf16[256,640]{1,0:T(8,128)(2,1)S(1)}, bf16[256,640]{1,0:T(8,128)(2,1)S(1)}, u32[]{:S(2)}, u32[]{:S(2)}) %collective-permute-start.15) | collective-permute-done | bytes 327712 | tf_op jit(solution)/shard_map/ppermute | solution.py:27
  106.6 0.9 collective-permute-start.21
  107.5 4.0 %collective-permute-done.16.refs_3_ = bf16[256,640]{1,0:T(8,128)(2,1)S(1)} collective-permute-done((bf16[256,640]{1,0:T(8,128)(2,1)S(1)}, bf16[256,640]{1,0:T(8,128)(2,1)S(1)}, u32[]{:S(2)}, u32[]{:S(2)}) %collective-permute-start.16) | collective-permute-done | bytes 327712 | tf_op jit(solution)/shard_map/ppermute | solution.py:27
  111.5 1.5 %collective-permute-start.19 = (bf16[256,640]{1,0:T(8,128)(2,1)S(1)}, bf16[256,640]{1,0:T(8,128)(2,1)S(1)}, u32[]{:S(2)}, u32[]{:S(2)}) collective-permute-start(bf16[256,640]{1,0:T(8,128)(2,1)S(1)} %get-tuple-element.50), channel_id=1, source_target_pairs={{0,2},{1,3},{2,0},{3,1},{4,6},{5,7},{6,4},{7,5},{8,10},{9,11},{10,... | collective-permute-start | bytes 983048 | tf_op jit(solution)/shard_map/ppermute | solution.py:27
  113.6 4.5 %combine_0.1 = (bf16[256,2560]{1,0:T(8,128)(2,1)}, bf16[6,256,2560]{2,1,0:T(8,128)(2,1)S(1)}) custom-call(s32[1]{0:T(128)} %bitcast.place, s32[2,8]{1,0:T(2,128)S(1)} %copy-done.5, bf16[20,256,1024]{2,1,0:T(8,128)(2,1)S(1)} %get-tuple-element.41.weights, f32[256,128]{1,0:T(8,128)S(1)} %get-tuple-element.42.own, ...), custom_call_target="tpu_custom_call", output_to_operand_aliasing={{1}: (5, {})} | custom-call | flops 1006632960 | bytes 7864320 | tf_op jit(solution)/shard_map/combine_0/pallas_call | solution.py:310
  118.1 2.1 %collective-permute-done.20.refs_2_ = bf16[256,640]{1,0:T(8,128)(2,1)S(1)} collective-permute-done((bf16[256,640]{1,0:T(8,128)(2,1)S(1)}, bf16[256,640]{1,0:T(8,128)(2,1)S(1)}, u32[]{:S(2)}, u32[]{:S(2)}) %collective-permute-start.20) | collective-permute-done | bytes 327712 | tf_op jit(solution)/shard_map/ppermute | solution.py:27
  120.2 2.3 %combine_15.1 = (bf16[256,2560]{1,0:T(8,128)(2,1)}, bf16[6,256,2560]{2,1,0:T(8,128)(2,1)S(1)}) custom-call(s32[1]{0:T(128)} %bitcast.place, s32[2,8]{1,0:T(2,128)S(1)} %copy-done.5, bf16[20,256,1024]{2,1,0:T(8,128)(2,1)S(1)} %get-tuple-element.41.weights, f32[256,128]{1,0:T(8,128)S(1)} %get-tuple-element.42.own, ...), custom_call_target="tpu_custom_call", output_to_operand_aliasing={{1}: (5, {}), {0}: (9, {})} | custom-call | flops 335544320 | bytes 2621440 | tf_op jit(solution)/shard_map/combine_15/pallas_call | solution.py:310
  (36 shorter events, 3.3 us)
Async XLA Ops:
  0.0 10.4 %collective-permute-start.1 = (bf16[256,2560]{1,0:T(8,128)(2,1)}, bf16[256,2560]{1,0:T(8,128)(2,1)S(1)}, u32[]{:S(2)}, u32[]{:S(2)}) collective-permute-start(bf16[256,2560]{1,0:T(8,128)(2,1)} %refs_6_.1), channel_id=1, source_target_pairs={{0,1},{1,0},{2,3},{3,2},{4,5},{5,4},{6,7},{7,6},{8,9},{9,8},{10,11... | collective-permute-start | bytes 3932168 | tf_op jit(solution)/shard_map/ppermute | solution.py:27
  0.5 15.8 %collective-permute-start.4 = (bf16[256,2560]{1,0:T(8,128)(2,1)}, bf16[256,2560]{1,0:T(8,128)(2,1)}, u32[]{:S(2)}, u32[]{:S(2)}) collective-permute-start(bf16[256,2560]{1,0:T(8,128)(2,1)} %refs_0_.5), channel_id=1, source_target_pairs={{4,8},{5,9},{6,10},{7,11},{8,4},{9,5},{10,6},{11,7},{20,24},{21,25... | collective-permute-start | bytes 3932168 | tf_op jit(solution)/shard_map/ppermute | solution.py:27
  2.2 34.3 %collective-permute-start.3 = (bf16[256,2560]{1,0:T(8,128)(2,1)}, bf16[256,2560]{1,0:T(8,128)(2,1)}, u32[]{:S(2)}, u32[]{:S(2)}) collective-permute-start(bf16[256,2560]{1,0:T(8,128)(2,1)} %refs_0_.5), channel_id=1, source_target_pairs={{0,4},{1,5},{2,6},{3,7},{4,0},{5,1},{6,2},{7,3},{8,12},{9,13},{10,... | collective-permute-start | bytes 3932168 | tf_op jit(solution)/shard_map/ppermute | solution.py:27
  6.6 3.8 %collective-permute-start = (s32[2,8]{1,0:T(2,128)}, s32[2,8]{1,0:T(2,128)S(1)}, u32[]{:S(2)}, u32[]{:S(2)}) collective-permute-start(s32[2,8]{1,0:T(2,128)} %kept.5), channel_id=1, source_target_pairs={{0,2},{1,3},{2,0},{3,1},{4,6},{5,7},{6,4},{7,5},{8,10},{9,11},{10,... | collective-permute-start | bytes 200 | tf_op jit(solution)/shard_map/ppermute | solution.py:27
  10.4 1.1 copy-start.1
  11.4 30.2 %collective-permute-start.2 = (bf16[256,2560]{1,0:T(8,128)(2,1)}, bf16[256,2560]{1,0:T(8,128)(2,1)}, u32[]{:S(2)}, u32[]{:S(2)}) collective-permute-start(bf16[256,2560]{1,0:T(8,128)(2,1)} %queries), channel_id=1, source_target_pairs={{0,2},{1,3},{2,0},{3,1},{4,6},{5,7},{6,4},{7,5},{8,10},{9,11},{10,... | collective-permute-start | bytes 3932168 | tf_op jit(solution)/shard_map/ppermute | solution.py:27
  12.9 29.4 %collective-permute-start.8 = (bf16[256,2560]{1,0:T(8,128)(2,1)}, bf16[256,2560]{1,0:T(8,128)(2,1)S(1)}, u32[]{:S(2)}, u32[]{:S(2)}) collective-permute-start(bf16[256,2560]{1,0:T(8,128)(2,1)} %refs_6_.1), channel_id=1, source_target_pairs={{4,8},{5,9},{6,10},{7,11},{8,4},{9,5},{10,6},{11,7},{20,24},{21,25... | collective-permute-start | bytes 3932168 | tf_op jit(solution)/shard_map/ppermute | solution.py:27
  13.7 50.8 %collective-permute-start.7 = (bf16[256,2560]{1,0:T(8,128)(2,1)}, bf16[256,2560]{1,0:T(8,128)(2,1)S(1)}, u32[]{:S(2)}, u32[]{:S(2)}) collective-permute-start(bf16[256,2560]{1,0:T(8,128)(2,1)} %refs_6_.1), channel_id=1, source_target_pairs={{0,4},{1,5},{2,6},{3,7},{4,0},{5,1},{6,2},{7,3},{8,12},{9,13},{10,... | collective-permute-start | bytes 3932168 | tf_op jit(solution)/shard_map/ppermute | solution.py:27
  36.4 28.3 %collective-permute-start.5 = (bf16[256,2560]{1,0:T(8,128)(2,1)}, bf16[256,2560]{1,0:T(8,128)(2,1)S(1)}, u32[]{:S(2)}, u32[]{:S(2)}) collective-permute-start(bf16[256,2560]{1,0:T(8,128)(2,1)} %refs_0_.5), channel_id=1, source_target_pairs={{0,1},{1,0},{2,3},{3,2},{4,5},{5,4},{6,7},{7,6},{8,9},{9,8},{10,11... | collective-permute-start | bytes 3932168 | tf_op jit(solution)/shard_map/ppermute | solution.py:27
  36.5 56.1 %collective-permute-start.11 = (bf16[256,2560]{1,0:T(8,128)(2,1)}, bf16[256,2560]{1,0:T(8,128)(2,1)S(1)}, u32[]{:S(2)}, u32[]{:S(2)}) collective-permute-start(bf16[256,2560]{1,0:T(8,128)(2,1)} %collective-permute-done.4.refs_3_), channel_id=1, source_target_pairs={{0,4},{1,5},{2,6},{3,7},{4,0},{5,1},{6,2},{7,3},{8,12},{9,13},{10,... | collective-permute-start | bytes 3932168 | tf_op jit(solution)/shard_map/ppermute | solution.py:27
  41.6 52.4 %collective-permute-start.12 = (bf16[256,2560]{1,0:T(8,128)(2,1)}, bf16[256,2560]{1,0:T(8,128)(2,1)S(1)}, u32[]{:S(2)}, u32[]{:S(2)}) collective-permute-start(bf16[256,2560]{1,0:T(8,128)(2,1)} %collective-permute-done.3.refs_2_), channel_id=1, source_target_pairs={{4,8},{5,9},{6,10},{7,11},{8,4},{9,5},{10,6},{11,7},{20,24},{21,25... | collective-permute-start | bytes 3932168 | tf_op jit(solution)/shard_map/ppermute | solution.py:27
  42.4 22.9 %collective-permute-start.6 = (bf16[256,2560]{1,0:T(8,128)(2,1)S(1)}, bf16[256,2560]{1,0:T(8,128)(2,1)S(1)}, u32[]{:S(2)}, u32[]{:S(2)}) collective-permute-start(bf16[256,2560]{1,0:T(8,128)(2,1)S(1)} %broadcast_select_fusion.1.refs_1_), channel_id=1, source_target_pairs={{0,1},{1,0},{2,3},{3,2},{4,5},{5,4},{6,7},{7,6},{8,9},{9,8},{10,11... | collective-permute-start | bytes 3932168 | tf_op jit(solution)/shard_map/ppermute | solution.py:27
  64.6 1.3 %copy-start.4 = (bf16[256,2560]{1,0:T(8,128)(2,1)S(1)}, bf16[256,2560]{1,0:T(8,128)(2,1)}, u32[]{:S(2)}) copy-start(bf16[256,2560]{1,0:T(8,128)(2,1)} %refs_0_.5) | copy-start | bytes 3932164
  64.7 18.4 %collective-permute-start.10 = (bf16[256,1280]{1,0:T(8,128)(2,1)S(1)}, bf16[256,1280]{1,0:T(8,128)(2,1)S(1)}, u32[]{:S(2)}, u32[]{:S(2)}) collective-permute-start(bf16[256,1280]{1,0:T(8,128)(2,1)S(1)} %get-tuple-element.55), channel_id=1, source_target_pairs={{0,1},{1,0},{2,3},{3,2},{4,5},{5,4},{6,7},{7,6},{8,9},{9,8},{10,11... | collective-permute-start | bytes 1966088 | tf_op jit(solution)/shard_map/ppermute | solution.py:27
  64.8 19.3 %collective-permute-start.9 = (bf16[256,1280]{1,0:T(8,128)(2,1)S(1)}, bf16[256,1280]{1,0:T(8,128)(2,1)S(1)}, u32[]{:S(2)}, u32[]{:S(2)}) collective-permute-start(bf16[256,1280]{1,0:T(8,128)(2,1)S(1)} %get-tuple-element.56), channel_id=1, source_target_pairs={{0,1},{1,0},{2,3},{3,2},{4,5},{5,4},{6,7},{7,6},{8,9},{9,8},{10,11... | collective-permute-start | bytes 1966088 | tf_op jit(solution)/shard_map/ppermute | solution.py:27
  75.6 5.0 %collective-permute-start.13 = (f32[256,128]{1,0:T(8,128)S(1)}, f32[256,128]{1,0:T(8,128)S(1)}, u32[]{:S(2)}, u32[]{:S(2)}) collective-permute-start(f32[256,128]{1,0:T(8,128)S(1)} %get-tuple-element.34.stats), channel_id=1, source_target_pairs={{0,2},{1,3},{2,0},{3,1},{4,6},{5,7},{6,4},{7,5},{8,10},{9,11},{10,... | collective-permute-start | bytes 393224 | tf_op jit(solution)/shard_map/ppermute | solution.py:27
  77.2 6.9 %copy-start.2 = (bf16[256,2560]{1,0:T(8,128)(2,1)S(1)}, bf16[256,2560]{1,0:T(8,128)(2,1)}, u32[]{:S(2)}) copy-start(bf16[256,2560]{1,0:T(8,128)(2,1)} %copy-done.1) | copy-start | bytes 3932164
  77.2 6.8 %copy-start = (bf16[256,2560]{1,0:T(8,128)(2,1)S(1)}, bf16[256,2560]{1,0:T(8,128)(2,1)}, u32[]{:S(2)}) copy-start(bf16[256,2560]{1,0:T(8,128)(2,1)} %refs_6_.1) | copy-start | bytes 3932164
  80.6 33.0 %collective-permute-start.17 = (bf16[256,1920]{1,0:T(8,128)(2,1)S(1)}, bf16[256,1920]{1,0:T(8,128)(2,1)S(1)}, u32[]{:S(2)}, u32[]{:S(2)}) collective-permute-start(bf16[256,1920]{1,0:T(8,128)(2,1)S(1)} %slice.26), channel_id=1, source_target_pairs={{0,4},{1,5},{2,6},{3,7},{4,0},{5,1},{6,2},{7,3},{8,12},{9,13},{10,... | collective-permute-start | bytes 2949128 | tf_op jit(solution)/shard_map/ppermute | solution.py:27
  83.1 30.5 %collective-permute-start.18 = (bf16[256,1920]{1,0:T(8,128)(2,1)S(1)}, bf16[256,1920]{1,0:T(8,128)(2,1)S(1)}, u32[]{:S(2)}, u32[]{:S(2)}) collective-permute-start(bf16[256,1920]{1,0:T(8,128)(2,1)S(1)} %slice.27), channel_id=1, source_target_pairs={{4,8},{5,9},{6,10},{7,11},{8,4},{9,5},{10,6},{11,7},{20,24},{21,25... | collective-permute-start | bytes 2949128 | tf_op jit(solution)/shard_map/ppermute | solution.py:27
  88.8 5.8 %copy-start.3 = (bf16[256,2560]{1,0:T(8,128)(2,1)S(1)}, bf16[256,2560]{1,0:T(8,128)(2,1)}, u32[]{:S(2)}) copy-start(bf16[256,2560]{1,0:T(8,128)(2,1)} %queries) | copy-start | bytes 3932164
  88.9 5.8 %copy-start.5 = (s32[2,8]{1,0:T(2,128)S(1)}, s32[2,8]{1,0:T(2,128)}, u32[]{:S(2)}) copy-start(s32[2,8]{1,0:T(2,128)} %kept.5) | copy-start | bytes 196
  88.9 14.2 %collective-permute-start.14 = (bf16[256,640]{1,0:T(8,128)(2,1)S(1)}, bf16[256,640]{1,0:T(8,128)(2,1)S(1)}, u32[]{:S(2)}, u32[]{:S(2)}) collective-permute-start(bf16[256,640]{1,0:T(8,128)(2,1)S(1)} %get-tuple-element.44), channel_id=1, source_target_pairs={{0,2},{1,3},{2,0},{3,1},{4,6},{5,7},{6,4},{7,5},{8,10},{9,11},{10,... | collective-permute-start | bytes 983048 | tf_op jit(solution)/shard_map/ppermute | solution.py:27
  92.5 14.1 %collective-permute-start.15 = (bf16[256,640]{1,0:T(8,128)(2,1)S(1)}, bf16[256,640]{1,0:T(8,128)(2,1)S(1)}, u32[]{:S(2)}, u32[]{:S(2)}) collective-permute-start(bf16[256,640]{1,0:T(8,128)(2,1)S(1)} %get-tuple-element.45), channel_id=1, source_target_pairs={{0,2},{1,3},{2,0},{3,1},{4,6},{5,7},{6,4},{7,5},{8,10},{9,11},{10,... | collective-permute-start | bytes 983048 | tf_op jit(solution)/shard_map/ppermute | solution.py:27
  94.0 17.4 %collective-permute-start.16 = (bf16[256,640]{1,0:T(8,128)(2,1)S(1)}, bf16[256,640]{1,0:T(8,128)(2,1)S(1)}, u32[]{:S(2)}, u32[]{:S(2)}) collective-permute-start(bf16[256,640]{1,0:T(8,128)(2,1)S(1)} %get-tuple-element.46), channel_id=1, source_target_pairs={{0,2},{1,3},{2,0},{3,1},{4,6},{5,7},{6,4},{7,5},{8,10},{9,11},{10,... | collective-permute-start | bytes 983048 | tf_op jit(solution)/shard_map/ppermute | solution.py:27
  103.1 17.1 %collective-permute-start.20 = (bf16[256,640]{1,0:T(8,128)(2,1)S(1)}, bf16[256,640]{1,0:T(8,128)(2,1)S(1)}, u32[]{:S(2)}, u32[]{:S(2)}) collective-permute-start(bf16[256,640]{1,0:T(8,128)(2,1)S(1)} %slice.28), channel_id=1, source_target_pairs={{0,4},{1,5},{2,6},{3,7},{4,0},{5,1},{6,2},{7,3},{8,12},{9,13},{10,... | collective-permute-start | bytes 983048 | tf_op jit(solution)/shard_map/ppermute | solution.py:27
  106.6 13.6 %collective-permute-start.21 = (bf16[256,640]{1,0:T(8,128)(2,1)S(1)}, bf16[256,640]{1,0:T(8,128)(2,1)S(1)}, u32[]{:S(2)}, u32[]{:S(2)}) collective-permute-start(bf16[256,640]{1,0:T(8,128)(2,1)S(1)} %slice.29), channel_id=1, source_target_pairs={{4,8},{5,9},{6,10},{7,11},{8,4},{9,5},{10,6},{11,7},{20,24},{21,25... | collective-permute-start | bytes 983048 | tf_op jit(solution)/shard_map/ppermute | solution.py:27
  111.5 8.7 %collective-permute-start.19 = (bf16[256,640]{1,0:T(8,128)(2,1)S(1)}, bf16[256,640]{1,0:T(8,128)(2,1)S(1)}, u32[]{:S(2)}, u32[]{:S(2)}) collective-permute-start(bf16[256,640]{1,0:T(8,128)(2,1)S(1)} %get-tuple-element.50), channel_id=1, source_target_pairs={{0,2},{1,3},{2,0},{3,1},{4,6},{5,7},{6,4},{7,5},{8,10},{9,11},{10,... | collective-permute-start | bytes 983048 | tf_op jit(solution)/shard_map/ppermute | solution.py:27
